TPU v7x, 32 devices: a whole 2x2x4 slice. The times are simulated.
32 devices in a mesh: groups: 2 (over x), solver: 8 (over z, y), trainer: 2 (over core).
Axes of the slice: x: 2, y: 2, z: 4, core: 2. Of those that a mesh axis runs over, the one named last changes fastest.
Arguments:
- initial_field: float32 [512, 8192], P(('groups', 'solver'), 'trainer'), parts along dimension 0, may hold values from -40 to 40
- coef_index: int32 [512, 8192], P(('groups', 'solver'), 'trainer'), parts along dimension 0, may hold values from 0 to 15
- kappa_table: float32 [32], P('groups'), parts along dimension 0, may hold values from 0.02 to 0.15
- drift_table: float32 [4, 16], P('groups'), parts along dimension 0, may hold values from -0.2 to 0.2
- tile_pos: int32 [4, 8, 2, 24], P('groups', 'solver', 'trainer'), parts along dimension 0, may hold values from 0 to 255
- tile_dest: int32 [4, 8, 2, 24, 1], P('groups', 'solver', 'trainer'), parts along dimension 0, may hold values from 0 to 7; in each aligned block of 24 rows (0 to 23, 24 to 47, ..., all dimensions but the last counted through in order) at most 4 rows name the same one
- conv_in: float32 [18, 64, 4], P('groups'), parts along dimension 0, may hold values from -1 to 1
- mix_weight: float32 [128, 64], P('groups'), parts along dimension 0, may hold values from -0.75 to 0.75
- conv_out: float32 [18, 1, 64], P('groups'), parts along dimension 0, may hold values from -0.25 to 0.25
Outputs:
- final_field: float32 [512, 8192], P(('groups', 'solver'), 'trainer'), parts along dimension 0
- conv_in_change: float32 [18, 64, 4], P('groups'), parts along dimension 0
- mix_change: float32 [128, 64], P('groups'), parts along dimension 0
- conv_out_change: float32 [18, 1, 64], P('groups'), parts along dimension 0
There are 2 independent parts, one for each index of `groups`. A program takes and returns all parts, laid end to end along the dimension named above; each array names one. Nothing has to cross between parts.
Inputs may be any that keep to these rules, and one draw needn't show every extreme that they name: `tile_dest`: in each aligned block of 24 rows (one snapshot of one device) no buffer is named more than 4 times.
All inputs are finite; a program needn't handle non-finite values.
Results may differ from a plain program's by a relative error of at most 0.0003.
Values sent between devices are 32-bit elements; how exact they have to be, the bound alone decides.
No kernel may reach another device: no remote copies, remote signals or barrier semaphores. Data moves between devices by JAX's collectives and lax.ppermute only.
A program may use at most 128 MiB of HBM per device.

v0:
```python
import jax
import jax.numpy as jnp
from jax import lax
from jax.sharding import PartitionSpec as P

TR = 4
TW = 128
SNAPS = 2


HIGH = lax.Precision.HIGHEST
STEP_RATE = 0.05
NORM_EPS = 1e-06


def with_halo(cells, sides, width):
    for axis, dim in sides:
        count = lax.axis_size(axis)
        ends = count - 1
        head = lax.slice_in_dim(cells, 0, width, axis=dim)
        tail = lax.slice_in_dim(cells, cells.shape[dim] - width, cells.shape[dim], axis=dim)
        cells = jnp.concatenate(
            [
                lax.ppermute(tail, axis, [(i, (i + 1) % count) for i in range(ends)]),
                cells,
                lax.ppermute(head, axis, [((i + 1) % count, i) for i in range(ends)]),
            ],
            axis=dim,
        )
    return cells


def coefficients(cell_index, kappa_table, drift_table):
    diffusion = jnp.zeros(cell_index.shape, jnp.float32)
    drift_rows = jnp.zeros(cell_index.shape, jnp.float32)
    drift_cols = jnp.zeros(cell_index.shape, jnp.float32)
    for entry in range(kappa_table.shape[0]):
        chosen = cell_index == entry
        diffusion = jnp.where(chosen, kappa_table[entry], diffusion)
        drift_rows = jnp.where(chosen, drift_table[0, entry], drift_rows)
        drift_cols = jnp.where(chosen, drift_table[1, entry], drift_cols)
    return (diffusion, drift_rows, drift_cols)


def advance(padded, diffusion, drift_rows, drift_cols):
    center = padded[1:-1, 1:-1]
    above = padded[:-2, 1:-1]
    below = padded[2:, 1:-1]
    left_side = padded[1:-1, :-2]
    right_side = padded[1:-1, 2:]
    laplace = above + below + left_side + right_side - 4.0 * center
    upwind = jnp.maximum(drift_rows, 0.0) * (center - above) + jnp.minimum(drift_rows, 0.0) * (
        below - center
    )
    upwind = (
        upwind
        + jnp.maximum(drift_cols, 0.0) * (center - left_side)
        + jnp.minimum(drift_cols, 0.0) * (right_side - center)
    )
    return center + diffusion * laplace - upwind


def convolve(inputs, kernel):
    padded = jnp.pad(inputs, ((0, 0), (0, 0), (1, 1), (1, 1)))
    height = inputs.shape[2]
    breadth = inputs.shape[3]
    summed = jnp.zeros((kernel.shape[1], inputs.shape[1], height, breadth), jnp.float32)
    for row_shift in range(3):
        for col_shift in range(3):
            window = padded[:, :, row_shift : row_shift + height, col_shift : col_shift + breadth]
            summed = summed + jnp.einsum(
                "oc,cbrw->obrw", kernel[3 * row_shift + col_shift], window, precision=HIGH
            )
    return summed


def surrogate(params, tiles):
    inputs = jnp.transpose(tiles[:, 0:4], (1, 0, 2, 3))
    first = jax.nn.gelu(convolve(inputs, params[0]))
    second = jax.nn.gelu(jnp.einsum("oc,cbrw->obrw", params[1], first, precision=HIGH))
    return tiles[:, 0] + convolve(second, params[2])[0]


def tile_loss(params, tiles, weights):
    misfit = surrogate(params, tiles) - tiles[:, 4]
    return jnp.sum(weights[:, None, None] * misfit * misfit)


def flatten(tree):
    return jnp.concatenate([leaf.reshape(-1) for leaf in tree])


def unflatten(vector, params):
    pieces = []
    offset = 0
    for weight in params:
        entries = weight.size
        pieces.append(vector[offset : offset + entries].reshape(weight.shape))
        offset = offset + entries
    return tuple(pieces)


def cut_tiles(channels, height, per_row):
    layers = len(channels)
    stacked = jnp.stack(channels)
    shaped = stacked.reshape(layers, height // TR, TR, per_row, TW)
    return jnp.transpose(shaped, (1, 3, 0, 2, 4)).reshape(height // TR * per_row, layers, TR, TW)


def local(
    initial_field,
    coef_index,
    kappa_table,
    drift_table,
    tile_pos,
    tile_dest,
    conv_in,
    mix_weight,
    conv_out,
):
    height, breadth = initial_field.shape
    solvers = lax.axis_size("solver")
    trainers = lax.axis_size("trainer")
    fields = []
    diffusion, drift_rows, drift_cols = coefficients(coef_index, kappa_table, drift_table)
    current = initial_field
    for step_number in range(4):
        padded = with_halo(current, (("solver", 0), ("trainer", 1)), 1)
        current = advance(padded, diffusion, drift_rows, drift_cols)
        fields.append(current)
    send_count = tile_pos.shape[-1]
    most = max(2, 3 * send_count // (2 * solvers))
    slots_total = solvers * most
    per_row = breadth // TW
    params = (conv_in, mix_weight, conv_out)
    total = jnp.zeros((flatten(params).shape[0],), jnp.float32)
    for snapshot in range(SNAPS):
        positions = tile_pos[snapshot, 0, 0]
        destination = tile_dest[snapshot, 0, 0, :, 0]
        onehot_dest = (destination[:, None] == jnp.arange(solvers, dtype=jnp.int32)).astype(
            jnp.int32
        )
        slot_rank = jnp.sum((jnp.cumsum(onehot_dest, axis=0) - onehot_dest) * onehot_dest, axis=1)
        marks = jnp.zeros((solvers, most), jnp.float32).at[destination, slot_rank].set(1.0)
        shaped = cut_tiles(
            [fields[2 * snapshot], diffusion, drift_rows, drift_cols, fields[2 * snapshot + 1]],
            height,
            per_row,
        )
        picks = shaped[positions]
        outgoing = (
            jnp.zeros((solvers, most, 5, TR, TW), jnp.float32).at[destination, slot_rank].set(picks)
        )
        arrived, arrived_marks = (
            lax.all_to_all(outgoing, "solver", split_axis=0, concat_axis=0, tiled=True),
            lax.all_to_all(marks, "solver", split_axis=0, concat_axis=0, tiled=True),
        )
        arrived = arrived.reshape(slots_total, 5, TR, TW)
        weights = arrived_marks.reshape(slots_total)
        starting = jax.tree.map(jnp.zeros_like, params)
        tile_blocks = arrived.reshape((slots_total // 16, 16, 5, TR, TW))
        weight_blocks = weights.reshape(slots_total // 16, 16)

        def accumulate(running, portion):
            grads = jax.grad(tile_loss)(params, portion[0], portion[1])
            return (jax.tree.map(jnp.add, running, grads), None)

        local_grads, unused = lax.scan(accumulate, starting, (tile_blocks, weight_blocks))
        buffer_flat = flatten(local_grads)
        scale = lax.rsqrt(jnp.mean(buffer_flat * buffer_flat) + NORM_EPS)
        share = buffer_flat * scale / (solvers * trainers)
        direction = lax.psum(share, ("solver", "trainer"))
        total = total + direction
        params = tuple(
            (
                weight - STEP_RATE * change
                for weight, change in zip(params, unflatten(direction, params))
            )
        )
    changes = unflatten(total, params)
    return (fields[3], changes[0], changes[1], changes[2])


def solution(mesh):
    return jax.shard_map(
        local,
        mesh=mesh,
        in_specs=(
            P(("groups", "solver"), "trainer"),
            P(("groups", "solver"), "trainer"),
            P("groups"),
            P("groups", None),
            P("groups", "solver", "trainer", None),
            P("groups", "solver", "trainer", None, None),
            P("groups", None, None),
            P("groups", None),
            P("groups", None, None),
        ),
        out_specs=(
            P(("groups", "solver"), "trainer"),
            P("groups", None, None),
            P("groups", None),
            P("groups", None, None),
        ),
        check_vma=False,
    )
```

profile of v0, /device:TPU:0, one launch (start us, length us, event | category | flops | bytes accessed | tf_op | source)
XLA Modules:
  0.0 621.2 jit_solution(12370365812488091491)
XLA Ops:
  1.7 4.9 collective-permute-start
  18.8 34.2 %fusion.320 = (f32[32,4096]{1,0:T(8,128)S(1)}, f32[32,4096]{1,0:T(8,128)S(1)}, f32[32,4096]{1,0:T(8,128)S(1)}, f32[32,4096]{1,0:T(8,128)S(1)}) fusion(f32[32,4096]{1,0:T(8,128)S(1)} %copy-done.6, f32[34,1]{1,0:T(8,128)S(1)} %collective-permute-done.3, f32[1,4096]{1,0:T(1,128)} %copy-done.21, f32[1,4096]{1,0:T(1,128)} %copy-done.20, ...), kind=kLoop, calls=%fused_computation.491 | loop fusion | flops 10354688 | bytes 4751824 | tf_op jit(solution)/shard_map/sub | solution.py:60
  53.0 4.4 collective-permute-start.4
  61.5 7.8 %all-to-all-start = ((f32[8,1,4]{2,1,0:T(1,128)}), f32[8,1,4]{2,1,0:T(1,128)S(1)}, u32[]{:S(2)}, u32[]{:S(2)}) async-start(f32[8,1,4]{2,1,0:T(1,128)} %copy.61), calls=%async_computation | async-start | bytes 8192 | tf_op jit(solution)/shard_map/all_to_all | solution.py:156
  74.4 3.9 collective-permute-start.8
  83.4 6.6 %all-to-all-start.2 = ((f32[8,1,4]{2,1,0:T(1,128)}), f32[8,1,4]{2,1,0:T(1,128)S(1)}, u32[]{:S(2)}, u32[]{:S(2)}) async-start(f32[8,1,4]{2,1,0:T(1,128)} %copy.67), calls=%async_computation.2 | async-start | bytes 8192 | tf_op jit(solution)/shard_map/all_to_all | solution.py:156
  91.3 5.2 all-to-all-done.2
  115.8 4.7 scatter_fusion.1
  123.7 4.8 all-to-all-start.1
  137.2 4.7 scatter_fusion.3
  141.8 6.0 all-to-all-start.3
  147.9 172.2 %while.36 = (s32[]{:T(128)}, f32[9,64,4]{1,2,0:T(4,128)S(1)}, f32[64,64]{1,0:T(8,128)S(1)}, f32[9,1,64]{2,1,0:T(1,128)S(1)}, f32[2,16]{1,0:T(2,128)S(1)}, /*inde...) while((s32[]{:T(128)}, f32[9,64,4]{1,2,0:T(4,128)S(1)}, ...), condition=%wide.region_5.6_spmd.clone, body=%wide.region_4.5_spmd.clone.sunk | while | flops 1820479616 | bytes 177629840 | solution.py:168
  165.0 4.5 bitcast_multiply_fusion.19
  197.9 4.0 multiply_bitcast_fusion.20
  201.9 4.6 pad_add_fusion.16
  206.5 4.2 fusion.596
  250.0 4.5 bitcast_multiply_fusion.19
  283.0 4.0 multiply_bitcast_fusion.20
  287.0 4.6 pad_add_fusion.16
  291.6 4.2 fusion.596
  298.6 3.2 fusion.597
  321.9 61.8 %psum.14 = f32[6976]{0:T(1024)S(1)} all-reduce(f32[6976]{0:T(1024)S(1)} %multiply_multiply_fusion.9), channel_id=1, replica_groups=mesh['groups'=2,'solver'=8,'trainer'=2] {'solver','trainer'}, use_global_device_ids=true, to_apply=%region_7.8 | all-reduce | flops 6976 | bytes 55808 | tf_op jit(solution)/shard_map/psum | solution.py:172
  384.6 173.7 %while.37 = (s32[]{:T(128)}, f32[9,64,4]{1,2,0:T(4,128)S(1)}, f32[64,64]{1,0:T(8,128)S(1)}, f32[9,1,64]{2,1,0:T(1,128)S(1)}, f32[2,16]{1,0:T(2,128)S(1)}, /*inde...) while((s32[]{:T(128)}, f32[9,64,4]{1,2,0:T(4,128)S(1)}, ...), condition=%wide.region_13.14_spmd.clone, body=%wide.region_12.13_spmd.clone.sunk | while | flops 1820479616 | bytes 177629840 | solution.py:168
  402.4 4.5 bitcast_multiply_fusion.21
  435.3 4.0 multiply_bitcast_fusion.21
  439.3 4.6 pad_add_fusion.17
  443.9 4.3 fusion.667
  488.4 4.5 bitcast_multiply_fusion.21
  521.3 4.0 multiply_bitcast_fusion.21
  525.3 4.6 pad_add_fusion.17
  529.9 4.3 fusion.667
  560.1 57.6 %psum.15 = f32[6976]{0:T(1024)S(1)} all-reduce(f32[6976]{0:T(1024)S(1)} %multiply_multiply_fusion.8), channel_id=1, replica_groups=mesh['groups'=2,'solver'=8,'trainer'=2] {'solver','trainer'}, use_global_device_ids=true, to_apply=%region_15.16 | all-reduce | flops 6976 | bytes 55808 | tf_op jit(solution)/shard_map/psum | solution.py:172
  (385 shorter events, 333.0 us)
Async XLA Ops:
  0.6 16.4 %copy-start.13 = (f32[2,16]{1,0:T(2,128)S(1)}, f32[2,16]{1,0:T(2,128)}, u32[]{:S(2)}) copy-start(f32[2,16]{1,0:T(2,128)} %param.16) | copy-start | bytes 388
  1.7 12.4 %collective-permute-start = (f32[1,4096]{1,0:T(1,128)S(1)}, f32[1,4096]{1,0:T(1,128)S(1)}, u32[]{:S(2)}, u32[]{:S(2)}) collective-permute-start(f32[1,4096]{1,0:T(1,128)S(1)} %get-tuple-element.549), channel_id=1, source_target_pairs={{0,2},{2,4},{4,6},{6,8},{8,10},{10,12},{12,14},{1,3},{3,5},{5,7},{... | collective-permute-start | bytes 49160 | tf_op jit(solution)/shard_map/ppermute | solution.py:24
  6.6 7.5 %collective-permute-start.1 = (f32[1,4096]{1,0:T(1,128)S(1)}, f32[1,4096]{1,0:T(1,128)S(1)}, u32[]{:S(2)}, u32[]{:S(2)}) collective-permute-start(f32[1,4096]{1,0:T(1,128)S(1)} %get-tuple-element.550), channel_id=1, source_target_pairs={{2,0},{4,2},{6,4},{8,6},{10,8},{12,10},{14,12},{3,1},{5,3},{7,5},{... | collective-permute-start | bytes 49160 | tf_op jit(solution)/shard_map/ppermute | solution.py:26
  14.2 3.5 collective-permute-start.2
  15.7 3.1 collective-permute-start.3
  18.8 53.2 %copy-start.25 = (s32[2,1,1,24]{3,2,1,0:T(1,128)S(1)}, s32[2,1,1,24]{3,2,1,0:T(1,128)}, u32[]{:S(2)}) copy-start(s32[2,1,1,24]{3,2,1,0:T(1,128)} %param.17) | copy-start | bytes 580
  53.0 16.3 %collective-permute-start.4 = (f32[1,4096]{1,0:T(1,128)S(1)}, f32[1,4096]{1,0:T(1,128)S(1)}, u32[]{:S(2)}, u32[]{:S(2)}) collective-permute-start(f32[1,4096]{1,0:T(1,128)S(1)} %get-tuple-element.531), channel_id=1, source_target_pairs={{0,2},{2,4},{4,6},{6,8},{8,10},{10,12},{12,14},{1,3},{3,5},{5,7},{... | collective-permute-start | bytes 49160 | tf_op jit(solution)/shard_map/ppermute | solution.py:24
  57.4 11.9 %collective-permute-start.5 = (f32[1,4096]{1,0:T(1,128)S(1)}, f32[1,4096]{1,0:T(1,128)S(1)}, u32[]{:S(2)}, u32[]{:S(2)}) collective-permute-start(f32[1,4096]{1,0:T(1,128)S(1)} %get-tuple-element.532), channel_id=1, source_target_pairs={{2,0},{4,2},{6,4},{8,6},{10,8},{12,10},{14,12},{3,1},{5,3},{7,5},{... | collective-permute-start | bytes 49160 | tf_op jit(solution)/shard_map/ppermute | solution.py:26
  58.8 21.0 %copy-start.15 = (f32[64,64]{1,0:T(8,128)S(1)}, f32[64,64]{1,0:T(8,128)}, u32[]{:S(2)}) copy-start(f32[64,64]{1,0:T(8,128)} %param.20) | copy-start | bytes 49156
  58.8 21.1 %copy-start.10 = (f32[9,64,4]{1,2,0:T(4,128)S(1)}, f32[9,64,4]{1,2,0:T(4,128)}, u32[]{:S(2)}) copy-start(f32[9,64,4]{1,2,0:T(4,128)} %param.19) | copy-start | bytes 27652
  61.5 22.0 %all-to-all-start = ((f32[8,1,4]{2,1,0:T(1,128)}), f32[8,1,4]{2,1,0:T(1,128)S(1)}, u32[]{:S(2)}, u32[]{:S(2)}) async-start(f32[8,1,4]{2,1,0:T(1,128)} %copy.61), calls=%async_computation | async-start | bytes 8192 | tf_op jit(solution)/shard_map/all_to_all | solution.py:156
  69.4 2.6 collective-permute-start.6
  70.7 3.1 collective-permute-start.7
  74.4 23.8 %collective-permute-start.8 = (f32[1,4096]{1,0:T(1,128)S(1)}, f32[1,4096]{1,0:T(1,128)S(1)}, u32[]{:S(2)}, u32[]{:S(2)}) collective-permute-start(f32[1,4096]{1,0:T(1,128)S(1)} %get-tuple-element.529), channel_id=1, source_target_pairs={{0,2},{2,4},{4,6},{6,8},{8,10},{10,12},{12,14},{1,3},{3,5},{5,7},{... | collective-permute-start | bytes 49160 | tf_op jit(solution)/shard_map/ppermute | solution.py:24
  78.4 19.9 %collective-permute-start.9 = (f32[1,4096]{1,0:T(1,128)S(1)}, f32[1,4096]{1,0:T(1,128)S(1)}, u32[]{:S(2)}, u32[]{:S(2)}) collective-permute-start(f32[1,4096]{1,0:T(1,128)S(1)} %get-tuple-element.530), channel_id=1, source_target_pairs={{2,0},{4,2},{6,4},{8,6},{10,8},{12,10},{14,12},{3,1},{5,3},{7,5},{... | collective-permute-start | bytes 49160 | tf_op jit(solution)/shard_map/ppermute | solution.py:26
  83.4 13.1 %all-to-all-start.2 = ((f32[8,1,4]{2,1,0:T(1,128)}), f32[8,1,4]{2,1,0:T(1,128)S(1)}, u32[]{:S(2)}, u32[]{:S(2)}) async-start(f32[8,1,4]{2,1,0:T(1,128)} %copy.67), calls=%async_computation.2 | async-start | bytes 8192 | tf_op jit(solution)/shard_map/all_to_all | solution.py:156
  98.4 2.7 collective-permute-start.10
  99.7 3.1 collective-permute-start.11
  103.5 17.0 %collective-permute-start.12 = (f32[1,4096]{1,0:T(1,128)S(1)}, f32[1,4096]{1,0:T(1,128)S(1)}, u32[]{:S(2)}, u32[]{:S(2)}) collective-permute-start(f32[1,4096]{1,0:T(1,128)S(1)} %get-tuple-element.527), channel_id=1, source_target_pairs={{0,2},{2,4},{4,6},{6,8},{8,10},{10,12},{12,14},{1,3},{3,5},{5,7},{... | collective-permute-start | bytes 49160 | tf_op jit(solution)/shard_map/ppermute | solution.py:24
  106.0 14.5 %collective-permute-start.13 = (f32[1,4096]{1,0:T(1,128)S(1)}, f32[1,4096]{1,0:T(1,128)S(1)}, u32[]{:S(2)}, u32[]{:S(2)}) collective-permute-start(f32[1,4096]{1,0:T(1,128)S(1)} %get-tuple-element.528), channel_id=1, source_target_pairs={{2,0},{4,2},{6,4},{8,6},{10,8},{12,10},{14,12},{3,1},{5,3},{7,5},{... | collective-permute-start | bytes 49160 | tf_op jit(solution)/shard_map/ppermute | solution.py:26
  120.6 7.9 %collective-permute-start.14 = (f32[34,1]{1,0:T(8,128)S(1)}, f32[34,1]{1,0:T(8,128)S(1)}, u32[]{:S(2)}, u32[]{:S(2)}) collective-permute-start(f32[34,1]{1,0:T(8,128)S(1)} %get-tuple-element.513), channel_id=1, source_target_pairs={{0,1},{2,3},{4,5},{6,7},{8,9},{10,11},{12,13},{14,15},{16,17},{18,... | collective-permute-start | bytes 416 | tf_op jit(solution)/shard_map/ppermute | solution.py:24
  122.4 6.1 collective-permute-start.15
  123.7 18.2 %all-to-all-start.1 = ((f32[8,4,5,4,128]{4,3,2,1,0:T(4,128)}), f32[8,4,5,4,128]{4,3,2,1,0:T(4,128)S(1)}, u32[]{:S(2)}, u32[]{:S(2)}) async-start(f32[8,4,5,4,128]{4,3,2,1,0:T(4,128)} %scatter_fusion.1), calls=%async_computation.1 | async-start | bytes 655360 | tf_op jit(solution)/shard_map/all_to_all | solution.py:155
  141.8 242.7 %all-to-all-start.3 = ((f32[8,4,5,4,128]{4,3,2,1,0:T(4,128)}), f32[8,4,5,4,128]{4,3,2,1,0:T(4,128)}, u32[]{:S(2)}, u32[]{:S(2)}) async-start(f32[8,4,5,4,128]{4,3,2,1,0:T(4,128)} %scatter_fusion.3), calls=%async_computation.3 | async-start | bytes 655360 | tf_op jit(solution)/shard_map/all_to_all | solution.py:155
  147.8 172.8 %copy-start.19 = (f32[6976]{0:T(1024)S(1)}, f32[6976]{0:T(1024)}, u32[]{:S(2)}) copy-start(f32[6976]{0:T(1024)} %custom-call.16) | copy-start | bytes 83716
  147.9 236.2 %copy-start.8 = (f32[9,64,4]{2,1,0:T(8,128)S(1)}, f32[9,64,4]{2,1,0:T(8,128)}, u32[]{:S(2)}) copy-start(f32[9,64,4]{2,1,0:T(8,128)} %copy.70) | copy-start | bytes 27652
  320.1 64.3 %copy-start.16 = (f32[64,64]{1,0:T(8,128)S(1)}, f32[64,64]{1,0:T(8,128)}, u32[]{:S(2)}) copy-start(f32[64,64]{1,0:T(8,128)} %param.20) | copy-start | bytes 49156
  320.1 64.5 %copy-start.9 = (f32[9,64,4]{1,2,0:T(4,128)S(1)}, f32[9,64,4]{1,2,0:T(4,128)}, u32[]{:S(2)}) copy-start(f32[9,64,4]{1,2,0:T(4,128)} %custom-call.11) | copy-start | bytes 27652
  320.1 64.5 %copy-start.14 = (f32[9,1,64]{2,1,0:T(1,128)S(1)}, f32[9,1,64]{2,1,0:T(1,128)}, u32[]{:S(2)}) copy-start(f32[9,1,64]{2,1,0:T(1,128)} %custom-call.13) | copy-start | bytes 6916
  320.1 64.5 %copy-start.22 = (f32[64,64]{1,0:T(8,128)S(1)}, f32[64,64]{1,0:T(8,128)}, u32[]{:S(2)}) copy-start(f32[64,64]{1,0:T(8,128)} %custom-call.12) | copy-start | bytes 49156
  320.1 64.5 %copy-start.24 = (f32[2,16]{1,0:T(2,128)S(1)}, f32[2,16]{1,0:T(2,128)}, u32[]{:S(2)}) copy-start(f32[2,16]{1,0:T(2,128)} %reshape_reshape.14) | copy-start | bytes 388
  384.6 174.2 %copy-start.18 = (f32[6976]{0:T(1024)S(1)}, f32[6976]{0:T(1024)}, u32[]{:S(2)}) copy-start(f32[6976]{0:T(1024)} %custom-call.14) | copy-start | bytes 83716
  (18 other events, 102.9 us)
where the time goes:
time: 632 us; the launch traced here: 621 us
  matrix products  286 us (45%)
  blocking collectives  119 us (19%)
  other arithmetic  95.3 us (15%)
  starting transfers between devices  57 us (9%)
  local copies, waits for them, and re-layouts  45.3 us (7%)
  waiting for transfers between devices  9.74 us (2%)
    dot_general x144, matrix products, convolve(): jnp.einsum('oc,cbrw->obrw', kernel[3 * row_shift + col_shift], window, pr...  244 us
    psum x2, blocking collectives, local(): direction = lax.psum(share, ('solver', 'trainer'))  119 us
    dot_general x12, matrix products, surrogate(): jnp.einsum('oc,cbrw->obrw', params[1], first, precision=HIGH)  41.9 us
    sub x4, other arithmetic, advance(): return center + diffusion * laplace - upwind  36.1 us
    ppermute x8, starting transfers between devices, with_halo(): lax.ppermute(tail, axis, [(i, (i + 1) % count) for i in range(ends)])  21.4 us
    add_any x4, other arithmetic, convolve(): padded[:, :, row_shift:row_shift + height, col_shift:col_shift + breadth]  18.5 us
    add_any x4, other arithmetic, surrogate(): jax.nn.gelu(jnp.einsum('oc,cbrw->obrw', params[1], first, precision=HIGH))  17 us
    transpose x4, other arithmetic, convolve(): jnp.einsum('oc,cbrw->obrw', kernel[3 * row_shift + col_shift], window, pr...  15.9 us
  transfers between devices with their start and end apart: 20, of which 4 were waited for; matrix products, arithmetic and copies ran while one was open for 34% of the time, Pallas kernels for 0%

commit v1 on v0

v1 whole, which is shorter than its diff:
```python
import functools

import jax
import jax.numpy as jnp
from jax import lax
from jax.experimental import pallas as pl
from jax.experimental.pallas import tpu as pltpu
from jax.sharding import PartitionSpec as P

TR = 4
TW = 128
SNAPS = 2
STEPS = 4
EXT = 128
LIVE = 64
BATCH = 6

F32 = jnp.float32
BF16 = jnp.bfloat16
STEP_RATE = 0.05
NORM_EPS = 1e-06
GELU_A = 0.7978845608028654
GELU_B = 0.044715

VMEM = pl.BlockSpec(memory_space=pltpu.VMEM)
SMEM = pl.BlockSpec(memory_space=pltpu.SMEM)
PARAMS = pltpu.CompilerParams(vmem_limit_bytes=40 * 1024 * 1024)


def field_kernel(
    sizes, place, tile_pos, tile_dest, u0, index, ext, above, below, tables, picks, final, xin, base, slots,
    counts, fields, ids, coef,
):
    rows, lanes, sends, per_row, half = sizes
    tall = rows + 2 * STEPS
    wide = lanes + EXT
    columns = wide // 128

    ids[0:rows, 0:lanes] = index[...] + 1
    ids[0:rows, lanes:wide] = ext[1].astype(jnp.int32)
    ids[rows : rows + STEPS, :] = below[1].astype(jnp.int32)
    ids[rows + STEPS : tall, :] = above[1].astype(jnp.int32)
    fields[0, 0:rows, 0:lanes] = u0[...]
    fields[0, 0:rows, lanes:wide] = ext[0]
    fields[0, rows : rows + STEPS, :] = below[0]
    fields[0, rows + STEPS : tall, :] = above[0]

    table = [jnp.broadcast_to(tables[k : k + 1, :], (8, 128)) for k in range(4)]
    for c in range(columns):
        for r in range(tall // 8):
            here = (slice(8 * r, 8 * r + 8), slice(128 * c, 128 * c + 128))
            which = ids[here]
            for k in range(4):
                coef[(k,) + here] = jnp.take_along_axis(table[k], which, axis=1)

    lane = lax.broadcasted_iota(jnp.int32, (tall, 128), 1)
    for step in range(STEPS):
        cut = [slice(128 * c, 128 * c + 128) for c in range(columns)]
        shifted = lambda c, by: pltpu.roll(fields[step, :, cut[c % columns]], by % 128, 1)
        before, first = shifted(-1, 1), shifted(0, -1)
        ahead = first
        for c in range(columns):
            center = fields[step, :, cut[c]]
            up = pltpu.roll(center, 1, 0)
            down = pltpu.roll(center, tall - 1, 0)
            own = shifted(c, 1)
            left = jnp.where(lane == 0, before, own)
            following = shifted(c + 1, -1) if c + 1 < columns else first
            right = jnp.where(lane == 127, following, ahead)
            before, ahead = own, following
            new = (
                center
                + coef[0, :, cut[c]] * (up - center)
                + coef[1, :, cut[c]] * (down - center)
                + coef[2, :, cut[c]] * (left - center)
                + coef[3, :, cut[c]] * (right - center)
            )
            fields[step + 1, :, cut[c]] = new
            if step + 1 == STEPS and c < lanes // 128:
                final[:, cut[c]] = new[0:rows]

    mine = place[0] // half
    xin[...] = jnp.zeros_like(xin)
    base[...] = jnp.zeros_like(base)
    sub = lax.broadcasted_iota(jnp.int32, (8, 128), 0)
    channel = picks[...]
    for snapshot in range(SNAPS):
        before, after = 2 * snapshot + 1, 2 * snapshot + 2

        def pick(k, filled):
            far, near = filled
            dest = tile_dest[snapshot, k]
            away = dest // half != mine
            slot = jnp.where(away, far, sends + near)
            slots[snapshot, slot] = lax.rem(dest, half)
            where = tile_pos[snapshot, k]
            top = lax.div(where, per_row) * TR
            start = pl.multiple_of(lax.rem(where, per_row) * TW, TW)
            spot = (pl.ds(pl.multiple_of(top // 8 * 8, 8), 8), pl.ds(start, TW))
            lower = lax.rem(top, 8) == TR
            tile = lambda x: jnp.where(lower, pltpu.roll(x, TR, 0), x)
            value = tile(fields[(before,) + spot])
            which = tile(ids[spot])
            base[snapshot, slot] = (value - tile(fields[(after,) + spot]))[0:TR]
            for r in range(TR):
                row = lambda x: jnp.broadcast_to(x[r : r + 1], (8, 128))
                found = jnp.take_along_axis(channel, row(which), axis=1)
                xin[snapshot, slot, r] = jnp.where(sub % 4 == 0, row(value), found)
            return (jnp.where(away, far + 1, far), jnp.where(away, near, near + 1))

        far, near = lax.fori_loop(0, sends, pick, (jnp.int32(0), jnp.int32(0)))
        counts[snapshot, 0] = far
        counts[snapshot, 1] = near


def split(x):
    high = x.astype(BF16)
    return high, (x - high.astype(F32)).astype(BF16)


def weights3(w):
    high = w.astype(BF16).astype(F32)
    return jnp.concatenate([high, high, w - high], axis=1).astype(BF16)


def values3(high, low):
    return jnp.concatenate([high, low, high], axis=0)


def times(a, b):
    return lax.dot_general(a, b, (((1,), (0,)), ((), ())), preferred_element_type=F32)


def over_cells(a, b):
    return lax.dot_general(a, b, (((1,), (1,)), ((), ())), preferred_element_type=F32)


def gelu_and_slope(z):
    square = z * z
    t = jnp.tanh(z * (GELU_A + (GELU_A * GELU_B) * square))
    gate = 0.5 + 0.5 * t
    value = z * gate
    return value, gate + (value - value * gate) * (2 * GELU_A + (6 * GELU_A * GELU_B) * square)


def lane_shift(x, by):
    lane = lax.broadcasted_iota(jnp.int32, x.shape, 1)
    return jnp.where(lane == (0 if by == 1 else TW - 1), 0.0, pltpu.roll(x, by % TW, 1))


def batch_gradients(cells, gaps, weights):
    w1, mix, w3, w3_t, mix_t = weights
    number = len(cells)
    zero8 = jnp.zeros((8, TW), F32)
    sub8 = lax.broadcasted_iota(jnp.int32, (8, TW), 0)
    columns = []
    for tile in cells:
        sides = [jnp.where(sub8 < 4, lane_shift(x, 1), lane_shift(x, -1)) for x in tile]
        sides = [zero8] + sides + [zero8]
        center = [zero8] + list(tile) + [zero8]
        for r in range(TR):
            stacked = []
            for dr in range(3):
                stacked += [sides[r + dr], center[r + dr]]
            columns.append(jnp.concatenate(stacked, axis=0))
    x_hi, x_lo = split(jnp.concatenate(columns, axis=1))
    h1, slope1 = gelu_and_slope(times(w1, values3(x_hi, x_lo)))
    h1_hi, h1_lo = split(h1)
    h2, slope2 = gelu_and_slope(times(mix, values3(h1_hi, h1_lo)))
    h2_hi, h2_lo = split(h2)
    taps = times(w3, values3(h2_hi, h2_lo))

    sub = lax.broadcasted_iota(jnp.int32, (16, TW), 0)
    tap_col, tap_row = lax.rem(sub, 3), lax.div(sub, 3)
    zero16 = jnp.zeros((16, TW), F32)

    def by_col(x, by):
        return jnp.where(
            tap_col == 0, lane_shift(x, by), jnp.where(tap_col == 2, lane_shift(x, -by), x)
        )

    def by_row(first, middle, last):
        return jnp.where(
            tap_row == 0, first, jnp.where(tap_row == 1, middle, jnp.where(tap_row == 2, last, 0.0))
        )

    spread = []
    for t in range(number):
        moved = [zero16]
        for r in range(TR):
            at = (t * TR + r) * TW
            moved.append(by_col(taps[:, at : at + TW], 1))
        moved.append(zero16)
        errors = [zero16]
        for r in range(TR):
            summed = jnp.sum(by_row(moved[r], moved[r + 1], moved[r + 2]), axis=0, keepdims=True)
            errors.append(by_col(jnp.broadcast_to(2.0 * (summed + gaps[t][r]), (16, TW)), -1))
        errors.append(zero16)
        spread += [by_row(errors[r + 2], errors[r + 1], errors[r]) for r in range(TR)]
    e_hi, e_lo = split(jnp.concatenate(spread, axis=1))
    d2_hi, d2_lo = split(times(w3_t, values3(e_hi, e_lo)) * slope2)
    d1_hi, d1_lo = split(times(mix_t, values3(d2_hi, d2_lo)) * slope1)

    result = []
    for t in range(number):
        own = slice(t * TR * TW, (t + 1) * TR * TW)
        both = lambda high, low: jnp.concatenate([high[:, own], low[:, own]], axis=0)
        result.append(
            jnp.concatenate(
                [
                    over_cells(both(d2_hi, d2_lo), both(h1_hi, h1_lo)),
                    over_cells(both(x_hi, x_lo), both(d1_hi, d1_lo)),
                    over_cells(both(e_hi, e_lo), both(h2_hi, h2_lo)),
                ],
                axis=0,
            )
        )
    return result


def gradient_kernel(snapshot, part, sends, slots, counts, xin, base, params, out, total):
    buffers = out.shape[0]
    total[...] = jnp.zeros_like(total)
    packed = params[...]
    mix = packed[:, 0:64]
    w1 = packed[0:48, 64:128]
    w3 = packed[48:64, 64:128]
    weights = (weights3(w1.T), weights3(mix), weights3(w3), weights3(w3.T), weights3(mix.T))

    def body(i, carry):
        at = [part * sends + i * BATCH + k for k in range(BATCH)]
        cells = [[xin[j, r] for r in range(TR)] for j in at]
        gaps = [[base[j, r : r + 1, :] for r in range(TR)] for j in at]
        number = counts[snapshot, part]
        for k, grad in enumerate(batch_gradients(cells, gaps, weights)):
            buffer = jnp.where(i * BATCH + k < number, slots[snapshot, at[k]], 0)
            total[buffer] += grad
        return carry

    lax.fori_loop(0, lax.div(counts[snapshot, part] + (BATCH - 1), BATCH), body, 0)

    row = lax.broadcasted_iota(jnp.int32, (48, 64), 0)

    def fold(b, carry):
        def parts(first, height):
            x = total[b, first : first + 2 * height, :]
            x = x[:height] + x[height:]
            return x[:, 0:64] + x[:, 64:128]

        d_w1 = jnp.where(lax.rem(row, 16) < 12, parts(128, 48), 0.0)
        out[b] = jnp.concatenate(
            [parts(0, 64), jnp.concatenate([d_w1, parts(224, 16)], axis=0)], axis=1
        )
        return carry

    lax.fori_loop(0, buffers, fold, 0)


def combine_kernel(entries, own, other, out):
    result = jnp.zeros(out.shape, F32)
    for b in range(own.shape[0]):
        full = own[b] + other[b]
        square = jnp.sum(full * full, keepdims=True)
        result = result + full * lax.rsqrt(square / entries + NORM_EPS)
    out[...] = result


def pack_weights(conv_in, mix_weight, conv_out):
    taps = conv_in.reshape(3, 3, conv_in.shape[1], 4)
    sides = jnp.concatenate([taps[:, 0], taps[:, 2], taps[:, 1], jnp.zeros_like(taps[:, 1])], axis=2)
    first = jnp.transpose(sides, (0, 2, 1)).reshape(48, conv_in.shape[1])
    last = jnp.pad(conv_out[:, 0, :], ((0, 7), (0, 0)))
    return jnp.concatenate([mix_weight, jnp.concatenate([first, last], axis=0)], axis=1)


def unpack_weights(packed):
    first = packed[0:48, 64:128].reshape(3, 4, 4, 64)
    taps = jnp.stack([first[:, 0], first[:, 2], first[:, 1]], axis=1)
    conv_in = jnp.transpose(taps.reshape(9, 4, 64), (0, 2, 1))
    return conv_in, packed[:, 0:64], packed[48:57, 64:128][:, None, :]


def local(
    initial_field,
    coef_index,
    kappa_table,
    drift_table,
    tile_pos,
    tile_dest,
    conv_in,
    mix_weight,
    conv_out,
):
    rows, lanes = initial_field.shape
    solvers = lax.axis_size("solver")
    trainers = lax.axis_size("trainer")
    half = solvers // 2
    j = lax.axis_index("solver")
    t = lax.axis_index("trainer")
    sends = tile_pos.shape[-1]
    entries = conv_in.size + mix_weight.size + conv_out.size

    def swap(x, axis, bit):
        count = lax.axis_size(axis)
        return lax.ppermute(x, axis, [(i, i ^ bit) for i in range(count)])

    both = jnp.stack([initial_field, (coef_index + 1).astype(F32)])
    edge = jnp.where(t == 0, both[:, :, lanes - EXT :], both[:, :, :EXT])
    ext = swap(edge, "trainer", 1)
    lane = lax.broadcasted_iota(jnp.int32, ext.shape, 2)
    ext = jnp.where((lane < LIVE) == (t == 0), ext, 0.0)
    down = jnp.concatenate([both[:, rows - STEPS :], ext[:, rows - STEPS :]], axis=2)
    up = jnp.concatenate([both[:, :STEPS], ext[:, :STEPS]], axis=2)
    above = lax.ppermute(down, "solver", [(i, i + 1) for i in range(solvers - 1)])
    below = lax.ppermute(up, "solver", [(i + 1, i) for i in range(solvers - 1)])

    vr, vc = drift_table[0], drift_table[1]
    coef = jnp.stack(
        [
            kappa_table + jnp.maximum(vr, 0.0),
            kappa_table - jnp.minimum(vr, 0.0),
            kappa_table + jnp.maximum(vc, 0.0),
            kappa_table - jnp.minimum(vc, 0.0),
        ]
    )
    none = jnp.zeros_like(kappa_table)
    channel = jnp.stack([none, kappa_table, vr, vc, none, kappa_table, vr, vc])
    fill = 127 - kappa_table.shape[0]
    coef = jnp.pad(coef, ((0, 4), (1, fill)))
    channel = jnp.pad(channel, ((0, 0), (1, fill)))

    sizes = (rows, lanes, sends, lanes // TW, half)
    tall, wide = rows + 2 * STEPS, lanes + EXT
    spare = -(-sends // BATCH) * BATCH
    final, xin, base, slots, counts = pl.pallas_call(
        functools.partial(field_kernel, sizes),
        out_shape=(
            jax.ShapeDtypeStruct((rows, lanes), F32),
            jax.ShapeDtypeStruct((SNAPS, sends + spare, TR, 8, TW), F32),
            jax.ShapeDtypeStruct((SNAPS, sends + spare, TR, TW), F32),
            jax.ShapeDtypeStruct((SNAPS, sends + spare), jnp.int32),
            jax.ShapeDtypeStruct((SNAPS, 2), jnp.int32),
        ),
        in_specs=[SMEM] * 3 + [VMEM] * 7,
        out_specs=(VMEM, VMEM, VMEM, SMEM, SMEM),
        scratch_shapes=[
            pltpu.VMEM((STEPS + 1, tall, wide), F32),
            pltpu.VMEM((tall, wide), jnp.int32),
            pltpu.VMEM((4, tall, wide), F32),
        ],
        compiler_params=PARAMS,
    )(
        j.reshape(1),
        tile_pos.reshape(SNAPS, sends),
        tile_dest.reshape(SNAPS, sends),
        initial_field,
        coef_index,
        ext,
        above,
        below,
        coef,
        channel,
    )

    params = pack_weights(conv_in, mix_weight, conv_out)
    change = jnp.zeros_like(params)
    work = 3 * 2 * 20000 * TR * TW * sends // 2

    def gradients(snapshot, part, params):
        return pl.pallas_call(
            functools.partial(gradient_kernel, snapshot, part, sends),
            out_shape=jax.ShapeDtypeStruct((half,) + params.shape, F32),
            in_specs=[SMEM] * 2 + [VMEM] * 3,
            out_specs=VMEM,
            scratch_shapes=[pltpu.VMEM((half, 256, 128), F32)],
            compiler_params=PARAMS,
            cost_estimate=pl.CostEstimate(
                flops=work * 16, bytes_accessed=1 << 21, transcendentals=1 << 20
            ),
        )(slots, counts, xin[snapshot], base[snapshot], params)

    for snapshot in range(SNAPS):
        far = gradients(snapshot, 0, params)
        arrived = swap(far, "solver", half)
        near = gradients(snapshot, 1, params) + arrived
        bit = 1
        while 2 * bit < half:
            near = near + swap(near, "solver", bit)
            bit = 2 * bit
        direction = pl.pallas_call(
            functools.partial(combine_kernel, entries),
            out_shape=jax.ShapeDtypeStruct(params.shape, F32),
            in_specs=[VMEM] * 2,
            out_specs=VMEM,
            compiler_params=PARAMS,
        )(near, swap(near, "solver", bit))
        direction = direction + swap(direction, "solver", half)
        direction = direction + swap(direction, "trainer", 1)
        direction = direction / (solvers * trainers)
        change = change + direction
        params = params - STEP_RATE * direction
    first, mix, last = unpack_weights(change)
    return (final, first, mix, last)


def solution(mesh):
    return jax.shard_map(
        local,
        mesh=mesh,
        in_specs=(
            P(("groups", "solver"), "trainer"),
            P(("groups", "solver"), "trainer"),
            P("groups"),
            P("groups", None),
            P("groups", "solver", "trainer", None),
            P("groups", "solver", "trainer", None, None),
            P("groups", None, None),
            P("groups", None),
            P("groups", None, None),
        ),
        out_specs=(
            P(("groups", "solver"), "trainer"),
            P("groups", None, None),
            P("groups", None),
            P("groups", None, None),
        ),
        check_vma=False,
    )
```

time: 632 us -> 95.4 us (0.15); the launches traced: 621 us -> 95.3 us
  matrix products: 286 us -> 0 us
  blocking collectives: 119 us -> 0 us
  other arithmetic: 95.3 us -> 3.03 us
  local copies, waits for them, and re-layouts: 45.3 us -> 1.14 us
  Pallas kernels: 0 us -> 38.9 us
  starting transfers between devices: 57 us -> 18.5 us
  waiting for transfers between devices: 9.74 us -> 32.9 us
    dot_general x156 -> x0, matrix products: 286 us -> none  [the longest x144 244 us: convolve(): jnp.einsum('oc,cbrw->obrw', kernel[3 * row_shift + col_shift], window, pr...]
    psum x2 -> x0, blocking collectives: 119 us -> none  [local(): direction = lax.psum(share, ('solver', 'trainer'))]
    pallas_call x0 -> x7, Pallas kernels: none -> 38.9 us  [the longest x4 30.2 us: gradients(): pl.pallas_call(functools.partial(gradient_kernel, snapshot, part, sends),...]
    sub x7 -> x1, other arithmetic: 36.2 us -> 0.08 us  [local(): params = params - STEP_RATE * direction]
    add_any x12 -> x0, other arithmetic: 35.8 us -> none  [the longest x4 18.5 us: convolve(): padded[:, :, row_shift:row_shift + height, col_shift:col_shift + breadth]]
    ppermute x16 -> x13, waiting for transfers between devices: 4.52 us -> 32.9 us  [the longest x11 27.2 us: swap(): return lax.ppermute(x, axis, [(i, i ^ bit) for i in range(count)])]
    all_to_all x4 -> x0, starting transfers between devices: 25.2 us -> none  [the longest x2 14.4 us: local(): lax.all_to_all(marks, 'solver', split_axis=0, concat_axis=0, tiled=True)]
    transpose x4 -> x0, other arithmetic: 15.9 us -> none  [convolve(): jnp.einsum('oc,cbrw->obrw', kernel[3 * row_shift + col_shift], window, pr...]
  transfers between devices with their start and end apart: 20 -> 13, of which waited for: 4 -> 13; matrix products, arithmetic and copies ran while one was open for 34% -> 0% of each run, Pallas kernels for 0% -> 13%
where the time goes in v1:
time: 95.4 us; the launch traced here: 95.3 us
  Pallas kernels  38.9 us (41%)
  waiting for transfers between devices  32.9 us (34%)
  starting transfers between devices  18.5 us (19%)
  other arithmetic  3.03 us (3%)
  local copies, waits for them, and re-layouts  1.14 us (1%)
    pallas_call x4, Pallas kernels, gradients(): pl.pallas_call(functools.partial(gradient_kernel, snapshot, part, sends),...  30.2 us
    ppermute x11, waiting for transfers between devices, swap(): return lax.ppermute(x, axis, [(i, i ^ bit) for i in range(count)])  27.2 us
    ppermute x11, starting transfers between devices, swap(): return lax.ppermute(x, axis, [(i, i ^ bit) for i in range(count)])  12.4 us
    pallas_call x1, Pallas kernels, local(): pl.pallas_call(functools.partial(field_kernel, sizes), out_shape=(jax.Sha...  8.4 us
    ppermute x1, starting transfers between devices, local(): lax.ppermute(down, 'solver', [(i, i + 1) for i in range(solvers - 1)])  4.77 us
    ppermute x1, waiting for transfers between devices, local(): below = lax.ppermute(up, 'solver', [(i + 1, i) for i in range(solvers - 1)])  4.12 us
  transfers between devices with their start and end apart: 13, of which 13 were waited for; matrix products, arithmetic and copies ran while one was open for 0% of the time, Pallas kernels for 13%

profile of v1, /device:TPU:0, one launch (start us, length us, event | category | flops | bytes accessed | tf_op | source)
XLA Modules:
  0.0 95.3 jit_solution(7959958450825884357)
XLA Ops:
  0.7 1.1 %convert_bitcast_fusion = f32[1,32,4096]{2,1,0:T(8,128)S(1)} fusion(s32[32,4096]{1,0:T(8,128)} %index.1), kind=kLoop, calls=%fused_computation.2 | loop fusion | flops 262144 | bytes 1048576 | tf_op jit(solution)/shard_map/stack | solution.py:307
  1.9 0.8 maximum_select_fusion
  2.7 0.5 collective-permute-start
  3.3 0.7 collective-permute-done
  4.1 4.8 %collective-permute-start.1 = (f32[2,4,4224]{2,1,0:T(4,128)S(1)}, f32[2,4,4224]{2,1,0:T(4,128)S(1)}, u32[]{:S(2)}, u32[]{:S(2)}) collective-permute-start(f32[2,4,4224]{2,1,0:T(4,128)S(1)} %get-tuple-element.23), channel_id=1, source_target_pairs={{0,2},{2,4},{4,6},{6,8},{8,10},{10,12},{12,14},{1,3},{3,5},{5,7},{... | collective-permute-start | bytes 405512 | tf_op jit(solution)/shard_map/ppermute | solution.py:314
  8.9 1.3 %collective-permute-start.2 = (f32[2,4,4224]{2,1,0:T(4,128)S(1)}, f32[2,4,4224]{2,1,0:T(4,128)S(1)}, u32[]{:S(2)}, u32[]{:S(2)}) collective-permute-start(f32[2,4,4224]{2,1,0:T(4,128)S(1)} %get-tuple-element.22), channel_id=1, source_target_pairs={{2,0},{4,2},{6,4},{8,6},{10,8},{12,10},{14,12},{3,1},{5,3},{7,5},{... | collective-permute-start | bytes 405512 | tf_op jit(solution)/shard_map/ppermute | solution.py:315
  10.4 1.6 %collective-permute-done.1.above = f32[2,4,4224]{2,1,0:T(4,128)S(1)} collective-permute-done((f32[2,4,4224]{2,1,0:T(4,128)S(1)}, f32[2,4,4224]{2,1,0:T(4,128)S(1)}, u32[]{:S(2)}, u32[]{:S(2)}) %collective-permute-start.1) | collective-permute-done | bytes 135200 | tf_op jit(solution)/shard_map/ppermute | solution.py:314
  12.0 4.1 %collective-permute-done.2.below = f32[2,4,4224]{2,1,0:T(4,128)S(1)} collective-permute-done((f32[2,4,4224]{2,1,0:T(4,128)S(1)}, f32[2,4,4224]{2,1,0:T(4,128)S(1)}, u32[]{:S(2)}, u32[]{:S(2)}) %collective-permute-start.2) | collective-permute-done | bytes 135200 | tf_op jit(solution)/shard_map/ppermute | solution.py:315
  16.1 8.4 %shard_map.120 = (f32[32,4096]{1,0:T(8,128)}, f32[2,48,4,8,128]{4,3,2,1,0:T(8,128)S(1)}, f32[2,48,4,128]{3,2,1,0:T(4,128)S(1)}, s32[2,48]{1,0:T(2,128)S(1)}, s32[2,2]{1,0:T(2,128)S(1)}) custom-call(s32[1]{0:T(128)} %bitcast.place, s32[2,24]{1,0:T(2,128)S(1)} %bitcast.67, s32[2,24]{1,0:T(2,128)S(1)} %bitcast.68, f32[32,4096]{1,0:T(8,128)S(1)} %copy-done, ...), custom_call_target="tpu_custom_call" | custom-call | tf_op jit(solution)/shard_map/pallas_call | solution.py:335
  24.7 8.7 %shard_map.122 = f32[4,64,128]{2,1,0:T(8,128)S(1)} custom-call(s32[2,48]{1,0:T(2,128)S(1)} %get-tuple-element.10.slots, s32[2,2]{1,0:T(2,128)S(1)} %get-tuple-element.11.counts, f32[48,4,8,128]{3,2,1,0:T(8,128)S(1)} %get-tuple-element.21.xin, f32[48,4,128]{2,1,0:T(4,128)S(1)} %get-tuple-element.25.base, f32[64,128]{1,0:T(8,128)S(1)} %fusion.2.params), custom_call_target="tpu_custom_call" | custom-call | flops 11796480000 | bytes 2097152 | tf_op jit(solution)/shard_map/pallas_call | solution.py:370
  33.4 0.9 collective-permute-start.3
  34.3 6.3 %shard_map.121 = f32[4,64,128]{2,1,0:T(8,128)S(1)} custom-call(s32[2,48]{1,0:T(2,128)S(1)} %get-tuple-element.10.slots, s32[2,2]{1,0:T(2,128)S(1)} %get-tuple-element.11.counts, f32[48,4,8,128]{3,2,1,0:T(8,128)S(1)} %get-tuple-element.21.xin, f32[48,4,128]{2,1,0:T(4,128)S(1)} %get-tuple-element.25.base, f32[64,128]{1,0:T(8,128)S(1)} %fusion.2.params), custom_call_target="tpu_custom_call" | custom-call | flops 11796480000 | bytes 2097152 | tf_op jit(solution)/shard_map/pallas_call | solution.py:370
  40.6 1.5 %collective-permute-done.3 = f32[4,64,128]{2,1,0:T(8,128)S(1)} collective-permute-done((f32[4,64,128]{2,1,0:T(8,128)S(1)}, f32[4,64,128]{2,1,0:T(8,128)S(1)}, u32[]{:S(2)}, u32[]{:S(2)}) %collective-permute-start.3) | collective-permute-done | bytes 131104 | tf_op jit(solution)/shard_map/ppermute | solution.py:305
  42.2 1.9 %collective-permute-start.4 = (f32[4,64,128]{2,1,0:T(8,128)S(1)}, f32[4,64,128]{2,1,0:T(8,128)S(1)}, u32[]{:S(2)}, u32[]{:S(2)}) collective-permute-start(f32[4,64,128]{2,1,0:T(8,128)S(1)} %add.50), channel_id=1, source_target_pairs={{0,2},{2,0},{4,6},{6,4},{8,10},{10,8},{12,14},{14,12},{1,3},{3,1},... | collective-permute-start | bytes 393224 | tf_op jit(solution)/shard_map/ppermute | solution.py:305
  44.1 3.1 %collective-permute-done.4 = f32[4,64,128]{2,1,0:T(8,128)S(1)} collective-permute-done((f32[4,64,128]{2,1,0:T(8,128)S(1)}, f32[4,64,128]{2,1,0:T(8,128)S(1)}, u32[]{:S(2)}, u32[]{:S(2)}) %collective-permute-start.4) | collective-permute-done | bytes 131104 | tf_op jit(solution)/shard_map/ppermute | solution.py:305
  47.3 4.9 %collective-permute-done.5.other = f32[4,64,128]{2,1,0:T(8,128)S(1)} collective-permute-done((f32[4,64,128]{2,1,0:T(8,128)S(1)}, f32[4,64,128]{2,1,0:T(8,128)S(1)}, u32[]{:S(2)}, u32[]{:S(2)}) %collective-permute-start.5) | collective-permute-done | bytes 131104 | tf_op jit(solution)/shard_map/ppermute | solution.py:305
  52.3 0.1 shard_map.123
  52.4 3.4 %collective-permute-start.6 = (f32[64,128]{1,0:T(8,128)S(1)}, f32[64,128]{1,0:T(8,128)S(1)}, u32[]{:S(2)}, u32[]{:S(2)}) collective-permute-start(f32[64,128]{1,0:T(8,128)S(1)} %shard_map.123), channel_id=1, source_target_pairs={{0,8},{2,10},{4,12},{6,14},{8,0},{10,2},{12,4},{14,6},{1,9},{3,11}... | collective-permute-start | bytes 98312 | tf_op jit(solution)/shard_map/ppermute | solution.py:305
  55.9 1.9 %collective-permute-done.6 = f32[64,128]{1,0:T(8,128)S(1)} collective-permute-done((f32[64,128]{1,0:T(8,128)S(1)}, f32[64,128]{1,0:T(8,128)S(1)}, u32[]{:S(2)}, u32[]{:S(2)}) %collective-permute-start.6) | collective-permute-done | bytes 32800 | tf_op jit(solution)/shard_map/ppermute | solution.py:305
  57.8 1.2 %collective-permute-done.7 = f32[64,128]{1,0:T(8,128)S(1)} collective-permute-done((f32[64,128]{1,0:T(8,128)S(1)}, f32[64,128]{1,0:T(8,128)S(1)}, u32[]{:S(2)}, u32[]{:S(2)}) %collective-permute-start.7) | collective-permute-done | bytes 32800 | tf_op jit(solution)/shard_map/ppermute | solution.py:305
  59.1 8.7 %shard_map.125 = f32[4,64,128]{2,1,0:T(8,128)S(1)} custom-call(s32[2,48]{1,0:T(2,128)S(1)} %get-tuple-element.10.slots, s32[2,2]{1,0:T(2,128)S(1)} %get-tuple-element.11.counts, f32[48,4,8,128]{3,2,1,0:T(8,128)S(1)} %get-tuple-element.20.xin, f32[48,4,128]{2,1,0:T(4,128)S(1)} %get-tuple-element.24.base, f32[64,128]{1,0:T(8,128)S(1)} %get-tuple-element.18.params), custom_call_target="tpu_custom_call" | custom-call | flops 11796480000 | bytes 2097152 | tf_op jit(solution)/shard_map/pallas_call | solution.py:370
  67.8 0.6 collective-permute-start.8
  68.3 6.4 %shard_map.124 = f32[4,64,128]{2,1,0:T(8,128)S(1)} custom-call(s32[2,48]{1,0:T(2,128)S(1)} %get-tuple-element.10.slots, s32[2,2]{1,0:T(2,128)S(1)} %get-tuple-element.11.counts, f32[48,4,8,128]{3,2,1,0:T(8,128)S(1)} %get-tuple-element.20.xin, f32[48,4,128]{2,1,0:T(4,128)S(1)} %get-tuple-element.24.base, f32[64,128]{1,0:T(8,128)S(1)} %get-tuple-element.18.params), custom_call_target="tpu_custom_call" | custom-call | flops 11796480000 | bytes 2097152 | tf_op jit(solution)/shard_map/pallas_call | solution.py:370
  74.8 2.3 %collective-permute-done.8 = f32[4,64,128]{2,1,0:T(8,128)S(1)} collective-permute-done((f32[4,64,128]{2,1,0:T(8,128)S(1)}, f32[4,64,128]{2,1,0:T(8,128)S(1)}, u32[]{:S(2)}, u32[]{:S(2)}) %collective-permute-start.8) | collective-permute-done | bytes 131104 | tf_op jit(solution)/shard_map/ppermute | solution.py:305
  77.1 2.4 %collective-permute-start.9 = (f32[4,64,128]{2,1,0:T(8,128)S(1)}, f32[4,64,128]{2,1,0:T(8,128)S(1)}, u32[]{:S(2)}, u32[]{:S(2)}) collective-permute-start(f32[4,64,128]{2,1,0:T(8,128)S(1)} %add.54), channel_id=1, source_target_pairs={{0,2},{2,0},{4,6},{6,4},{8,10},{10,8},{12,14},{14,12},{1,3},{3,1},... | collective-permute-start | bytes 393224 | tf_op jit(solution)/shard_map/ppermute | solution.py:305
  79.6 3.0 %collective-permute-done.9 = f32[4,64,128]{2,1,0:T(8,128)S(1)} collective-permute-done((f32[4,64,128]{2,1,0:T(8,128)S(1)}, f32[4,64,128]{2,1,0:T(8,128)S(1)}, u32[]{:S(2)}, u32[]{:S(2)}) %collective-permute-start.9) | collective-permute-done | bytes 131104 | tf_op jit(solution)/shard_map/ppermute | solution.py:305
  82.7 5.0 %collective-permute-done.10.other = f32[4,64,128]{2,1,0:T(8,128)S(1)} collective-permute-done((f32[4,64,128]{2,1,0:T(8,128)S(1)}, f32[4,64,128]{2,1,0:T(8,128)S(1)}, u32[]{:S(2)}, u32[]{:S(2)}) %collective-permute-start.10) | collective-permute-done | bytes 131104 | tf_op jit(solution)/shard_map/ppermute | solution.py:305
  87.8 2.5 %collective-permute-start.11 = (f32[64,128]{1,0:T(8,128)S(1)}, f32[64,128]{1,0:T(8,128)S(1)}, u32[]{:S(2)}, u32[]{:S(2)}) collective-permute-start(f32[64,128]{1,0:T(8,128)S(1)} %shard_map.126), channel_id=1, source_target_pairs={{0,8},{2,10},{4,12},{6,14},{8,0},{10,2},{12,4},{14,6},{1,9},{3,11}... | collective-permute-start | bytes 98312 | tf_op jit(solution)/shard_map/ppermute | solution.py:305
  90.3 2.4 %collective-permute-done.11 = f32[64,128]{1,0:T(8,128)S(1)} collective-permute-done((f32[64,128]{1,0:T(8,128)S(1)}, f32[64,128]{1,0:T(8,128)S(1)}, u32[]{:S(2)}, u32[]{:S(2)}) %collective-permute-start.11) | collective-permute-done | bytes 32800 | tf_op jit(solution)/shard_map/ppermute | solution.py:305
  92.7 1.2 %collective-permute-done.12 = f32[64,128]{1,0:T(8,128)S(1)} collective-permute-done((f32[64,128]{1,0:T(8,128)S(1)}, f32[64,128]{1,0:T(8,128)S(1)}, u32[]{:S(2)}, u32[]{:S(2)}) %collective-permute-start.12) | collective-permute-done | bytes 32800 | tf_op jit(solution)/shard_map/ppermute | solution.py:305
  94.1 0.6 copy.16
  94.7 0.6 pad_maximum_fusion.2
  (53 shorter events, 1.4 us)
Async XLA Ops:
  0.6 3.4 %copy-start = (f32[32,4096]{1,0:T(8,128)S(1)}, f32[32,4096]{1,0:T(8,128)}, u32[]{:S(2)}) copy-start(f32[32,4096]{1,0:T(8,128)} %u0.1) | copy-start | bytes 1572868
  0.6 2.5 %copy-start.6 = (f32[9,64,4]{1,2,0:T(4,128)S(1)}, f32[9,64,4]{1,2,0:T(4,128)}, u32[]{:S(2)}) copy-start(f32[9,64,4]{1,2,0:T(4,128)} %param.15) | copy-start | bytes 27652
  0.7 2.5 %copy-start.9 = (f32[16]{0:T(128)S(1)}, f32[16]{0:T(128)}, u32[]{:S(2)}) copy-start(f32[16]{0:T(128)} %param.11) | copy-start | bytes 196
  0.7 2.5 %copy-start.7 = (f32[2,16]{1,0:T(2,128)S(1)}, f32[2,16]{1,0:T(2,128)}, u32[]{:S(2)}) copy-start(f32[2,16]{1,0:T(2,128)} %param.12) | copy-start | bytes 388
  1.8 8.5 %copy-start.8 = (f32[9,1,64]{2,1,0:T(1,128)S(1)}, f32[9,1,64]{2,1,0:T(1,128)}, u32[]{:S(2)}) copy-start(f32[9,1,64]{2,1,0:T(1,128)} %param.17) | copy-start | bytes 6916
  1.8 8.5 %copy-start.4 = (f32[64,64]{1,0:T(8,128)S(1)}, f32[64,64]{1,0:T(8,128)}, u32[]{:S(2)}) copy-start(f32[64,64]{1,0:T(8,128)} %param.16) | copy-start | bytes 49156
  1.8 14.3 %copy-start.1 = (s32[32,4096]{1,0:T(8,128)S(1)}, s32[32,4096]{1,0:T(8,128)}, u32[]{:S(2)}) copy-start(s32[32,4096]{1,0:T(8,128)} %index.1) | copy-start | bytes 1572868
  1.8 14.3 %copy-start.2 = (s32[2,1,1,24]{3,2,1,0:T(1,128)S(1)}, s32[2,1,1,24]{3,2,1,0:T(1,128)}, u32[]{:S(2)}) copy-start(s32[2,1,1,24]{3,2,1,0:T(1,128)} %param.13) | copy-start | bytes 580
  1.9 14.3 %copy-start.3 = (s32[2,1,1,24,1]{3,4,2,1,0:T(1,128)S(1)}, s32[2,1,1,24,1]{3,4,2,1,0:T(1,128)}, u32[]{:S(2)}) copy-start(s32[2,1,1,24,1]{3,4,2,1,0:T(1,128)} %param.14) | copy-start | bytes 580
  2.7 1.3 %collective-permute-start = (f32[2,32,128]{2,1,0:T(8,128)S(1)}, f32[2,32,128]{2,1,0:T(8,128)S(1)}, u32[]{:S(2)}, u32[]{:S(2)}) collective-permute-start(f32[2,32,128]{2,1,0:T(8,128)S(1)} %maximum_select_fusion), channel_id=1, source_target_pairs={{0,1},{1,0},{2,3},{3,2},{4,5},{5,4},{6,7},{7,6},{8,9},{9,8},{10,11... | collective-permute-start | bytes 98312 | tf_op jit(solution)/shard_map/ppermute | solution.py:305
  4.1 7.9 %collective-permute-start.1 = (f32[2,4,4224]{2,1,0:T(4,128)S(1)}, f32[2,4,4224]{2,1,0:T(4,128)S(1)}, u32[]{:S(2)}, u32[]{:S(2)}) collective-permute-start(f32[2,4,4224]{2,1,0:T(4,128)S(1)} %get-tuple-element.23), channel_id=1, source_target_pairs={{0,2},{2,4},{4,6},{6,8},{8,10},{10,12},{12,14},{1,3},{3,5},{5,7},{... | collective-permute-start | bytes 405512 | tf_op jit(solution)/shard_map/ppermute | solution.py:314
  8.9 7.3 %collective-permute-start.2 = (f32[2,4,4224]{2,1,0:T(4,128)S(1)}, f32[2,4,4224]{2,1,0:T(4,128)S(1)}, u32[]{:S(2)}, u32[]{:S(2)}) collective-permute-start(f32[2,4,4224]{2,1,0:T(4,128)S(1)} %get-tuple-element.22), channel_id=1, source_target_pairs={{2,0},{4,2},{6,4},{8,6},{10,8},{12,10},{14,12},{3,1},{5,3},{7,5},{... | collective-permute-start | bytes 405512 | tf_op jit(solution)/shard_map/ppermute | solution.py:315
  33.4 8.7 %collective-permute-start.3 = (f32[4,64,128]{2,1,0:T(8,128)S(1)}, f32[4,64,128]{2,1,0:T(8,128)S(1)}, u32[]{:S(2)}, u32[]{:S(2)}) collective-permute-start(f32[4,64,128]{2,1,0:T(8,128)S(1)} %shard_map.122), channel_id=1, source_target_pairs={{0,8},{2,10},{4,12},{6,14},{8,0},{10,2},{12,4},{14,6},{1,9},{3,11}... | collective-permute-start | bytes 393224 | tf_op jit(solution)/shard_map/ppermute | solution.py:305
  42.2 5.0 %collective-permute-start.4 = (f32[4,64,128]{2,1,0:T(8,128)S(1)}, f32[4,64,128]{2,1,0:T(8,128)S(1)}, u32[]{:S(2)}, u32[]{:S(2)}) collective-permute-start(f32[4,64,128]{2,1,0:T(8,128)S(1)} %add.50), channel_id=1, source_target_pairs={{0,2},{2,0},{4,6},{6,4},{8,10},{10,8},{12,14},{14,12},{1,3},{3,1},... | collective-permute-start | bytes 393224 | tf_op jit(solution)/shard_map/ppermute | solution.py:305
  47.2 5.0 %collective-permute-start.5 = (f32[4,64,128]{2,1,0:T(8,128)S(1)}, f32[4,64,128]{2,1,0:T(8,128)S(1)}, u32[]{:S(2)}, u32[]{:S(2)}) collective-permute-start(f32[4,64,128]{2,1,0:T(8,128)S(1)} %add.51.own), channel_id=1, source_target_pairs={{0,4},{2,6},{4,0},{6,2},{8,12},{10,14},{12,8},{14,10},{1,5},{3,7},... | collective-permute-start | bytes 393224 | tf_op jit(solution)/shard_map/ppermute | solution.py:305
  52.4 5.3 %collective-permute-start.6 = (f32[64,128]{1,0:T(8,128)S(1)}, f32[64,128]{1,0:T(8,128)S(1)}, u32[]{:S(2)}, u32[]{:S(2)}) collective-permute-start(f32[64,128]{1,0:T(8,128)S(1)} %shard_map.123), channel_id=1, source_target_pairs={{0,8},{2,10},{4,12},{6,14},{8,0},{10,2},{12,4},{14,6},{1,9},{3,11}... | collective-permute-start | bytes 98312 | tf_op jit(solution)/shard_map/ppermute | solution.py:305
  57.8 1.2 %collective-permute-start.7 = (f32[64,128]{1,0:T(8,128)S(1)}, f32[64,128]{1,0:T(8,128)S(1)}, u32[]{:S(2)}, u32[]{:S(2)}) collective-permute-start(f32[64,128]{1,0:T(8,128)S(1)} %add.52), channel_id=1, source_target_pairs={{0,1},{1,0},{2,3},{3,2},{4,5},{5,4},{6,7},{7,6},{8,9},{9,8},{10,11... | collective-permute-start | bytes 98312 | tf_op jit(solution)/shard_map/ppermute | solution.py:305
  67.8 9.3 %collective-permute-start.8 = (f32[4,64,128]{2,1,0:T(8,128)S(1)}, f32[4,64,128]{2,1,0:T(8,128)S(1)}, u32[]{:S(2)}, u32[]{:S(2)}) collective-permute-start(f32[4,64,128]{2,1,0:T(8,128)S(1)} %shard_map.125), channel_id=1, source_target_pairs={{0,8},{2,10},{4,12},{6,14},{8,0},{10,2},{12,4},{14,6},{1,9},{3,11}... | collective-permute-start | bytes 393224 | tf_op jit(solution)/shard_map/ppermute | solution.py:305
  77.1 5.5 %collective-permute-start.9 = (f32[4,64,128]{2,1,0:T(8,128)S(1)}, f32[4,64,128]{2,1,0:T(8,128)S(1)}, u32[]{:S(2)}, u32[]{:S(2)}) collective-permute-start(f32[4,64,128]{2,1,0:T(8,128)S(1)} %add.54), channel_id=1, source_target_pairs={{0,2},{2,0},{4,6},{6,4},{8,10},{10,8},{12,14},{14,12},{1,3},{3,1},... | collective-permute-start | bytes 393224 | tf_op jit(solution)/shard_map/ppermute | solution.py:305
  82.6 5.0 %collective-permute-start.10 = (f32[4,64,128]{2,1,0:T(8,128)S(1)}, f32[4,64,128]{2,1,0:T(8,128)S(1)}, u32[]{:S(2)}, u32[]{:S(2)}) collective-permute-start(f32[4,64,128]{2,1,0:T(8,128)S(1)} %add.55.own), channel_id=1, source_target_pairs={{0,4},{2,6},{4,0},{6,2},{8,12},{10,14},{12,8},{14,10},{1,5},{3,7},... | collective-permute-start | bytes 393224 | tf_op jit(solution)/shard_map/ppermute | solution.py:305
  87.8 4.9 %collective-permute-start.11 = (f32[64,128]{1,0:T(8,128)S(1)}, f32[64,128]{1,0:T(8,128)S(1)}, u32[]{:S(2)}, u32[]{:S(2)}) collective-permute-start(f32[64,128]{1,0:T(8,128)S(1)} %shard_map.126), channel_id=1, source_target_pairs={{0,8},{2,10},{4,12},{6,14},{8,0},{10,2},{12,4},{14,6},{1,9},{3,11}... | collective-permute-start | bytes 98312 | tf_op jit(solution)/shard_map/ppermute | solution.py:305
  92.7 1.2 %collective-permute-start.12 = (f32[64,128]{1,0:T(8,128)S(1)}, f32[64,128]{1,0:T(8,128)S(1)}, u32[]{:S(2)}, u32[]{:S(2)}) collective-permute-start(f32[64,128]{1,0:T(8,128)S(1)} %add.56), channel_id=1, source_target_pairs={{0,1},{1,0},{2,3},{3,2},{4,5},{5,4},{6,7},{7,6},{8,9},{9,8},{10,11... | collective-permute-start | bytes 98312 | tf_op jit(solution)/shard_map/ppermute | solution.py:305
  93.9 1.4 %copy-start.5 = (f32[64,128]{1,0:T(8,128)}, f32[64,128]{1,0:T(8,128)S(1)}, u32[]{:S(2)}) copy-start(f32[64,128]{1,0:T(8,128)S(1)} %add_multiply_fusion) | copy-start | bytes 98308

commit v2 on v1

v2 whole, which is shorter than its diff:
```python
import functools

import jax
import jax.numpy as jnp
from jax import lax
from jax.experimental import pallas as pl
from jax.experimental.pallas import tpu as pltpu
from jax.sharding import PartitionSpec as P

TR = 4
TW = 128
SNAPS = 2
STEPS = 4
EXT = 128
LIVE = 64
BATCH = 4
FIRST = 3

F32 = jnp.float32
BF16 = jnp.bfloat16
STEP_RATE = 0.05
NORM_EPS = 1e-06
GELU_A = 0.7978845608028654
GELU_B = 0.044715

VMEM = pl.BlockSpec(memory_space=pltpu.VMEM)
SMEM = pl.BlockSpec(memory_space=pltpu.SMEM)
PARAMS = pltpu.CompilerParams(vmem_limit_bytes=24 * 1024 * 1024)


def look_up(tables, which, out):
    rows = [jnp.broadcast_to(tables[k : k + 1, :], (8, 128)) for k in range(4)]
    for c in range(which.shape[1] // 128):
        for r in range(which.shape[0] // 8):
            here = (slice(8 * r, 8 * r + 8), slice(128 * c, 128 * c + 128))
            for k in range(4):
                out[(k,) + here] = jnp.take_along_axis(rows[k], which[here], axis=1)


def advance(read, coef, write, tall, columns):
    lane = lax.broadcasted_iota(jnp.int32, (tall, 128), 1)
    cut = [slice(128 * c, 128 * c + 128) for c in range(columns)]
    before = pltpu.roll(read(cut[-1]), 1, 1)
    first = pltpu.roll(read(cut[0]), 127, 1)
    ahead = first
    for c in range(columns):
        center = read(cut[c])
        own = pltpu.roll(center, 1, 1)
        left = jnp.where(lane == 0, before, own)
        following = pltpu.roll(read(cut[c + 1]), 127, 1) if c + 1 < columns else first
        right = jnp.where(lane == 127, following, ahead)
        before, ahead = own, following
        up = pltpu.roll(center, 1, 0)
        down = pltpu.roll(center, tall - 1, 0)
        write(
            cut[c],
            center
            + coef(0, cut[c]) * (up - center)
            + coef(1, cut[c]) * (down - center)
            + coef(2, cut[c]) * (left - center)
            + coef(3, cut[c]) * (right - center),
        )


def inner_kernel(both, ext, tables, fields, coef, ids, start):
    rows, lanes = both.shape[1:]
    wide = lanes + EXT
    ids[:, 0:lanes] = both[1].astype(jnp.int32)
    ids[:, lanes:wide] = ext[1].astype(jnp.int32)
    start[:, 0:lanes] = both[0]
    start[:, lanes:wide] = ext[0]
    look_up(tables, ids, coef)
    for step in range(STEPS):
        source = start if step == 0 else fields.at[step - 1]
        target = fields.at[step]

        def write(cut, new):
            target[:, cut] = new

        advance(lambda cut: source[:, cut], lambda k, cut: coef[k, :, cut], write, rows, wide // 128)


def pick_tiles(snapshot, sizes, place, tile_pos, tile_dest, both, main, strip, picks, xin, base, slots, counts):
    sends, per_row, half, blocks = sizes
    mine = lax.div(place[0], half)
    sub = lax.broadcasted_iota(jnp.int32, (8, 128), 0)
    channel = picks[...]
    aways = [(lax.div(tile_dest[snapshot, k], half) != mine).astype(jnp.int32) for k in range(sends)]
    counts[0] = sum(aways)
    far, near = jnp.int32(0), sum(aways)
    for k in range(sends):
        away = aways[k]
        slot = jnp.where(away == 1, far, near)
        far, near = far + away, near + 1 - away
        slots[slot] = lax.rem(tile_dest[snapshot, k], half) + half * (1 - away)
        where = tile_pos[snapshot, k]
        block = lax.div(where, per_row)
        lanes = pl.ds(pl.multiple_of(lax.rem(where, per_row) * TW, TW), TW)
        group = pl.ds(pl.multiple_of(lax.div(block, 2) * 8, 8), 8)
        edge = (block == 0) | (block == blocks - 1)
        beside = pl.ds(pl.multiple_of(jnp.where(block == 0, 16, 0), 8), 8)
        lower = lax.rem(block, 2) == 1

        def tile(x):
            return jnp.where(lower, pltpu.roll(x, TR, 0), x)

        def value(at):
            return tile(jnp.where(edge, strip[at][beside, lanes], main[at][group, lanes]))

        old = value(0)
        which = tile(both[1, group, lanes]).astype(jnp.int32)
        base[slot] = (old - value(1))[0:TR]
        for r in range(TR):
            found = jnp.take_along_axis(channel, jnp.broadcast_to(which[r : r + 1], (8, 128)), axis=1)
            xin[slot, r] = jnp.where(sub % 4 == 0, jnp.broadcast_to(old[r : r + 1], (8, 128)), found)


def strip_coef(coef, outer, rows):
    return lambda k, cut: jnp.concatenate(
        [coef[k, rows - 8 : rows, cut], outer[k, :, cut], coef[k, 0:8, cut]], axis=0
    )


def first_strip_kernel(
    sizes, place, tile_pos, tile_dest, both, ext, first, second, tables, picks, coef, fields,
    xin, base, slots, counts, strip, outer, ids, work,
):
    rows, lanes = both.shape[1:]
    wide = lanes + EXT
    odd = lax.rem(place[0], 2) == 1
    above = [jnp.where(odd, first[k], second[k]) for k in range(2)]
    below = [jnp.where(odd, second[k], first[k]) for k in range(2)]
    ids[...] = jnp.concatenate([below[1], above[1]], axis=0).astype(jnp.int32)
    look_up(tables, ids, outer)
    work[0, 0:8, 0:lanes] = both[0, rows - 8 : rows]
    work[0, 0:8, lanes:wide] = ext[0, rows - 8 : rows]
    work[0, 8:16] = jnp.concatenate([below[0], above[0]], axis=0)
    work[0, 16:24, 0:lanes] = both[0, 0:8]
    work[0, 16:24, lanes:wide] = ext[0, 0:8]
    for step in range(2):
        source = work.at[step]
        target = work.at[1] if step == 0 else strip

        def write(cut, new):
            target[:, cut] = new

        advance(lambda cut: source[:, cut], strip_coef(coef, outer, rows), write, 24, wide // 128)
    pick_tiles(
        0, sizes, place, tile_pos, tile_dest, both, (fields.at[0], fields.at[1]), (work.at[1], strip),
        picks, xin, base, slots, counts,
    )


def second_strip_kernel(
    sizes, place, tile_pos, tile_dest, both, picks, coef, fields, strip, outer,
    final, xin, base, slots, counts, work,
):
    rows, lanes = both.shape[1:]
    wide = lanes + EXT
    for step in range(2):
        source = strip if step == 0 else work.at[0]
        target = work.at[step]

        def write(cut, new):
            target[:, cut] = new

        advance(lambda cut: source[:, cut], strip_coef(coef, outer, rows), write, 24, wide // 128)
    sub = lax.broadcasted_iota(jnp.int32, (8, lanes), 0)
    final[0:8] = jnp.where(sub < STEPS, work[1, 16:24, 0:lanes], fields[3, 0:8, 0:lanes])
    final[8 : rows - 8] = fields[3, 8 : rows - 8, 0:lanes]
    final[rows - 8 : rows] = jnp.where(sub >= 8 - STEPS, work[1, 0:8, 0:lanes], fields[3, rows - 8 : rows, 0:lanes])
    pick_tiles(
        1, sizes, place, tile_pos, tile_dest, both, (fields.at[2], fields.at[3]), (work.at[0], work.at[1]),
        picks, xin, base, slots, counts,
    )


def split(x):
    high = x.astype(BF16)
    return high, (x - high.astype(F32)).astype(BF16)


def weights3(w):
    high = w.astype(BF16).astype(F32)
    return jnp.concatenate([high, high, w - high], axis=1).astype(BF16)


def values3(high, low):
    return jnp.concatenate([high, low, high], axis=0)


def times(a, b):
    return lax.dot_general(a, b, (((1,), (0,)), ((), ())), preferred_element_type=F32)


def over_cells(a, b):
    return lax.dot_general(a, b, (((1,), (1,)), ((), ())), preferred_element_type=F32)


def gelu_and_slope(z):
    square = z * z
    t = jnp.tanh(z * (GELU_A + (GELU_A * GELU_B) * square))
    gate = 0.5 + 0.5 * t
    value = z * gate
    return value, gate + (value - value * gate) * (2 * GELU_A + (6 * GELU_A * GELU_B) * square)


def lane_shift(x, by):
    lane = lax.broadcasted_iota(jnp.int32, x.shape, 1)
    return jnp.where(lane == (0 if by == 1 else TW - 1), 0.0, pltpu.roll(x, by % TW, 1))


def batch_gradients(cells, gaps, weights):
    w1, mix, w3, w3_t, mix_t = weights
    number = len(cells)
    zero8 = jnp.zeros((8, TW), F32)
    sub8 = lax.broadcasted_iota(jnp.int32, (8, TW), 0)
    columns = []
    for tile in cells:
        sides = [jnp.where(sub8 < 4, lane_shift(x, 1), lane_shift(x, -1)) for x in tile]
        sides = [zero8] + sides + [zero8]
        center = [zero8] + list(tile) + [zero8]
        for r in range(TR):
            stacked = []
            for dr in range(3):
                stacked += [sides[r + dr], center[r + dr]]
            columns.append(jnp.concatenate(stacked, axis=0))
    x_hi, x_lo = split(jnp.concatenate(columns, axis=1))
    h1, slope1 = gelu_and_slope(times(w1, values3(x_hi, x_lo)))
    h1_hi, h1_lo = split(h1)
    h2, slope2 = gelu_and_slope(times(mix, values3(h1_hi, h1_lo)))
    h2_hi, h2_lo = split(h2)
    taps = times(w3, values3(h2_hi, h2_lo))

    sub = lax.broadcasted_iota(jnp.int32, (16, TW), 0)
    tap_col, tap_row = lax.rem(sub, 3), lax.div(sub, 3)
    zero16 = jnp.zeros((16, TW), F32)

    def by_col(x, by):
        return jnp.where(
            tap_col == 0, lane_shift(x, by), jnp.where(tap_col == 2, lane_shift(x, -by), x)
        )

    def by_row(first, middle, last):
        return jnp.where(
            tap_row == 0, first, jnp.where(tap_row == 1, middle, jnp.where(tap_row == 2, last, 0.0))
        )

    spread = []
    for t in range(number):
        moved = [zero16]
        for r in range(TR):
            at = (t * TR + r) * TW
            moved.append(by_col(taps[:, at : at + TW], 1))
        moved.append(zero16)
        errors = [zero16]
        for r in range(TR):
            summed = jnp.sum(by_row(moved[r], moved[r + 1], moved[r + 2]), axis=0, keepdims=True)
            errors.append(by_col(jnp.broadcast_to(2.0 * (summed + gaps[t][r]), (16, TW)), -1))
        errors.append(zero16)
        spread += [by_row(errors[r + 2], errors[r + 1], errors[r]) for r in range(TR)]
    e_hi, e_lo = split(jnp.concatenate(spread, axis=1))
    d2_hi, d2_lo = split(times(w3_t, values3(e_hi, e_lo)) * slope2)
    d1_hi, d1_lo = split(times(mix_t, values3(d2_hi, d2_lo)) * slope1)

    result = []
    for t in range(number):
        own = slice(t * TR * TW, (t + 1) * TR * TW)
        both = lambda high, low: jnp.concatenate([high[:, own], low[:, own]], axis=0)
        result.append(
            jnp.concatenate(
                [
                    over_cells(both(d2_hi, d2_lo), both(h1_hi, h1_lo)),
                    over_cells(both(x_hi, x_lo), both(d1_hi, d1_lo)),
                    over_cells(both(e_hi, e_lo), both(h2_hi, h2_lo)),
                ],
                axis=0,
            )
        )
    return result


def add_batches(first, last, sends, slots, xin, base, params, total):
    mix = jnp.concatenate([params[0:32, 0:64], params[0:32, 64:128]], axis=0)
    side, rest = params[32:56, 0:64], params[32:56, 64:128]
    none = jnp.zeros((8, 64), F32)
    taps = [[side[8 * r : 8 * r + 8], rest[4 * r : 4 * r + 4], none[0:4]] for r in range(3)]
    w1 = jnp.concatenate(sum(taps, []), axis=0)
    w3 = jnp.concatenate([rest[12:21], none[0:7]], axis=0)
    weights = (weights3(w1.T), weights3(mix), weights3(w3), weights3(w3.T), weights3(mix.T))

    def body(i, carry):
        at = [i * BATCH + k for k in range(BATCH)]
        cells = [[xin[j, r] for r in range(TR)] for j in at]
        gaps = [[base[j, r : r + 1, :] for r in range(TR)] for j in at]
        into = [slots[j] for j in at]
        if sends % BATCH:
            cells = [[jnp.where(j < sends, x, 0.0) for x in tile] for j, tile in zip(at, cells)]
            gaps = [[jnp.where(j < sends, x, 0.0) for x in tile] for j, tile in zip(at, gaps)]
            into = [jnp.where(j < sends, slot, 0) for j, slot in zip(at, into)]
        for buffer, grad in zip(into, batch_gradients(cells, gaps, weights)):
            total[buffer] += grad
        return carry

    lax.fori_loop(first, last, body, 0)


def fold(sums):
    def parts(first, height):
        x = sums[first : first + height, :] + sums[first + height : first + 2 * height, :]
        return x[:, 0:64] + x[:, 64:128]

    d_mix, d_w1, d_w3 = parts(0, 64), parts(128, 48), parts(224, 16)
    side = [d_w1[16 * r : 16 * r + 8] for r in range(3)]
    center = [d_w1[16 * r + 8 : 16 * r + 12] for r in range(3)]
    rest = jnp.concatenate(center + [d_w3[0:9], jnp.zeros((3, 64), F32)], axis=0)
    return jnp.concatenate(
        [
            jnp.concatenate([d_mix[0:32], d_mix[32:64]], axis=1),
            jnp.concatenate([jnp.concatenate(side, axis=0), rest], axis=1),
        ],
        axis=0,
    )


def batches_in_first(far, sends):
    return jnp.maximum(lax.div(far + (BATCH - 1), BATCH), FIRST * -(-sends // BATCH) // 4)


def first_gradient_kernel(sends, slots, counts, xin, base, params, far, total):
    half = far.shape[0]
    total[...] = jnp.zeros_like(total)
    add_batches(0, batches_in_first(counts[0], sends), sends, slots, xin, base, params, total)
    for b in range(half):
        far[b] = fold(total.at[b])


def second_gradient_kernel(sends, slots, counts, xin, base, params, begun, near, total):
    half = near.shape[0]
    total[half : 2 * half] = begun[half : 2 * half]
    last = -(-sends // BATCH)
    add_batches(batches_in_first(counts[0], sends), last, sends, slots, xin, base, params, total)
    for b in range(half):
        near[b] = fold(total.at[half + b])


def combine_kernel(entries, own, other, out):
    result = jnp.zeros(out.shape, F32)
    for b in range(own.shape[0]):
        full = own[b] + other[b]
        square = jnp.sum(full * full, keepdims=True)
        result = result + full * lax.rsqrt(square / entries + NORM_EPS)
    out[...] = result


def pack_weights(conv_in, mix_weight, conv_out):
    taps = jnp.transpose(conv_in, (0, 2, 1)).reshape(3, 3, 4, conv_in.shape[1])
    side = jnp.concatenate([taps[:, 0], taps[:, 2]], axis=1).reshape(24, conv_in.shape[1])
    rest = jnp.concatenate(
        [taps[:, 1].reshape(12, conv_in.shape[1]), jnp.pad(conv_out[:, 0, :], ((0, 3), (0, 0)))], axis=0
    )
    mix = jnp.concatenate([mix_weight[0:32], mix_weight[32:64]], axis=1)
    return jnp.concatenate([mix, jnp.concatenate([side, rest], axis=1)], axis=0)


def unpack_weights(packed):
    side = packed[32:56, 0:64].reshape(3, 2, 4, 64)
    center = packed[32:44, 64:128].reshape(3, 4, 64)
    taps = jnp.stack([side[:, 0], center, side[:, 1]], axis=1)
    conv_in = jnp.transpose(taps.reshape(9, 4, 64), (0, 2, 1))
    mix = jnp.concatenate([packed[0:32, 0:64], packed[0:32, 64:128]], axis=0)
    return conv_in, mix, packed[44:53, 64:128][:, None, :]


def local(
    initial_field,
    coef_index,
    kappa_table,
    drift_table,
    tile_pos,
    tile_dest,
    conv_in,
    mix_weight,
    conv_out,
):
    rows, lanes = initial_field.shape
    solvers = lax.axis_size("solver")
    trainers = lax.axis_size("trainer")
    half = solvers // 2
    j = lax.axis_index("solver")
    t = lax.axis_index("trainer")
    sends = tile_pos.shape[-1]
    entries = conv_in.size + mix_weight.size + conv_out.size

    def swap(x, axis, bit):
        count = lax.axis_size(axis)
        return lax.ppermute(x, axis, [(i, i ^ bit) for i in range(count)])

    both = lax.optimization_barrier(jnp.stack([initial_field, (coef_index + 1).astype(F32)]))
    ext = swap(jnp.where(t == 0, both[:, :, lanes - EXT :], both[:, :, :EXT]), "trainer", 1)
    lane = lax.broadcasted_iota(jnp.int32, ext.shape, 2)
    ext = jnp.where((lane < LIVE) == (t == 0), ext, 0.0)

    def rows_from(start):
        part = lambda x: lax.dynamic_slice_in_dim(x, start, STEPS, 1)
        return jnp.concatenate([part(both), part(ext)], axis=2)

    odd = j % 2 == 1
    last = rows - STEPS
    inner = [(i, i ^ 1) for i in range(solvers)]
    outer_pairs = [(i, i + 1) for i in range(1, solvers - 1, 2)] + [(i + 1, i) for i in range(1, solvers - 1, 2)]
    first = lax.ppermute(rows_from(jnp.where(odd, 0, last)), "solver", inner)
    second = lax.ppermute(rows_from(jnp.where(odd, last, 0)), "solver", outer_pairs)

    vr, vc = drift_table[0], drift_table[1]
    tables = jnp.stack(
        [
            kappa_table + jnp.maximum(vr, 0.0),
            kappa_table - jnp.minimum(vr, 0.0),
            kappa_table + jnp.maximum(vc, 0.0),
            kappa_table - jnp.minimum(vc, 0.0),
        ]
    )
    none = jnp.zeros_like(kappa_table)
    channel = jnp.stack([none, kappa_table, vr, vc, none, kappa_table, vr, vc])
    fill = 127 - kappa_table.shape[0]
    tables = jnp.pad(tables, ((0, 4), (1, fill)))
    channel = jnp.pad(channel, ((0, 0), (1, fill)))

    sizes = (sends, lanes // TW, half, rows // TR)
    wide = lanes + EXT
    spare = -sends % BATCH
    place = j.reshape(1)
    tile_pos = tile_pos.reshape(SNAPS, sends)
    tile_dest = tile_dest.reshape(SNAPS, sends)
    tile_shapes = (
        jax.ShapeDtypeStruct((sends + spare, TR, 8, TW), F32),
        jax.ShapeDtypeStruct((sends + spare, TR, TW), F32),
        jax.ShapeDtypeStruct((sends + spare,), jnp.int32),
        jax.ShapeDtypeStruct((1,), jnp.int32),
    )
    tile_specs = (VMEM, VMEM, SMEM, SMEM)
    fields, coef = pl.pallas_call(
        inner_kernel,
        out_shape=(
            jax.ShapeDtypeStruct((STEPS, rows, wide), F32),
            jax.ShapeDtypeStruct((4, rows, wide), F32),
        ),
        in_specs=[VMEM] * 3,
        out_specs=(VMEM, VMEM),
        scratch_shapes=[pltpu.VMEM((rows, wide), jnp.int32), pltpu.VMEM((rows, wide), F32)],
        compiler_params=PARAMS,
        cost_estimate=pl.CostEstimate(flops=1 << 31, bytes_accessed=1 << 23, transcendentals=0),
    )(both, ext, tables)
    *tiles_0, strip, outer = pl.pallas_call(
        functools.partial(first_strip_kernel, sizes),
        out_shape=tile_shapes
        + (jax.ShapeDtypeStruct((24, wide), F32), jax.ShapeDtypeStruct((4, 8, wide), F32)),
        in_specs=[SMEM] * 3 + [VMEM] * 8,
        out_specs=tile_specs + (VMEM, VMEM),
        scratch_shapes=[pltpu.VMEM((8, wide), jnp.int32), pltpu.VMEM((2, 24, wide), F32)],
        compiler_params=PARAMS,
    )(place, tile_pos, tile_dest, both, ext, first, second, tables, channel, coef, fields)

    def second_part(fields, strip):
        return pl.pallas_call(
            functools.partial(second_strip_kernel, sizes),
            out_shape=(jax.ShapeDtypeStruct((rows, lanes), F32),) + tile_shapes,
            in_specs=[SMEM] * 3 + [VMEM] * 6,
            out_specs=(VMEM,) + tile_specs,
            scratch_shapes=[pltpu.VMEM((2, 24, wide), F32)],
            compiler_params=PARAMS,
            cost_estimate=pl.CostEstimate(flops=1 << 31, bytes_accessed=1 << 23, transcendentals=0),
        )(place, tile_pos, tile_dest, both, channel, coef, fields, strip, outer)

    params = pack_weights(conv_in, mix_weight, conv_out)
    change = jnp.zeros_like(params)
    work = 3 * 2 * 20000 * TR * TW * sends // 2

    def gradients(kernel, tiles, params, begun, out_shape, scratch, share):
        xin, base, slots, counts = tiles
        return pl.pallas_call(
            functools.partial(kernel, sends),
            out_shape=out_shape,
            in_specs=[SMEM] * 2 + [VMEM] * (3 + len(begun)),
            out_specs=jax.tree.map(lambda _: VMEM, out_shape),
            scratch_shapes=scratch,
            compiler_params=PARAMS,
            cost_estimate=pl.CostEstimate(
                flops=int(work * 32 * share), bytes_accessed=1 << 21, transcendentals=1 << 20
            ),
        )(slots, counts, xin, base, params, *begun)

    folded = jax.ShapeDtypeStruct((half,) + params.shape, F32)
    totals = (2 * half, 256, 128)
    tiles = tiles_0
    for snapshot in range(SNAPS):
        far, begun = gradients(
            first_gradient_kernel, tiles, params, [], (folded, jax.ShapeDtypeStruct(totals, F32)), [], 0.75
        )
        arrived = swap(far, "solver", half)
        near = gradients(
            second_gradient_kernel, tiles, params, [begun], folded, [pltpu.VMEM(totals, F32)], 0.5
        )
        near = near + arrived
        if snapshot == 0:
            near, fields, strip = lax.optimization_barrier((near, fields, strip))
            final, *tiles = second_part(fields, strip)
        bit = 1
        while 2 * bit < half:
            near = near + swap(near, "solver", bit)
            bit = 2 * bit
            if snapshot == 0:
                near, *tiles = lax.optimization_barrier((near, *tiles))
        direction = pl.pallas_call(
            functools.partial(combine_kernel, entries),
            out_shape=jax.ShapeDtypeStruct(params.shape, F32),
            in_specs=[VMEM] * 2,
            out_specs=VMEM,
            compiler_params=PARAMS,
        )(near, swap(near, "solver", bit))
        across = [(i, i ^ (half * trainers + 1)) for i in range(solvers * trainers)]
        direction = direction + lax.ppermute(direction, ("solver", "trainer"), across)
        direction = direction + swap(direction, "trainer", 1)
        direction = direction / (solvers * trainers)
        change = change + direction
        params = params - STEP_RATE * direction
    first, mix, last = unpack_weights(change)
    return (final, first, mix, last)


def solution(mesh):
    return jax.shard_map(
        local,
        mesh=mesh,
        in_specs=(
            P(("groups", "solver"), "trainer"),
            P(("groups", "solver"), "trainer"),
            P("groups"),
            P("groups", None),
            P("groups", "solver", "trainer", None),
            P("groups", "solver", "trainer", None, None),
            P("groups", None, None),
            P("groups", None),
            P("groups", None, None),
        ),
        out_specs=(
            P(("groups", "solver"), "trainer"),
            P("groups", None, None),
            P("groups", None),
            P("groups", None, None),
        ),
        check_vma=False,
    )
```

time: 95.4 us -> 86.5 us (0.907)
  waiting for transfers between devices: 32.9 us -> 27.2 us
  Pallas kernels: 38.9 us -> 36.7 us
  starting transfers between devices: 18.5 us -> 16.5 us
    ppermute x11 -> x9, waiting for transfers between devices: 27.2 us -> 17.7 us  [swap(): return lax.ppermute(x, axis, [(i, i ^ bit) for i in range(count)])]
    ppermute x2 -> x4, waiting for transfers between devices: 5.69 us -> 9.43 us  [the longest x2 8.84 us: local(): lax.ppermute(direction, ('solver', 'trainer'), across)]
    ppermute x2 -> x4, starting transfers between devices: 6.07 us -> 3.74 us  [the longest x1 2.93 us: local(): first = lax.ppermute(rows_from(jnp.where(odd, 0, last)), 'solver', inner)]
    pallas_call x5 -> x7, Pallas kernels: 38.6 us -> 36.4 us  [the longest x4 29 us: gradients(): pl.pallas_call(functools.partial(kernel, sends), out_shape=out_shape, in_...]
    another operation x2 -> x3, other arithmetic: 1.74 us -> 2.23 us  [the longest x2 2.22 us: local(): jnp.stack([initial_field, (coef_index + 1).astype(F32)])]
    ppermute x11 -> x9, starting transfers between devices: 12.4 us -> 12.8 us  [swap(): return lax.ppermute(x, axis, [(i, i ^ bit) for i in range(count)])]
  transfers between devices with their start and end apart: 13 -> 13, of which waited for: 13 -> 11; matrix products, arithmetic and copies ran while one was open for 0% -> 0% of each run, Pallas kernels for 13% -> 18%
where the time goes in v2:
time: 86.5 us; the launch traced here: 86.2 us
  Pallas kernels  36.7 us (42%)
  waiting for transfers between devices  27.2 us (31%)
  starting transfers between devices  16.5 us (19%)
  other arithmetic  3.21 us (4%)
  local copies, waits for them, and re-layouts  1.67 us (2%)
  between operations  0.96 us (1%)
    pallas_call x4, Pallas kernels, gradients(): pl.pallas_call(functools.partial(kernel, sends), out_shape=out_shape, in_...  29 us
    ppermute x9, waiting for transfers between devices, swap(): return lax.ppermute(x, axis, [(i, i ^ bit) for i in range(count)])  17.7 us
    ppermute x9, starting transfers between devices, swap(): return lax.ppermute(x, axis, [(i, i ^ bit) for i in range(count)])  12.8 us
    ppermute x2, waiting for transfers between devices, local(): lax.ppermute(direction, ('solver', 'trainer'), across)  8.84 us
    ppermute x1, starting transfers between devices, local(): first = lax.ppermute(rows_from(jnp.where(odd, 0, last)), 'solver', inner)  2.93 us
    pallas_call x1, Pallas kernels, local(): pl.pallas_call(inner_kernel, out_shape=(jax.ShapeDtypeStruct((STEPS, rows...  2.58 us
    pallas_call x1, Pallas kernels, second_part(): pl.pallas_call(functools.partial(second_strip_kernel, sizes), out_shape=(...  2.46 us
    pallas_call x1, Pallas kernels, local(): pl.pallas_call(functools.partial(first_strip_kernel, sizes), out_shape=ti...  2.4 us
  transfers between devices with their start and end apart: 13, of which 11 were waited for; matrix products, arithmetic and copies ran while one was open for 0% of the time, Pallas kernels for 18%

profile of v2, /device:TPU:0, one launch (start us, length us, event | category | flops | bytes accessed | tf_op | source)
XLA Modules:
  0.0 86.2 jit_solution(18046291545257583408)
XLA Ops:
  0.7 1.1 %convert_bitcast_fusion = f32[1,32,4096]{2,1,0:T(8,128)S(1)} fusion(s32[32,4096]{1,0:T(8,128)} %param.10), kind=kLoop, calls=%fused_computation.1 | loop fusion | flops 262144 | bytes 1048576 | tf_op jit(solution)/shard_map/stack | solution.py:399
  1.8 1.1 %pad_maximum_fusion.both = f32[2,32,4096]{2,1,0:T(8,128)S(1)} fusion(f32[1,32,4096]{2,1,0:T(8,128)S(1)} %convert_bitcast_fusion, f32[1,32,4096]{2,1,0:T(8,128)} %bitcast.65), kind=kLoop, calls=%fused_computation | loop fusion | flops 262144 | bytes 2097152 | tf_op jit(solution)/shard_map/stack | solution.py:399
  2.9 0.5 collective-permute-start
  3.9 0.4 collective-permute-done
  4.4 2.9 %collective-permute-start.1 = (f32[2,4,4224]{2,1,0:T(4,128)S(1)}, f32[2,4,4224]{2,1,0:T(4,128)S(1)}, u32[]{:S(2)}, u32[]{:S(2)}) collective-permute-start(f32[2,4,4224]{2,1,0:T(4,128)S(1)} %pad_maximum_fusion.1), channel_id=1, source_target_pairs={{0,2},{2,0},{4,6},{6,4},{8,10},{10,8},{12,14},{14,12},{1,3},{3,1},... | collective-permute-start | bytes 405512 | tf_op jit(solution)/shard_map/ppermute | solution.py:412
  7.4 0.7 collective-permute-start.2
  8.0 2.6 %shard_map.120 = (f32[4,32,4224]{2,1,0:T(8,128)S(1)}, f32[4,32,4224]{2,1,0:T(8,128)S(1)}) custom-call(f32[2,32,4096]{2,1,0:T(8,128)S(1)} %pad_maximum_fusion.both, f32[2,32,128]{2,1,0:T(8,128)S(1)} %broadcast_select_fusion.ext, f32[8,128]{1,0:T(8,128)S(1)} %select_maximum_fusion.1.tables), custom_call_target="tpu_custom_call" | custom-call | flops 2147483648 | bytes 8388608 | tf_op jit(solution)/shard_map/pallas_call | solution.py:443
  10.6 0.6 collective-permute-done.1.first
  11.2 2.4 %shard_map.121 = (f32[24,4,8,128]{3,2,1,0:T(8,128)S(1)}, f32[24,4,128]{2,1,0:T(4,128)S(1)}, s32[24]{0:T(128)S(1)}, s32[1]{0:T(128)}, f32[24,4224]{1,0:T(8,128)S(1)}, /*index=5*/f32[4,8,4224]{2,1,0:T(8,128)S(1)}) custom-call(s32[1]{0:T(128)} %bitcast.place, s32[2,24]{1,0:T(2,128)S(1)} %bitcast.61, s32[2,24]{1,0:T(2,128)S(1)} %bitcast.63, ...), custom_call_target="tpu_custom_call" | custom-call | tf_op jit(solution)/shard_map/pallas_call | solution.py:455
  13.6 9.1 %shard_map.122 = (f32[4,56,128]{2,1,0:T(8,128)S(1)}, f32[8,256,128]{2,1,0:T(8,128)S(1)}) custom-call(s32[24]{0:T(128)S(1)} %get-tuple-element.31.slots, s32[1]{0:T(128)} %get-tuple-element.32.counts, f32[24,4,8,128]{3,2,1,0:T(8,128)S(1)} %get-tuple-element.33.xin, f32[24,4,128]{2,1,0:T(4,128)S(1)} %get-tuple-element.34.base, f32[56,128]{1,0:T(8,128)S(1)} %fusion.1.params), custom_call_target="tpu_custom_call" | custom-call | flops 17694720000 | bytes 2097152 | tf_op jit(solution)/shard_map/pallas_call | solution.py:482
  22.8 7.0 %collective-permute-start.3 = (f32[4,56,128]{2,1,0:T(8,128)S(1)}, f32[4,56,128]{2,1,0:T(8,128)S(1)}, u32[]{:S(2)}, u32[]{:S(2)}) collective-permute-start(f32[4,56,128]{2,1,0:T(8,128)S(1)} %get-tuple-element.36), channel_id=1, source_target_pairs={{0,8},{2,10},{4,12},{6,14},{8,0},{10,2},{12,4},{14,6},{1,9},{3,11}... | collective-permute-start | bytes 344072 | tf_op jit(solution)/shard_map/ppermute | solution.py:397
  29.7 5.4 %shard_map.123 = f32[4,56,128]{2,1,0:T(8,128)S(1)} custom-call(s32[24]{0:T(128)S(1)} %get-tuple-element.31.slots, s32[1]{0:T(128)} %get-tuple-element.32.counts, f32[24,4,8,128]{3,2,1,0:T(8,128)S(1)} %get-tuple-element.33.xin, f32[24,4,128]{2,1,0:T(4,128)S(1)} %get-tuple-element.34.base, f32[56,128]{1,0:T(8,128)S(1)} %fusion.1.params, ...), custom_call_target="tpu_custom_call" | custom-call | flops 11796480000 | bytes 2097152 | tf_op jit(solution)/shard_map/pallas_call | solution.py:482
  35.1 0.6 collective-permute-start.4
  35.7 2.5 %shard_map.124 = (f32[32,4096]{1,0:T(8,128)}, f32[24,4,8,128]{3,2,1,0:T(8,128)S(1)}, f32[24,4,128]{2,1,0:T(4,128)S(1)}, s32[24]{0:T(128)S(1)}, s32[1]{0:T(128)}) custom-call(s32[1]{0:T(128)} %bitcast.place, s32[2,24]{1,0:T(2,128)S(1)} %bitcast.62, s32[2,24]{1,0:T(2,128)S(1)} %bitcast.64, f32[2,32,4096]{2,1,0:T(8,128)S(1)} %pad_maximum_fusion.both, ...), custom_call_target="tpu_custom_call" | custom-call | flops 2147483648 | bytes 8388608 | tf_op jit(solution)/shard_map/pallas_call | solution.py:466
  38.2 1.8 %collective-permute-done.4 = f32[4,56,128]{2,1,0:T(8,128)S(1)} collective-permute-done((f32[4,56,128]{2,1,0:T(8,128)S(1)}, f32[4,56,128]{2,1,0:T(8,128)S(1)}, u32[]{:S(2)}, u32[]{:S(2)}) %collective-permute-start.4) | collective-permute-done | bytes 114720 | tf_op jit(solution)/shard_map/ppermute | solution.py:397
  40.0 1.6 %collective-permute-start.5 = (f32[4,56,128]{2,1,0:T(8,128)S(1)}, f32[4,56,128]{2,1,0:T(8,128)S(1)}, u32[]{:S(2)}, u32[]{:S(2)}) collective-permute-start(f32[4,56,128]{2,1,0:T(8,128)S(1)} %add.60.own), channel_id=1, source_target_pairs={{0,4},{2,6},{4,0},{6,2},{8,12},{10,14},{12,8},{14,10},{1,5},{3,7},... | collective-permute-start | bytes 344072 | tf_op jit(solution)/shard_map/ppermute | solution.py:397
  41.7 3.2 %collective-permute-done.5.other = f32[4,56,128]{2,1,0:T(8,128)S(1)} collective-permute-done((f32[4,56,128]{2,1,0:T(8,128)S(1)}, f32[4,56,128]{2,1,0:T(8,128)S(1)}, u32[]{:S(2)}, u32[]{:S(2)}) %collective-permute-start.5) | collective-permute-done | bytes 114720 | tf_op jit(solution)/shard_map/ppermute | solution.py:397
  45.1 4.2 %collective-permute-done.6 = f32[56,128]{1,0:T(8,128)S(1)} collective-permute-done((f32[56,128]{1,0:T(8,128)S(1)}, f32[56,128]{1,0:T(8,128)S(1)}, u32[]{:S(2)}, u32[]{:S(2)}) %collective-permute-start.6) | collective-permute-done | bytes 28704 | tf_op jit(solution)/shard_map/ppermute | solution.py:523
  49.3 1.2 %collective-permute-done.7 = f32[56,128]{1,0:T(8,128)S(1)} collective-permute-done((f32[56,128]{1,0:T(8,128)S(1)}, f32[56,128]{1,0:T(8,128)S(1)}, u32[]{:S(2)}, u32[]{:S(2)}) %collective-permute-start.7) | collective-permute-done | bytes 28704 | tf_op jit(solution)/shard_map/ppermute | solution.py:397
  50.5 9.1 %shard_map.126 = (f32[4,56,128]{2,1,0:T(8,128)S(1)}, f32[8,256,128]{2,1,0:T(8,128)S(1)}) custom-call(s32[24]{0:T(128)S(1)} %get-tuple-element.48.slots, s32[1]{0:T(128)} %get-tuple-element.49.counts, f32[24,4,8,128]{3,2,1,0:T(8,128)S(1)} %get-tuple-element.50.xin, f32[24,4,128]{2,1,0:T(4,128)S(1)} %get-tuple-element.51.base, ...), custom_call_target="tpu_custom_call" | custom-call | flops 17694720000 | bytes 2097152 | tf_op jit(solution)/shard_map/pallas_call | solution.py:482
  59.7 1.5 %collective-permute-start.8 = (f32[4,56,128]{2,1,0:T(8,128)S(1)}, f32[4,56,128]{2,1,0:T(8,128)S(1)}, u32[]{:S(2)}, u32[]{:S(2)}) collective-permute-start(f32[4,56,128]{2,1,0:T(8,128)S(1)} %get-tuple-element.53), channel_id=1, source_target_pairs={{0,8},{2,10},{4,12},{6,14},{8,0},{10,2},{12,4},{14,6},{1,9},{3,11}... | collective-permute-start | bytes 344072 | tf_op jit(solution)/shard_map/ppermute | solution.py:397
  61.2 5.4 %shard_map.127 = f32[4,56,128]{2,1,0:T(8,128)S(1)} custom-call(s32[24]{0:T(128)S(1)} %get-tuple-element.48.slots, s32[1]{0:T(128)} %get-tuple-element.49.counts, f32[24,4,8,128]{3,2,1,0:T(8,128)S(1)} %get-tuple-element.50.xin, f32[24,4,128]{2,1,0:T(4,128)S(1)} %get-tuple-element.51.base, f32[56,128]{1,0:T(8,128)S(1)} %get-tuple-element.58.params, ...), custom_call_target="tpu_custom_call" | custom-call | flops 11796480000 | bytes 2097152 | tf_op jit(solution)/shard_map/pallas_call | solution.py:482
  66.5 1.7 %collective-permute-done.8 = f32[4,56,128]{2,1,0:T(8,128)S(1)} collective-permute-done((f32[4,56,128]{2,1,0:T(8,128)S(1)}, f32[4,56,128]{2,1,0:T(8,128)S(1)}, u32[]{:S(2)}, u32[]{:S(2)}) %collective-permute-start.8) | collective-permute-done | bytes 114720 | tf_op jit(solution)/shard_map/ppermute | solution.py:397
  68.3 1.1 %collective-permute-start.9 = (f32[4,56,128]{2,1,0:T(8,128)S(1)}, f32[4,56,128]{2,1,0:T(8,128)S(1)}, u32[]{:S(2)}, u32[]{:S(2)}) collective-permute-start(f32[4,56,128]{2,1,0:T(8,128)S(1)} %add.63), channel_id=1, source_target_pairs={{0,2},{2,0},{4,6},{6,4},{8,10},{10,8},{12,14},{14,12},{1,3},{3,1},... | collective-permute-start | bytes 344072 | tf_op jit(solution)/shard_map/ppermute | solution.py:397
  69.4 3.8 %collective-permute-done.9 = f32[4,56,128]{2,1,0:T(8,128)S(1)} collective-permute-done((f32[4,56,128]{2,1,0:T(8,128)S(1)}, f32[4,56,128]{2,1,0:T(8,128)S(1)}, u32[]{:S(2)}, u32[]{:S(2)}) %collective-permute-start.9) | collective-permute-done | bytes 114720 | tf_op jit(solution)/shard_map/ppermute | solution.py:397
  73.2 0.5 collective-permute-start.10
  73.7 4.4 %collective-permute-done.10.other = f32[4,56,128]{2,1,0:T(8,128)S(1)} collective-permute-done((f32[4,56,128]{2,1,0:T(8,128)S(1)}, f32[4,56,128]{2,1,0:T(8,128)S(1)}, u32[]{:S(2)}, u32[]{:S(2)}) %collective-permute-start.10) | collective-permute-done | bytes 114720 | tf_op jit(solution)/shard_map/ppermute | solution.py:397
  78.3 4.7 %collective-permute-done.11 = f32[56,128]{1,0:T(8,128)S(1)} collective-permute-done((f32[56,128]{1,0:T(8,128)S(1)}, f32[56,128]{1,0:T(8,128)S(1)}, u32[]{:S(2)}, u32[]{:S(2)}) %collective-permute-start.11) | collective-permute-done | bytes 28704 | tf_op jit(solution)/shard_map/ppermute | solution.py:523
  83.0 1.2 %collective-permute-done.12 = f32[56,128]{1,0:T(8,128)S(1)} collective-permute-done((f32[56,128]{1,0:T(8,128)S(1)}, f32[56,128]{1,0:T(8,128)S(1)}, u32[]{:S(2)}, u32[]{:S(2)}) %collective-permute-start.12) | collective-permute-done | bytes 28704 | tf_op jit(solution)/shard_map/ppermute | solution.py:397
  84.4 0.6 copy.19
  85.0 0.6 copy.18
  85.6 0.6 pad_maximum_fusion.3
  (55 shorter events, 1.3 us)
Async XLA Ops:
  0.6 2.8 %copy-start.5 = (f32[9,1,64]{2,1,0:T(1,128)S(1)}, f32[9,1,64]{2,1,0:T(1,128)}, u32[]{:S(2)}) copy-start(f32[9,1,64]{2,1,0:T(1,128)} %param.17) | copy-start | bytes 6916
  0.6 2.8 %copy-start.3 = (f32[9,64,4]{1,2,0:T(4,128)S(1)}, f32[9,64,4]{1,2,0:T(4,128)}, u32[]{:S(2)}) copy-start(f32[9,64,4]{1,2,0:T(4,128)} %param.15) | copy-start | bytes 27652
  0.7 2.8 %copy-start.2 = (f32[64,64]{1,0:T(8,128)S(1)}, f32[64,64]{1,0:T(8,128)}, u32[]{:S(2)}) copy-start(f32[64,64]{1,0:T(8,128)} %param.16) | copy-start | bytes 49156
  0.7 2.8 %copy-start.4 = (f32[2,16]{1,0:T(2,128)S(1)}, f32[2,16]{1,0:T(2,128)}, u32[]{:S(2)}) copy-start(f32[2,16]{1,0:T(2,128)} %param.12) | copy-start | bytes 388
  0.7 2.8 %copy-start.6 = (f32[16]{0:T(128)S(1)}, f32[16]{0:T(128)}, u32[]{:S(2)}) copy-start(f32[16]{0:T(128)} %param.11) | copy-start | bytes 196
  2.9 1.4 %collective-permute-start = (f32[2,32,128]{2,1,0:T(8,128)S(1)}, f32[2,32,128]{2,1,0:T(8,128)S(1)}, u32[]{:S(2)}, u32[]{:S(2)}) collective-permute-start(f32[2,32,128]{2,1,0:T(8,128)S(1)} %slice_select_fusion), channel_id=1, source_target_pairs={{0,1},{1,0},{2,3},{3,2},{4,5},{5,4},{6,7},{7,6},{8,9},{9,8},{10,11... | collective-permute-start | bytes 98312 | tf_op jit(solution)/shard_map/ppermute | solution.py:397
  4.4 6.8 %collective-permute-start.1 = (f32[2,4,4224]{2,1,0:T(4,128)S(1)}, f32[2,4,4224]{2,1,0:T(4,128)S(1)}, u32[]{:S(2)}, u32[]{:S(2)}) collective-permute-start(f32[2,4,4224]{2,1,0:T(4,128)S(1)} %pad_maximum_fusion.1), channel_id=1, source_target_pairs={{0,2},{2,0},{4,6},{6,4},{8,10},{10,8},{12,14},{14,12},{1,3},{3,1},... | collective-permute-start | bytes 405512 | tf_op jit(solution)/shard_map/ppermute | solution.py:412
  7.3 3.9 %copy-start = (s32[2,1,1,24]{3,2,1,0:T(1,128)S(1)}, s32[2,1,1,24]{3,2,1,0:T(1,128)}, u32[]{:S(2)}) copy-start(s32[2,1,1,24]{3,2,1,0:T(1,128)} %param.13) | copy-start | bytes 580
  7.3 3.9 %copy-start.1 = (s32[2,1,1,24,1]{3,4,2,1,0:T(1,128)S(1)}, s32[2,1,1,24,1]{3,4,2,1,0:T(1,128)}, u32[]{:S(2)}) copy-start(s32[2,1,1,24,1]{3,4,2,1,0:T(1,128)} %param.14) | copy-start | bytes 580
  7.4 3.9 %collective-permute-start.2 = (f32[2,4,4224]{2,1,0:T(4,128)S(1)}, f32[2,4,4224]{2,1,0:T(4,128)S(1)}, u32[]{:S(2)}, u32[]{:S(2)}) collective-permute-start(f32[2,4,4224]{2,1,0:T(4,128)S(1)} %pad_maximum_fusion.2), channel_id=1, source_target_pairs={{2,4},{6,8},{10,12},{4,2},{8,6},{12,10},{3,5},{7,9},{11,13},{5,3},... | collective-permute-start | bytes 405512 | tf_op jit(solution)/shard_map/ppermute | solution.py:413
  22.8 12.3 %collective-permute-start.3 = (f32[4,56,128]{2,1,0:T(8,128)S(1)}, f32[4,56,128]{2,1,0:T(8,128)S(1)}, u32[]{:S(2)}, u32[]{:S(2)}) collective-permute-start(f32[4,56,128]{2,1,0:T(8,128)S(1)} %get-tuple-element.36), channel_id=1, source_target_pairs={{0,8},{2,10},{4,12},{6,14},{8,0},{10,2},{12,4},{14,6},{1,9},{3,11}... | collective-permute-start | bytes 344072 | tf_op jit(solution)/shard_map/ppermute | solution.py:397
  35.1 4.9 %collective-permute-start.4 = (f32[4,56,128]{2,1,0:T(8,128)S(1)}, f32[4,56,128]{2,1,0:T(8,128)S(1)}, u32[]{:S(2)}, u32[]{:S(2)}) collective-permute-start(f32[4,56,128]{2,1,0:T(8,128)S(1)} %add.59), channel_id=1, source_target_pairs={{0,2},{2,0},{4,6},{6,4},{8,10},{10,8},{12,14},{14,12},{1,3},{3,1},... | collective-permute-start | bytes 344072 | tf_op jit(solution)/shard_map/ppermute | solution.py:397
  40.0 4.9 %collective-permute-start.5 = (f32[4,56,128]{2,1,0:T(8,128)S(1)}, f32[4,56,128]{2,1,0:T(8,128)S(1)}, u32[]{:S(2)}, u32[]{:S(2)}) collective-permute-start(f32[4,56,128]{2,1,0:T(8,128)S(1)} %add.60.own), channel_id=1, source_target_pairs={{0,4},{2,6},{4,0},{6,2},{8,12},{10,14},{12,8},{14,10},{1,5},{3,7},... | collective-permute-start | bytes 344072 | tf_op jit(solution)/shard_map/ppermute | solution.py:397
  45.0 4.3 %collective-permute-start.6 = (f32[56,128]{1,0:T(8,128)S(1)}, f32[56,128]{1,0:T(8,128)S(1)}, u32[]{:S(2)}, u32[]{:S(2)}) collective-permute-start(f32[56,128]{1,0:T(8,128)S(1)} %shard_map.125), channel_id=1, source_target_pairs={{0,9},{1,8},{2,11},{3,10},{4,13},{5,12},{6,15},{7,14},{8,1},{9,0},... | collective-permute-start | bytes 86024 | tf_op jit(solution)/shard_map/ppermute | solution.py:523
  49.3 1.2 %collective-permute-start.7 = (f32[56,128]{1,0:T(8,128)S(1)}, f32[56,128]{1,0:T(8,128)S(1)}, u32[]{:S(2)}, u32[]{:S(2)}) collective-permute-start(f32[56,128]{1,0:T(8,128)S(1)} %add.61), channel_id=1, source_target_pairs={{0,1},{1,0},{2,3},{3,2},{4,5},{5,4},{6,7},{7,6},{8,9},{9,8},{10,11... | collective-permute-start | bytes 86024 | tf_op jit(solution)/shard_map/ppermute | solution.py:397
  59.7 8.6 %collective-permute-start.8 = (f32[4,56,128]{2,1,0:T(8,128)S(1)}, f32[4,56,128]{2,1,0:T(8,128)S(1)}, u32[]{:S(2)}, u32[]{:S(2)}) collective-permute-start(f32[4,56,128]{2,1,0:T(8,128)S(1)} %get-tuple-element.53), channel_id=1, source_target_pairs={{0,8},{2,10},{4,12},{6,14},{8,0},{10,2},{12,4},{14,6},{1,9},{3,11}... | collective-permute-start | bytes 344072 | tf_op jit(solution)/shard_map/ppermute | solution.py:397
  68.3 4.9 %collective-permute-start.9 = (f32[4,56,128]{2,1,0:T(8,128)S(1)}, f32[4,56,128]{2,1,0:T(8,128)S(1)}, u32[]{:S(2)}, u32[]{:S(2)}) collective-permute-start(f32[4,56,128]{2,1,0:T(8,128)S(1)} %add.63), channel_id=1, source_target_pairs={{0,2},{2,0},{4,6},{6,4},{8,10},{10,8},{12,14},{14,12},{1,3},{3,1},... | collective-permute-start | bytes 344072 | tf_op jit(solution)/shard_map/ppermute | solution.py:397
  73.2 4.9 %collective-permute-start.10 = (f32[4,56,128]{2,1,0:T(8,128)S(1)}, f32[4,56,128]{2,1,0:T(8,128)S(1)}, u32[]{:S(2)}, u32[]{:S(2)}) collective-permute-start(f32[4,56,128]{2,1,0:T(8,128)S(1)} %add.64.own), channel_id=1, source_target_pairs={{0,4},{2,6},{4,0},{6,2},{8,12},{10,14},{12,8},{14,10},{1,5},{3,7},... | collective-permute-start | bytes 344072 | tf_op jit(solution)/shard_map/ppermute | solution.py:397
  78.2 4.7 %collective-permute-start.11 = (f32[56,128]{1,0:T(8,128)S(1)}, f32[56,128]{1,0:T(8,128)S(1)}, u32[]{:S(2)}, u32[]{:S(2)}) collective-permute-start(f32[56,128]{1,0:T(8,128)S(1)} %shard_map.128), channel_id=1, source_target_pairs={{0,9},{1,8},{2,11},{3,10},{4,13},{5,12},{6,15},{7,14},{8,1},{9,0},... | collective-permute-start | bytes 86024 | tf_op jit(solution)/shard_map/ppermute | solution.py:523
  82.9 1.2 %collective-permute-start.12 = (f32[56,128]{1,0:T(8,128)S(1)}, f32[56,128]{1,0:T(8,128)S(1)}, u32[]{:S(2)}, u32[]{:S(2)}) collective-permute-start(f32[56,128]{1,0:T(8,128)S(1)} %add.65), channel_id=1, source_target_pairs={{0,1},{1,0},{2,3},{3,2},{4,5},{5,4},{6,7},{7,6},{8,9},{9,8},{10,11... | collective-permute-start | bytes 86024 | tf_op jit(solution)/shard_map/ppermute | solution.py:397

commit v3 on v2

--- a/solution.py
+++ b/solution.py
@@ -13,8 +13,8 @@
 STEPS = 4
 EXT = 128
 LIVE = 64
-BATCH = 4
-FIRST = 3
+BATCH = 8
+FIRST = 2
 
 F32 = jnp.float32
 BF16 = jnp.bfloat16
@@ -80,13 +80,17 @@
         advance(lambda cut: source[:, cut], lambda k, cut: coef[k, :, cut], write, rows, wide // 128)
 
 
-def pick_tiles(snapshot, sizes, place, tile_pos, tile_dest, both, main, strip, picks, xin, base, slots, counts):
+def spare_slots(sends):
+    return -sends % BATCH
+
+
+def pick_tiles(snapshot, sizes, place, tile_pos, tile_dest, both, main, strip, tables, xin, base, slots):
     sends, per_row, half, blocks = sizes
     mine = lax.div(place[0], half)
     sub = lax.broadcasted_iota(jnp.int32, (8, 128), 0)
-    channel = picks[...]
+    channel = tables[8:16]
     aways = [(lax.div(tile_dest[snapshot, k], half) != mine).astype(jnp.int32) for k in range(sends)]
-    counts[0] = sum(aways)
+    slots[sends + spare_slots(sends)] = sum(aways)
     far, near = jnp.int32(0), sum(aways)
     for k in range(sends):
         away = aways[k]
@@ -122,19 +126,19 @@
 
 
 def first_strip_kernel(
-    sizes, place, tile_pos, tile_dest, both, ext, first, second, tables, picks, coef, fields,
-    xin, base, slots, counts, strip, outer, ids, work,
+    sizes, place, tile_pos, tile_dest, both, ext, first, second, tables, coef, fields, xin, base, slots, strip, outer, ids, work,
 ):
     rows, lanes = both.shape[1:]
     wide = lanes + EXT
     odd = lax.rem(place[0], 2) == 1
-    above = [jnp.where(odd, first[k], second[k]) for k in range(2)]
-    below = [jnp.where(odd, second[k], first[k]) for k in range(2)]
-    ids[...] = jnp.concatenate([below[1], above[1]], axis=0).astype(jnp.int32)
+    above = jnp.where(odd, first[...], second[...])
+    below = jnp.where(odd, second[...], first[...])
+    none = jnp.zeros((2, wide), F32)
+    ids[...] = jnp.concatenate([below[STEPS:], none, above[STEPS:]], axis=0).astype(jnp.int32)
     look_up(tables, ids, outer)
     work[0, 0:8, 0:lanes] = both[0, rows - 8 : rows]
     work[0, 0:8, lanes:wide] = ext[0, rows - 8 : rows]
-    work[0, 8:16] = jnp.concatenate([below[0], above[0]], axis=0)
+    work[0, 8:16] = jnp.concatenate([below[:STEPS], above[:STEPS]], axis=0)
     work[0, 16:24, 0:lanes] = both[0, 0:8]
     work[0, 16:24, lanes:wide] = ext[0, 0:8]
     for step in range(2):
@@ -147,13 +151,12 @@
         advance(lambda cut: source[:, cut], strip_coef(coef, outer, rows), write, 24, wide // 128)
     pick_tiles(
         0, sizes, place, tile_pos, tile_dest, both, (fields.at[0], fields.at[1]), (work.at[1], strip),
-        picks, xin, base, slots, counts,
+        tables, xin, base, slots,
     )
 
 
 def second_strip_kernel(
-    sizes, place, tile_pos, tile_dest, both, picks, coef, fields, strip, outer,
-    final, xin, base, slots, counts, work,
+    sizes, place, tile_pos, tile_dest, both, tables, coef, fields, strip, outer, final, xin, base, slots, work,
 ):
     rows, lanes = both.shape[1:]
     wide = lanes + EXT
@@ -171,7 +174,7 @@
     final[rows - 8 : rows] = jnp.where(sub >= 8 - STEPS, work[1, 0:8, 0:lanes], fields[3, rows - 8 : rows, 0:lanes])
     pick_tiles(
         1, sizes, place, tile_pos, tile_dest, both, (fields.at[2], fields.at[3]), (work.at[0], work.at[1]),
-        picks, xin, base, slots, counts,
+        tables, xin, base, slots,
     )
 
 
@@ -324,22 +327,22 @@
 
 
 def batches_in_first(far, sends):
-    return jnp.maximum(lax.div(far + (BATCH - 1), BATCH), FIRST * -(-sends // BATCH) // 4)
-
-
-def first_gradient_kernel(sends, slots, counts, xin, base, params, far, total):
+    return jnp.maximum(lax.div(far + (BATCH - 1), BATCH), FIRST * -(-sends // BATCH) // 3)
+
+
+def first_gradient_kernel(sends, slots, xin, base, params, far, total):
     half = far.shape[0]
     total[...] = jnp.zeros_like(total)
-    add_batches(0, batches_in_first(counts[0], sends), sends, slots, xin, base, params, total)
+    add_batches(0, batches_in_first(slots[sends + spare_slots(sends)], sends), sends, slots, xin, base, params, total)
     for b in range(half):
         far[b] = fold(total.at[b])
 
 
-def second_gradient_kernel(sends, slots, counts, xin, base, params, begun, near, total):
+def second_gradient_kernel(sends, slots, xin, base, params, begun, near, total):
     half = near.shape[0]
     total[half : 2 * half] = begun[half : 2 * half]
     last = -(-sends // BATCH)
-    add_batches(batches_in_first(counts[0], sends), last, sends, slots, xin, base, params, total)
+    add_batches(batches_in_first(slots[sends + spare_slots(sends)], sends), last, sends, slots, xin, base, params, total)
     for b in range(half):
         near[b] = fold(total.at[half + b])
 
@@ -363,13 +366,19 @@
     return jnp.concatenate([mix, jnp.concatenate([side, rest], axis=1)], axis=0)
 
 
-def unpack_weights(packed):
-    side = packed[32:56, 0:64].reshape(3, 2, 4, 64)
-    center = packed[32:44, 64:128].reshape(3, 4, 64)
-    taps = jnp.stack([side[:, 0], center, side[:, 1]], axis=1)
-    conv_in = jnp.transpose(taps.reshape(9, 4, 64), (0, 2, 1))
-    mix = jnp.concatenate([packed[0:32, 0:64], packed[0:32, 64:128]], axis=0)
-    return conv_in, mix, packed[44:53, 64:128][:, None, :]
+def unpack_kernel(one, other, conv_in, mix, conv_out):
+    mix_rows = mix.shape[0] // 2
+    for k in range(2):
+        at = slice(64 * k, 64 * k + 64)
+        mix[mix_rows * k : mix_rows * (k + 1)] = one[0:mix_rows, at] + other[0:mix_rows, at]
+    side = one[32:56, 0:64] + other[32:56, 0:64]
+    rest = one[32:56, 64:128] + other[32:56, 64:128]
+    for r in range(3):
+        conv_in[3 * r] = side[8 * r : 8 * r + 4]
+        conv_in[3 * r + 1] = rest[4 * r : 4 * r + 4]
+        conv_in[3 * r + 2] = side[8 * r + 4 : 8 * r + 8]
+    for k in range(9):
+        conv_out[k] = rest[12 + k : 13 + k]
 
 
 def local(
@@ -396,21 +405,27 @@
         count = lax.axis_size(axis)
         return lax.ppermute(x, axis, [(i, i ^ bit) for i in range(count)])
 
+    place = j.reshape(1)
+    tile_pos = tile_pos.reshape(SNAPS, sends)
+    tile_dest = tile_dest.reshape(SNAPS, sends)
     both = lax.optimization_barrier(jnp.stack([initial_field, (coef_index + 1).astype(F32)]))
     ext = swap(jnp.where(t == 0, both[:, :, lanes - EXT :], both[:, :, :EXT]), "trainer", 1)
     lane = lax.broadcasted_iota(jnp.int32, ext.shape, 2)
     ext = jnp.where((lane < LIVE) == (t == 0), ext, 0.0)
 
-    def rows_from(start):
-        part = lambda x: lax.dynamic_slice_in_dim(x, start, STEPS, 1)
-        return jnp.concatenate([part(both), part(ext)], axis=2)
+    def edge_rows(bottom):
+        def part(k, height):
+            start = jnp.where(bottom, rows - height, 0)
+            own = lax.dynamic_slice_in_dim(both[k], start, height, 0)
+            return jnp.concatenate([own, lax.dynamic_slice_in_dim(ext[k], start, height, 0)], axis=1)
+
+        return jnp.concatenate([part(0, STEPS), part(1, STEPS - 1)], axis=0)
 
     odd = j % 2 == 1
-    last = rows - STEPS
     inner = [(i, i ^ 1) for i in range(solvers)]
     outer_pairs = [(i, i + 1) for i in range(1, solvers - 1, 2)] + [(i + 1, i) for i in range(1, solvers - 1, 2)]
-    first = lax.ppermute(rows_from(jnp.where(odd, 0, last)), "solver", inner)
-    second = lax.ppermute(rows_from(jnp.where(odd, last, 0)), "solver", outer_pairs)
+    first = lax.ppermute(edge_rows(~odd), "solver", inner)
+    second = lax.ppermute(edge_rows(odd), "solver", outer_pairs)
 
     vr, vc = drift_table[0], drift_table[1]
     tables = jnp.stack(
@@ -424,22 +439,17 @@
     none = jnp.zeros_like(kappa_table)
     channel = jnp.stack([none, kappa_table, vr, vc, none, kappa_table, vr, vc])
     fill = 127 - kappa_table.shape[0]
-    tables = jnp.pad(tables, ((0, 4), (1, fill)))
-    channel = jnp.pad(channel, ((0, 0), (1, fill)))
+    tables = jnp.pad(jnp.concatenate([tables, jnp.zeros_like(tables), channel]), ((0, 0), (1, fill)))
 
     sizes = (sends, lanes // TW, half, rows // TR)
     wide = lanes + EXT
-    spare = -sends % BATCH
-    place = j.reshape(1)
-    tile_pos = tile_pos.reshape(SNAPS, sends)
-    tile_dest = tile_dest.reshape(SNAPS, sends)
+    spare = spare_slots(sends)
     tile_shapes = (
         jax.ShapeDtypeStruct((sends + spare, TR, 8, TW), F32),
         jax.ShapeDtypeStruct((sends + spare, TR, TW), F32),
-        jax.ShapeDtypeStruct((sends + spare,), jnp.int32),
-        jax.ShapeDtypeStruct((1,), jnp.int32),
-    )
-    tile_specs = (VMEM, VMEM, SMEM, SMEM)
+        jax.ShapeDtypeStruct((sends + spare + 1,), jnp.int32),
+    )
+    tile_specs = (VMEM, VMEM, SMEM)
     fields, coef = pl.pallas_call(
         inner_kernel,
         out_shape=(
@@ -447,7 +457,7 @@
             jax.ShapeDtypeStruct((4, rows, wide), F32),
         ),
         in_specs=[VMEM] * 3,
-        out_specs=(VMEM, VMEM),
+        out_specs=(VMEM,) * 2,
         scratch_shapes=[pltpu.VMEM((rows, wide), jnp.int32), pltpu.VMEM((rows, wide), F32)],
         compiler_params=PARAMS,
         cost_estimate=pl.CostEstimate(flops=1 << 31, bytes_accessed=1 << 23, transcendentals=0),
@@ -456,11 +466,11 @@
         functools.partial(first_strip_kernel, sizes),
         out_shape=tile_shapes
         + (jax.ShapeDtypeStruct((24, wide), F32), jax.ShapeDtypeStruct((4, 8, wide), F32)),
-        in_specs=[SMEM] * 3 + [VMEM] * 8,
+        in_specs=[SMEM] * 3 + [VMEM] * 7,
         out_specs=tile_specs + (VMEM, VMEM),
         scratch_shapes=[pltpu.VMEM((8, wide), jnp.int32), pltpu.VMEM((2, 24, wide), F32)],
         compiler_params=PARAMS,
-    )(place, tile_pos, tile_dest, both, ext, first, second, tables, channel, coef, fields)
+    )(place, tile_pos, tile_dest, both, ext, first, second, tables, coef, fields)
 
     def second_part(fields, strip):
         return pl.pallas_call(
@@ -471,25 +481,25 @@
             scratch_shapes=[pltpu.VMEM((2, 24, wide), F32)],
             compiler_params=PARAMS,
             cost_estimate=pl.CostEstimate(flops=1 << 31, bytes_accessed=1 << 23, transcendentals=0),
-        )(place, tile_pos, tile_dest, both, channel, coef, fields, strip, outer)
+        )(place, tile_pos, tile_dest, both, tables, coef, fields, strip, outer)
 
     params = pack_weights(conv_in, mix_weight, conv_out)
-    change = jnp.zeros_like(params)
+    changes = []
     work = 3 * 2 * 20000 * TR * TW * sends // 2
 
     def gradients(kernel, tiles, params, begun, out_shape, scratch, share):
-        xin, base, slots, counts = tiles
+        xin, base, slots = tiles
         return pl.pallas_call(
             functools.partial(kernel, sends),
             out_shape=out_shape,
-            in_specs=[SMEM] * 2 + [VMEM] * (3 + len(begun)),
+            in_specs=[SMEM] + [VMEM] * (3 + len(begun)),
             out_specs=jax.tree.map(lambda _: VMEM, out_shape),
             scratch_shapes=scratch,
             compiler_params=PARAMS,
             cost_estimate=pl.CostEstimate(
                 flops=int(work * 32 * share), bytes_accessed=1 << 21, transcendentals=1 << 20
             ),
-        )(slots, counts, xin, base, params, *begun)
+        )(slots, xin, base, params, *begun)
 
     folded = jax.ShapeDtypeStruct((half,) + params.shape, F32)
     totals = (2 * half, 256, 128)
@@ -523,10 +533,16 @@
         direction = direction + lax.ppermute(direction, ("solver", "trainer"), across)
         direction = direction + swap(direction, "trainer", 1)
         direction = direction / (solvers * trainers)
-        change = change + direction
+        changes.append(direction)
         params = params - STEP_RATE * direction
-    first, mix, last = unpack_weights(change)
-    return (final, first, mix, last)
+    first, mix, last = pl.pallas_call(
+        unpack_kernel,
+        out_shape=tuple(jax.ShapeDtypeStruct(w.shape, F32) for w in (jnp.transpose(conv_in, (0, 2, 1)), mix_weight, conv_out)),
+        in_specs=[VMEM] * 2,
+        out_specs=(VMEM,) * 3,
+        compiler_params=PARAMS,
+    )(*changes)
+    return (final, jnp.transpose(first, (0, 2, 1)), mix, last)
 
 
 def solution(mesh):

time: 86.5 us -> 80.5 us (0.931)
  Pallas kernels: 36.7 us -> 31.4 us
  local copies, waits for them, and re-layouts: 1.67 us -> 0.37 us
  waiting for transfers between devices: 27.2 us -> 28.4 us
    pallas_call x4, Pallas kernels: 29 us -> 22.9 us  [gradients(): pl.pallas_call(functools.partial(kernel, sends), out_shape=out_shape, in_...]
    ppermute x9, waiting for transfers between devices: 17.7 us -> 19.3 us  [swap(): return lax.ppermute(x, axis, [(i, i ^ bit) for i in range(count)])]
  transfers between devices with their start and end apart: 13 -> 13, of which waited for: 11 -> 12; matrix products, arithmetic and copies ran while one was open for 0% -> 1% of each run, Pallas kernels for 18% -> 17%
where the time goes in v3:
time: 80.5 us; the launch traced here: 80.3 us
  Pallas kernels  31.4 us (39%)
  waiting for transfers between devices  28.4 us (35%)
  starting transfers between devices  16.6 us (21%)
  other arithmetic  2.48 us (3%)
  between operations  1 us (1%)
    pallas_call x4, Pallas kernels, gradients(): pl.pallas_call(functools.partial(kernel, sends), out_shape=out_shape, in_...  22.9 us
    ppermute x9, waiting for transfers between devices, swap(): return lax.ppermute(x, axis, [(i, i ^ bit) for i in range(count)])  19.3 us
    ppermute x9, starting transfers between devices, swap(): return lax.ppermute(x, axis, [(i, i ^ bit) for i in range(count)])  12.9 us
    ppermute x2, waiting for transfers between devices, local(): lax.ppermute(direction, ('solver', 'trainer'), across)  8.57 us
    ppermute x1, starting transfers between devices, local(): first = lax.ppermute(edge_rows(~odd), 'solver', inner)  2.93 us
    pallas_call x1, Pallas kernels, local(): pl.pallas_call(inner_kernel, out_shape=(jax.ShapeDtypeStruct((STEPS, rows...  2.67 us
    pallas_call x1, Pallas kernels, second_part(): pl.pallas_call(functools.partial(second_strip_kernel, sizes), out_shape=(...  2.47 us
    pallas_call x1, Pallas kernels, local(): pl.pallas_call(functools.partial(first_strip_kernel, sizes), out_shape=ti...  2.41 us
  transfers between devices with their start and end apart: 13, of which 12 were waited for; matrix products, arithmetic and copies ran while one was open for 1% of the time, Pallas kernels for 17%

profile of v3, /device:TPU:0, one launch (start us, length us, event | category | flops | bytes accessed | tf_op | source)
XLA Modules:
  0.0 80.3 jit_solution(4114178976367939236)
XLA Ops:
  0.6 1.1 %convert_bitcast_fusion = f32[1,32,4096]{2,1,0:T(8,128)S(1)} fusion(s32[32,4096]{1,0:T(8,128)} %param.10), kind=kLoop, calls=%fused_computation.1 | loop fusion | flops 262144 | bytes 1048576 | tf_op jit(solution)/shard_map/stack | solution.py:411
  1.8 1.1 %pad_maximum_fusion.both = f32[2,32,4096]{2,1,0:T(8,128)S(1)} fusion(f32[1,32,4096]{2,1,0:T(8,128)S(1)} %convert_bitcast_fusion, f32[1,32,4096]{2,1,0:T(8,128)} %bitcast.72), kind=kLoop, calls=%fused_computation | loop fusion | flops 262144 | bytes 2097152 | tf_op jit(solution)/shard_map/stack | solution.py:411
  2.9 0.5 collective-permute-start
  4.0 0.3 collective-permute-done
  4.4 2.9 %collective-permute-start.1 = (f32[7,4224]{1,0:T(8,128)S(1)}, f32[7,4224]{1,0:T(8,128)S(1)}, u32[]{:S(2)}, u32[]{:S(2)}) collective-permute-start(f32[7,4224]{1,0:T(8,128)S(1)} %maximum_maximum_fusion), channel_id=1, source_target_pairs={{0,2},{2,0},{4,6},{6,4},{8,10},{10,8},{12,14},{14,12},{1,3},{3,1},... | collective-permute-start | bytes 354824 | tf_op jit(solution)/shard_map/ppermute | solution.py:427
  7.4 0.7 collective-permute-start.2
  8.1 2.7 %shard_map.120 = (f32[4,32,4224]{2,1,0:T(8,128)S(1)}, f32[4,32,4224]{2,1,0:T(8,128)S(1)}) custom-call(f32[2,32,4096]{2,1,0:T(8,128)S(1)} %pad_maximum_fusion.both, f32[2,32,128]{2,1,0:T(8,128)S(1)} %broadcast_select_fusion.ext, f32[16,128]{1,0:T(8,128)S(1)} %pad.8.tables), custom_call_target="tpu_custom_call" | custom-call | flops 2147483648 | bytes 8388608 | tf_op jit(solution)/shard_map/pallas_call | solution.py:453
  10.8 0.5 collective-permute-done.1.first
  11.3 2.4 %shard_map.121 = (f32[24,4,8,128]{3,2,1,0:T(8,128)S(1)}, f32[24,4,128]{2,1,0:T(4,128)S(1)}, s32[25]{0:T(128)S(1)}, f32[24,4224]{1,0:T(8,128)S(1)}, f32[4,8,4224]{2,1,0:T(8,128)S(1)}) custom-call(s32[1]{0:T(128)} %bitcast.place, s32[2,24]{1,0:T(2,128)S(1)} %bitcast.68, s32[2,24]{1,0:T(2,128)S(1)} %bitcast.70, f32[2,32,4096]{2,1,0:T(8,128)S(1)} %pad_maximum_fusion.both, ...), custom_call_target="tpu_custom_call" | custom-call | tf_op jit(solution)/shard_map/pallas_call | solution.py:465
  13.7 7.2 %shard_map.122 = (f32[4,56,128]{2,1,0:T(8,128)S(1)}, f32[8,256,128]{2,1,0:T(8,128)S(1)}) custom-call(s32[25]{0:T(128)S(1)} %get-tuple-element.31.slots, f32[24,4,8,128]{3,2,1,0:T(8,128)S(1)} %get-tuple-element.32.xin, f32[24,4,128]{2,1,0:T(4,128)S(1)} %get-tuple-element.33.base, f32[56,128]{1,0:T(8,128)S(1)} %fusion.1.params), custom_call_target="tpu_custom_call" | custom-call | flops 17694720000 | bytes 2097152 | tf_op jit(solution)/shard_map/pallas_call | solution.py:492
  20.9 7.0 %collective-permute-start.3 = (f32[4,56,128]{2,1,0:T(8,128)S(1)}, f32[4,56,128]{2,1,0:T(8,128)S(1)}, u32[]{:S(2)}, u32[]{:S(2)}) collective-permute-start(f32[4,56,128]{2,1,0:T(8,128)S(1)} %get-tuple-element.35), channel_id=1, source_target_pairs={{0,8},{2,10},{4,12},{6,14},{8,0},{10,2},{12,4},{14,6},{1,9},{3,11}... | collective-permute-start | bytes 344072 | tf_op jit(solution)/shard_map/ppermute | solution.py:406
  27.9 4.3 %shard_map.123 = f32[4,56,128]{2,1,0:T(8,128)S(1)} custom-call(s32[25]{0:T(128)S(1)} %get-tuple-element.31.slots, f32[24,4,8,128]{3,2,1,0:T(8,128)S(1)} %get-tuple-element.32.xin, f32[24,4,128]{2,1,0:T(4,128)S(1)} %get-tuple-element.33.base, f32[56,128]{1,0:T(8,128)S(1)} %fusion.1.params, f32[8,256,128]{2,1,0:T(8,128)S(1)} %get-tuple-element.34.begun), custom_call_target="tpu_custom_call" | custom-call | flops 11796480000 | bytes 2097152 | tf_op jit(solution)/shard_map/pallas_call | solution.py:492
  32.2 0.5 collective-permute-done.3
  32.7 0.8 %collective-permute-start.4 = (f32[4,56,128]{2,1,0:T(8,128)S(1)}, f32[4,56,128]{2,1,0:T(8,128)S(1)}, u32[]{:S(2)}, u32[]{:S(2)}) collective-permute-start(f32[4,56,128]{2,1,0:T(8,128)S(1)} %add.57), channel_id=1, source_target_pairs={{0,2},{2,0},{4,6},{6,4},{8,10},{10,8},{12,14},{14,12},{1,3},{3,1},... | collective-permute-start | bytes 344072 | tf_op jit(solution)/shard_map/ppermute | solution.py:406
  33.5 2.5 %shard_map.124 = (f32[32,4096]{1,0:T(8,128)}, f32[24,4,8,128]{3,2,1,0:T(8,128)S(1)}, f32[24,4,128]{2,1,0:T(4,128)S(1)}, s32[25]{0:T(128)S(1)}) custom-call(s32[1]{0:T(128)} %bitcast.place, s32[2,24]{1,0:T(2,128)S(1)} %bitcast.69, s32[2,24]{1,0:T(2,128)S(1)} %bitcast.71, f32[2,32,4096]{2,1,0:T(8,128)S(1)} %pad_maximum_fusion.both, f32[16,128]{1,0:T(8,128)S(1)} %pad.8.tables, ...), custom_call_target="tpu_custom_call" | custom-call | flops 2147483648 | bytes 8388608 | tf_op jit(solution)/shard_map/pallas_call | solution.py:476
  36.0 1.5 %collective-permute-done.4 = f32[4,56,128]{2,1,0:T(8,128)S(1)} collective-permute-done((f32[4,56,128]{2,1,0:T(8,128)S(1)}, f32[4,56,128]{2,1,0:T(8,128)S(1)}, u32[]{:S(2)}, u32[]{:S(2)}) %collective-permute-start.4) | collective-permute-done | bytes 114720 | tf_op jit(solution)/shard_map/ppermute | solution.py:406
  37.6 1.2 %collective-permute-start.5 = (f32[4,56,128]{2,1,0:T(8,128)S(1)}, f32[4,56,128]{2,1,0:T(8,128)S(1)}, u32[]{:S(2)}, u32[]{:S(2)}) collective-permute-start(f32[4,56,128]{2,1,0:T(8,128)S(1)} %add.58.own), channel_id=1, source_target_pairs={{0,4},{2,6},{4,0},{6,2},{8,12},{10,14},{12,8},{14,10},{1,5},{3,7},... | collective-permute-start | bytes 344072 | tf_op jit(solution)/shard_map/ppermute | solution.py:406
  38.7 3.7 %collective-permute-done.5.other = f32[4,56,128]{2,1,0:T(8,128)S(1)} collective-permute-done((f32[4,56,128]{2,1,0:T(8,128)S(1)}, f32[4,56,128]{2,1,0:T(8,128)S(1)}, u32[]{:S(2)}, u32[]{:S(2)}) %collective-permute-start.5) | collective-permute-done | bytes 114720 | tf_op jit(solution)/shard_map/ppermute | solution.py:406
  42.4 0.1 shard_map.125
  42.7 4.2 %collective-permute-done.6 = f32[56,128]{1,0:T(8,128)S(1)} collective-permute-done((f32[56,128]{1,0:T(8,128)S(1)}, f32[56,128]{1,0:T(8,128)S(1)}, u32[]{:S(2)}, u32[]{:S(2)}) %collective-permute-start.6) | collective-permute-done | bytes 28704 | tf_op jit(solution)/shard_map/ppermute | solution.py:533
  46.9 1.2 %collective-permute-done.7 = f32[56,128]{1,0:T(8,128)S(1)} collective-permute-done((f32[56,128]{1,0:T(8,128)S(1)}, f32[56,128]{1,0:T(8,128)S(1)}, u32[]{:S(2)}, u32[]{:S(2)}) %collective-permute-start.7) | collective-permute-done | bytes 28704 | tf_op jit(solution)/shard_map/ppermute | solution.py:406
  48.1 7.3 %shard_map.126 = (f32[4,56,128]{2,1,0:T(8,128)S(1)}, f32[8,256,128]{2,1,0:T(8,128)S(1)}) custom-call(s32[25]{0:T(128)S(1)} %get-tuple-element.46.slots, f32[24,4,8,128]{3,2,1,0:T(8,128)S(1)} %get-tuple-element.47.xin, f32[24,4,128]{2,1,0:T(4,128)S(1)} %get-tuple-element.48.base, f32[56,128]{1,0:T(8,128)S(1)} %get-tuple-element.60.params), custom_call_target="tpu_custom_call" | custom-call | flops 17694720000 | bytes 2097152 | tf_op jit(solution)/shard_map/pallas_call | solution.py:492
  55.4 2.1 %collective-permute-start.8 = (f32[4,56,128]{2,1,0:T(8,128)S(1)}, f32[4,56,128]{2,1,0:T(8,128)S(1)}, u32[]{:S(2)}, u32[]{:S(2)}) collective-permute-start(f32[4,56,128]{2,1,0:T(8,128)S(1)} %get-tuple-element.50), channel_id=1, source_target_pairs={{0,8},{2,10},{4,12},{6,14},{8,0},{10,2},{12,4},{14,6},{1,9},{3,11}... | collective-permute-start | bytes 344072 | tf_op jit(solution)/shard_map/ppermute | solution.py:406
  57.5 4.1 %shard_map.127 = f32[4,56,128]{2,1,0:T(8,128)S(1)} custom-call(s32[25]{0:T(128)S(1)} %get-tuple-element.46.slots, f32[24,4,8,128]{3,2,1,0:T(8,128)S(1)} %get-tuple-element.47.xin, f32[24,4,128]{2,1,0:T(4,128)S(1)} %get-tuple-element.48.base, f32[56,128]{1,0:T(8,128)S(1)} %get-tuple-element.60.params, f32[8,256,128]{2,1,0:T(8,128)S(1)} %get-tuple-element.49.begun), custom_call_target="tpu_custom_call" | custom-call | flops 11796480000 | bytes 2097152 | tf_op jit(solution)/shard_map/pallas_call | solution.py:492
  61.6 2.4 %collective-permute-done.8 = f32[4,56,128]{2,1,0:T(8,128)S(1)} collective-permute-done((f32[4,56,128]{2,1,0:T(8,128)S(1)}, f32[4,56,128]{2,1,0:T(8,128)S(1)}, u32[]{:S(2)}, u32[]{:S(2)}) %collective-permute-start.8) | collective-permute-done | bytes 114720 | tf_op jit(solution)/shard_map/ppermute | solution.py:406
  64.0 0.8 %collective-permute-start.9 = (f32[4,56,128]{2,1,0:T(8,128)S(1)}, f32[4,56,128]{2,1,0:T(8,128)S(1)}, u32[]{:S(2)}, u32[]{:S(2)}) collective-permute-start(f32[4,56,128]{2,1,0:T(8,128)S(1)} %add.61), channel_id=1, source_target_pairs={{0,2},{2,0},{4,6},{6,4},{8,10},{10,8},{12,14},{14,12},{1,3},{3,1},... | collective-permute-start | bytes 344072 | tf_op jit(solution)/shard_map/ppermute | solution.py:406
  64.9 4.0 %collective-permute-done.9 = f32[4,56,128]{2,1,0:T(8,128)S(1)} collective-permute-done((f32[4,56,128]{2,1,0:T(8,128)S(1)}, f32[4,56,128]{2,1,0:T(8,128)S(1)}, u32[]{:S(2)}, u32[]{:S(2)}) %collective-permute-start.9) | collective-permute-done | bytes 114720 | tf_op jit(solution)/shard_map/ppermute | solution.py:406
  68.9 0.5 collective-permute-start.10
  69.4 4.4 %collective-permute-done.10.other = f32[4,56,128]{2,1,0:T(8,128)S(1)} collective-permute-done((f32[4,56,128]{2,1,0:T(8,128)S(1)}, f32[4,56,128]{2,1,0:T(8,128)S(1)}, u32[]{:S(2)}, u32[]{:S(2)}) %collective-permute-start.10) | collective-permute-done | bytes 114720 | tf_op jit(solution)/shard_map/ppermute | solution.py:406
  74.0 4.3 %collective-permute-done.11 = f32[56,128]{1,0:T(8,128)S(1)} collective-permute-done((f32[56,128]{1,0:T(8,128)S(1)}, f32[56,128]{1,0:T(8,128)S(1)}, u32[]{:S(2)}, u32[]{:S(2)}) %collective-permute-start.11) | collective-permute-done | bytes 28704 | tf_op jit(solution)/shard_map/ppermute | solution.py:533
  78.4 1.2 %collective-permute-done.12 = f32[56,128]{1,0:T(8,128)S(1)} collective-permute-done((f32[56,128]{1,0:T(8,128)S(1)}, f32[56,128]{1,0:T(8,128)S(1)}, u32[]{:S(2)}, u32[]{:S(2)}) %collective-permute-start.12) | collective-permute-done | bytes 28704 | tf_op jit(solution)/shard_map/ppermute | solution.py:406
  79.6 0.7 shard_map.129
  (50 shorter events, 0.9 us)
Async XLA Ops:
  1.7 1.8 %copy-start.5 = (f32[9,1,64]{2,1,0:T(1,128)S(1)}, f32[9,1,64]{2,1,0:T(1,128)}, u32[]{:S(2)}) copy-start(f32[9,1,64]{2,1,0:T(1,128)} %param.17) | copy-start | bytes 6916
  1.7 1.8 %copy-start.3 = (f32[9,64,4]{1,2,0:T(4,128)S(1)}, f32[9,64,4]{1,2,0:T(4,128)}, u32[]{:S(2)}) copy-start(f32[9,64,4]{1,2,0:T(4,128)} %param.15) | copy-start | bytes 27652
  1.7 1.8 %copy-start.2 = (f32[64,64]{1,0:T(8,128)S(1)}, f32[64,64]{1,0:T(8,128)}, u32[]{:S(2)}) copy-start(f32[64,64]{1,0:T(8,128)} %param.16) | copy-start | bytes 49156
  1.8 1.9 %copy-start.4 = (f32[2,16]{1,0:T(2,128)S(1)}, f32[2,16]{1,0:T(2,128)}, u32[]{:S(2)}) copy-start(f32[2,16]{1,0:T(2,128)} %param.12) | copy-start | bytes 388
  1.8 1.9 %copy-start.6 = (f32[16]{0:T(128)S(1)}, f32[16]{0:T(128)}, u32[]{:S(2)}) copy-start(f32[16]{0:T(128)} %param.11) | copy-start | bytes 196
  2.9 1.4 %collective-permute-start = (f32[2,32,128]{2,1,0:T(8,128)S(1)}, f32[2,32,128]{2,1,0:T(8,128)S(1)}, u32[]{:S(2)}, u32[]{:S(2)}) collective-permute-start(f32[2,32,128]{2,1,0:T(8,128)S(1)} %slice_select_fusion), channel_id=1, source_target_pairs={{0,1},{1,0},{2,3},{3,2},{4,5},{5,4},{6,7},{7,6},{8,9},{9,8},{10,11... | collective-permute-start | bytes 98312 | tf_op jit(solution)/shard_map/ppermute | solution.py:406
  4.4 6.8 %collective-permute-start.1 = (f32[7,4224]{1,0:T(8,128)S(1)}, f32[7,4224]{1,0:T(8,128)S(1)}, u32[]{:S(2)}, u32[]{:S(2)}) collective-permute-start(f32[7,4224]{1,0:T(8,128)S(1)} %maximum_maximum_fusion), channel_id=1, source_target_pairs={{0,2},{2,0},{4,6},{6,4},{8,10},{10,8},{12,14},{14,12},{1,3},{3,1},... | collective-permute-start | bytes 354824 | tf_op jit(solution)/shard_map/ppermute | solution.py:427
  7.4 3.9 %copy-start = (s32[2,1,1,24]{3,2,1,0:T(1,128)S(1)}, s32[2,1,1,24]{3,2,1,0:T(1,128)}, u32[]{:S(2)}) copy-start(s32[2,1,1,24]{3,2,1,0:T(1,128)} %param.13) | copy-start | bytes 580
  7.4 3.9 %copy-start.1 = (s32[2,1,1,24,1]{3,4,2,1,0:T(1,128)S(1)}, s32[2,1,1,24,1]{3,4,2,1,0:T(1,128)}, u32[]{:S(2)}) copy-start(s32[2,1,1,24,1]{3,4,2,1,0:T(1,128)} %param.14) | copy-start | bytes 580
  7.4 3.9 %collective-permute-start.2 = (f32[7,4224]{1,0:T(8,128)S(1)}, f32[7,4224]{1,0:T(8,128)S(1)}, u32[]{:S(2)}, u32[]{:S(2)}) collective-permute-start(f32[7,4224]{1,0:T(8,128)S(1)} %maximum_maximum_fusion.1), channel_id=1, source_target_pairs={{2,4},{6,8},{10,12},{4,2},{8,6},{12,10},{3,5},{7,9},{11,13},{5,3},... | collective-permute-start | bytes 354824 | tf_op jit(solution)/shard_map/ppermute | solution.py:428
  20.9 11.7 %collective-permute-start.3 = (f32[4,56,128]{2,1,0:T(8,128)S(1)}, f32[4,56,128]{2,1,0:T(8,128)S(1)}, u32[]{:S(2)}, u32[]{:S(2)}) collective-permute-start(f32[4,56,128]{2,1,0:T(8,128)S(1)} %get-tuple-element.35), channel_id=1, source_target_pairs={{0,8},{2,10},{4,12},{6,14},{8,0},{10,2},{12,4},{14,6},{1,9},{3,11}... | collective-permute-start | bytes 344072 | tf_op jit(solution)/shard_map/ppermute | solution.py:406
  32.7 4.9 %collective-permute-start.4 = (f32[4,56,128]{2,1,0:T(8,128)S(1)}, f32[4,56,128]{2,1,0:T(8,128)S(1)}, u32[]{:S(2)}, u32[]{:S(2)}) collective-permute-start(f32[4,56,128]{2,1,0:T(8,128)S(1)} %add.57), channel_id=1, source_target_pairs={{0,2},{2,0},{4,6},{6,4},{8,10},{10,8},{12,14},{14,12},{1,3},{3,1},... | collective-permute-start | bytes 344072 | tf_op jit(solution)/shard_map/ppermute | solution.py:406
  37.6 4.9 %collective-permute-start.5 = (f32[4,56,128]{2,1,0:T(8,128)S(1)}, f32[4,56,128]{2,1,0:T(8,128)S(1)}, u32[]{:S(2)}, u32[]{:S(2)}) collective-permute-start(f32[4,56,128]{2,1,0:T(8,128)S(1)} %add.58.own), channel_id=1, source_target_pairs={{0,4},{2,6},{4,0},{6,2},{8,12},{10,14},{12,8},{14,10},{1,5},{3,7},... | collective-permute-start | bytes 344072 | tf_op jit(solution)/shard_map/ppermute | solution.py:406
  42.6 4.3 %collective-permute-start.6 = (f32[56,128]{1,0:T(8,128)S(1)}, f32[56,128]{1,0:T(8,128)S(1)}, u32[]{:S(2)}, u32[]{:S(2)}) collective-permute-start(f32[56,128]{1,0:T(8,128)S(1)} %shard_map.125), channel_id=1, source_target_pairs={{0,9},{1,8},{2,11},{3,10},{4,13},{5,12},{6,15},{7,14},{8,1},{9,0},... | collective-permute-start | bytes 86024 | tf_op jit(solution)/shard_map/ppermute | solution.py:533
  46.9 1.2 %collective-permute-start.7 = (f32[56,128]{1,0:T(8,128)S(1)}, f32[56,128]{1,0:T(8,128)S(1)}, u32[]{:S(2)}, u32[]{:S(2)}) collective-permute-start(f32[56,128]{1,0:T(8,128)S(1)} %add.59), channel_id=1, source_target_pairs={{0,1},{1,0},{2,3},{3,2},{4,5},{5,4},{6,7},{7,6},{8,9},{9,8},{10,11... | collective-permute-start | bytes 86024 | tf_op jit(solution)/shard_map/ppermute | solution.py:406
  55.4 8.6 %collective-permute-start.8 = (f32[4,56,128]{2,1,0:T(8,128)S(1)}, f32[4,56,128]{2,1,0:T(8,128)S(1)}, u32[]{:S(2)}, u32[]{:S(2)}) collective-permute-start(f32[4,56,128]{2,1,0:T(8,128)S(1)} %get-tuple-element.50), channel_id=1, source_target_pairs={{0,8},{2,10},{4,12},{6,14},{8,0},{10,2},{12,4},{14,6},{1,9},{3,11}... | collective-permute-start | bytes 344072 | tf_op jit(solution)/shard_map/ppermute | solution.py:406
  64.0 4.9 %collective-permute-start.9 = (f32[4,56,128]{2,1,0:T(8,128)S(1)}, f32[4,56,128]{2,1,0:T(8,128)S(1)}, u32[]{:S(2)}, u32[]{:S(2)}) collective-permute-start(f32[4,56,128]{2,1,0:T(8,128)S(1)} %add.61), channel_id=1, source_target_pairs={{0,2},{2,0},{4,6},{6,4},{8,10},{10,8},{12,14},{14,12},{1,3},{3,1},... | collective-permute-start | bytes 344072 | tf_op jit(solution)/shard_map/ppermute | solution.py:406
  68.9 4.9 %collective-permute-start.10 = (f32[4,56,128]{2,1,0:T(8,128)S(1)}, f32[4,56,128]{2,1,0:T(8,128)S(1)}, u32[]{:S(2)}, u32[]{:S(2)}) collective-permute-start(f32[4,56,128]{2,1,0:T(8,128)S(1)} %add.62.own), channel_id=1, source_target_pairs={{0,4},{2,6},{4,0},{6,2},{8,12},{10,14},{12,8},{14,10},{1,5},{3,7},... | collective-permute-start | bytes 344072 | tf_op jit(solution)/shard_map/ppermute | solution.py:406
  73.9 4.4 %collective-permute-start.11 = (f32[56,128]{1,0:T(8,128)S(1)}, f32[56,128]{1,0:T(8,128)S(1)}, u32[]{:S(2)}, u32[]{:S(2)}) collective-permute-start(f32[56,128]{1,0:T(8,128)S(1)} %shard_map.128), channel_id=1, source_target_pairs={{0,9},{1,8},{2,11},{3,10},{4,13},{5,12},{6,15},{7,14},{8,1},{9,0},... | collective-permute-start | bytes 86024 | tf_op jit(solution)/shard_map/ppermute | solution.py:533
  78.4 1.2 %collective-permute-start.12 = (f32[56,128]{1,0:T(8,128)S(1)}, f32[56,128]{1,0:T(8,128)S(1)}, u32[]{:S(2)}, u32[]{:S(2)}) collective-permute-start(f32[56,128]{1,0:T(8,128)S(1)} %add.63), channel_id=1, source_target_pairs={{0,1},{1,0},{2,3},{3,2},{4,5},{5,4},{6,7},{7,6},{8,9},{9,8},{10,11... | collective-permute-start | bytes 86024 | tf_op jit(solution)/shard_map/ppermute | solution.py:406

commit v4 on v3

--- a/solution.py
+++ b/solution.py
@@ -14,7 +14,6 @@
 EXT = 128
 LIVE = 64
 BATCH = 8
-FIRST = 2
 
 F32 = jnp.float32
 BF16 = jnp.bfloat16
@@ -62,7 +61,8 @@
         )
 
 
-def inner_kernel(both, ext, tables, fields, coef, ids, start):
+def inner_kernel(sizes, place, tile_pos, tile_dest, both, ext, tables, fields, coef, xin, base, slots, ids, start):
+    order_tiles(0, sizes, True, place, tile_pos, tile_dest, slots)
     rows, lanes = both.shape[1:]
     wide = lanes + EXT
     ids[:, 0:lanes] = both[1].astype(jnp.int32)
@@ -78,26 +78,57 @@
             target[:, cut] = new
 
         advance(lambda cut: source[:, cut], lambda k, cut: coef[k, :, cut], write, rows, wide // 128)
-
-
-def spare_slots(sends):
-    return -sends % BATCH
-
-
-def pick_tiles(snapshot, sizes, place, tile_pos, tile_dest, both, main, strip, tables, xin, base, slots):
+    main = (fields.at[0], fields.at[1])
+    pick_tiles(0, sizes, True, 0, tile_pos, slots, both.at[1], main, None, tables, xin, base)
+
+
+def lead_of(early):
+    return BATCH if early else 0
+
+
+def slot_count(sends, early):
+    return lead_of(early) - (-sends // BATCH) * BATCH
+
+
+def order_tiles(snapshot, sizes, early, place, tile_pos, tile_dest, slots):
     sends, per_row, half, blocks = sizes
+    total, lead = slot_count(sends, early), lead_of(early)
     mine = lax.div(place[0], half)
+    for slot in range(2 * total):
+        slots[slot] = 0
+    buffers, aways, inners = [], [], []
+    for k in range(sends):
+        dest = tile_dest[snapshot, k]
+        away = (lax.div(dest, half) != mine).astype(jnp.int32)
+        block = lax.div(tile_pos[snapshot, k], per_row)
+        aways.append(away)
+        inners.append(((block != 0) & (block != blocks - 1)).astype(jnp.int32) if early else jnp.int32(0))
+        buffers.append(lax.rem(dest, half) + half * (1 - away))
+    early_far = jnp.minimum(lead, sum(x * y for x, y in zip(aways, inners)))
+    early_near = jnp.minimum(lead - early_far, sum((1 - x) * y for x, y in zip(aways, inners)))
+    rest_far = sum(aways) - early_far
+    one, two, three, four = jnp.int32(0), jnp.int32(0), jnp.int32(lead), lead + rest_far
+    for k in range(sends):
+        away, inner = aways[k], inners[k]
+        first = away * inner * (one < early_far).astype(jnp.int32)
+        second = (1 - away) * inner * (two < early_near).astype(jnp.int32)
+        slot = jnp.where(away == 1, jnp.where(first == 1, one, three), jnp.where(second == 1, early_far + two, four))
+        one, two = one + first, two + second
+        three, four = three + away - first, four + 1 - away - second
+        slots[slot] = buffers[k]
+        slots[total + slot] = k
+    slots[2 * total] = early_far + early_near
+    slots[2 * total + 1] = rest_far
+    slots[2 * total + 2] = sends - early_far - early_near
+
+
+def pick_tiles(snapshot, sizes, early, first, tile_pos, slots, numbers, main, strip, tables, xin, base):
+    sends, per_row, half, blocks = sizes
+    total = slot_count(sends, early)
     sub = lax.broadcasted_iota(jnp.int32, (8, 128), 0)
     channel = tables[8:16]
-    aways = [(lax.div(tile_dest[snapshot, k], half) != mine).astype(jnp.int32) for k in range(sends)]
-    slots[sends + spare_slots(sends)] = sum(aways)
-    far, near = jnp.int32(0), sum(aways)
-    for k in range(sends):
-        away = aways[k]
-        slot = jnp.where(away == 1, far, near)
-        far, near = far + away, near + 1 - away
-        slots[slot] = lax.rem(tile_dest[snapshot, k], half) + half * (1 - away)
-        where = tile_pos[snapshot, k]
+    for slot in range(xin.shape[0]):
+        where = tile_pos[snapshot, slots[total + first + slot]]
         block = lax.div(where, per_row)
         lanes = pl.ds(pl.multiple_of(lax.rem(where, per_row) * TW, TW), TW)
         group = pl.ds(pl.multiple_of(lax.div(block, 2) * 8, 8), 8)
@@ -109,10 +140,13 @@
             return jnp.where(lower, pltpu.roll(x, TR, 0), x)
 
         def value(at):
-            return tile(jnp.where(edge, strip[at][beside, lanes], main[at][group, lanes]))
+            inside = main[at][group, lanes]
+            if strip is None:
+                return tile(inside)
+            return tile(jnp.where(edge, strip[at][beside, lanes], inside))
 
         old = value(0)
-        which = tile(both[1, group, lanes]).astype(jnp.int32)
+        which = tile(numbers[group, lanes]).astype(jnp.int32)
         base[slot] = (old - value(1))[0:TR]
         for r in range(TR):
             found = jnp.take_along_axis(channel, jnp.broadcast_to(which[r : r + 1], (8, 128)), axis=1)
@@ -126,7 +160,7 @@
 
 
 def first_strip_kernel(
-    sizes, place, tile_pos, tile_dest, both, ext, first, second, tables, coef, fields, xin, base, slots, strip, outer, ids, work,
+    sizes, place, tile_pos, slots, both, ext, first, second, tables, coef, fields, xin, base, strip, outer, ids, work,
 ):
     rows, lanes = both.shape[1:]
     wide = lanes + EXT
@@ -149,10 +183,9 @@
             target[:, cut] = new
 
         advance(lambda cut: source[:, cut], strip_coef(coef, outer, rows), write, 24, wide // 128)
-    pick_tiles(
-        0, sizes, place, tile_pos, tile_dest, both, (fields.at[0], fields.at[1]), (work.at[1], strip),
-        tables, xin, base, slots,
-    )
+    main = (fields.at[0], fields.at[1])
+    edge = (work.at[1], strip)
+    pick_tiles(0, sizes, True, BATCH, tile_pos, slots, both.at[1], main, edge, tables, xin, base)
 
 
 def second_strip_kernel(
@@ -172,10 +205,10 @@
     final[0:8] = jnp.where(sub < STEPS, work[1, 16:24, 0:lanes], fields[3, 0:8, 0:lanes])
     final[8 : rows - 8] = fields[3, 8 : rows - 8, 0:lanes]
     final[rows - 8 : rows] = jnp.where(sub >= 8 - STEPS, work[1, 0:8, 0:lanes], fields[3, rows - 8 : rows, 0:lanes])
-    pick_tiles(
-        1, sizes, place, tile_pos, tile_dest, both, (fields.at[2], fields.at[3]), (work.at[0], work.at[1]),
-        tables, xin, base, slots,
-    )
+    order_tiles(1, sizes, False, place, tile_pos, tile_dest, slots)
+    main = (fields.at[2], fields.at[3])
+    edge = (work.at[0], work.at[1])
+    pick_tiles(1, sizes, False, 0, tile_pos, slots, both.at[1], main, edge, tables, xin, base)
 
 
 def split(x):
@@ -283,24 +316,31 @@
     return result
 
 
-def add_batches(first, last, sends, slots, xin, base, params, total):
+WEIGHTS = ((64, 144), (64, 192), (16, 192), (64, 48), (64, 192))
+
+
+def prepare(params, weights):
     mix = jnp.concatenate([params[0:32, 0:64], params[0:32, 64:128]], axis=0)
     side, rest = params[32:56, 0:64], params[32:56, 64:128]
     none = jnp.zeros((8, 64), F32)
     taps = [[side[8 * r : 8 * r + 8], rest[4 * r : 4 * r + 4], none[0:4]] for r in range(3)]
     w1 = jnp.concatenate(sum(taps, []), axis=0)
     w3 = jnp.concatenate([rest[12:21], none[0:7]], axis=0)
-    weights = (weights3(w1.T), weights3(mix), weights3(w3), weights3(w3.T), weights3(mix.T))
+    for ref, w in zip(weights, (w1.T, mix, w3, w3.T, mix.T)):
+        ref[...] = weights3(w)
+
+
+def add_batches(first, last, lead, number, masked, slots, xin, base, weights, total):
+    weights = [ref[...] for ref in weights]
 
     def body(i, carry):
         at = [i * BATCH + k for k in range(BATCH)]
         cells = [[xin[j, r] for r in range(TR)] for j in at]
         gaps = [[base[j, r : r + 1, :] for r in range(TR)] for j in at]
-        into = [slots[j] for j in at]
-        if sends % BATCH:
-            cells = [[jnp.where(j < sends, x, 0.0) for x in tile] for j, tile in zip(at, cells)]
-            gaps = [[jnp.where(j < sends, x, 0.0) for x in tile] for j, tile in zip(at, gaps)]
-            into = [jnp.where(j < sends, slot, 0) for j, slot in zip(at, into)]
+        into = [slots[lead + j] for j in at]
+        if masked:
+            cells = [[jnp.where(j < number, x, 0.0) for x in tile] for j, tile in zip(at, cells)]
+            gaps = [[jnp.where(j < number, x, 0.0) for x in tile] for j, tile in zip(at, gaps)]
         for buffer, grad in zip(into, batch_gradients(cells, gaps, weights)):
             total[buffer] += grad
         return carry
@@ -326,25 +366,54 @@
     )
 
 
-def batches_in_first(far, sends):
-    return jnp.maximum(lax.div(far + (BATCH - 1), BATCH), FIRST * -(-sends // BATCH) // 3)
-
-
-def first_gradient_kernel(sends, slots, xin, base, params, far, total):
-    half = far.shape[0]
+def batches(sends, early, slots):
+    at = 2 * slot_count(sends, early)
+    rest_far, rest = slots[at + 1], slots[at + 2]
+    every = lax.div(rest + (BATCH - 1), BATCH)
+    return jnp.maximum(lax.div(rest_far + (BATCH - 1), BATCH), every - 1), every, rest
+
+
+def first_gradients(sends, early, slots, xin, base, weights, far, total):
+    count, every, number = batches(sends, early, slots)
+    masked = early or sends % BATCH != 0
+    add_batches(0, count, lead_of(early), number, masked, slots, xin, base, weights, total)
+    for b in range(far.shape[0]):
+        far[b] = fold(total.at[b])
+
+
+def first_gradient_kernel(sends, slots, xin, base, params, far, total, *weights):
+    prepare(params, weights)
     total[...] = jnp.zeros_like(total)
-    add_batches(0, batches_in_first(slots[sends + spare_slots(sends)], sends), sends, slots, xin, base, params, total)
-    for b in range(half):
-        far[b] = fold(total.at[b])
-
-
-def second_gradient_kernel(sends, slots, xin, base, params, begun, near, total):
+    first_gradients(sends, False, slots, xin, base, weights, far, total)
+
+
+def second_gradient_kernel(sends, early, slots, xin, base, begun, *rest):
+    *weights, near, total = rest
     half = near.shape[0]
     total[half : 2 * half] = begun[half : 2 * half]
-    last = -(-sends // BATCH)
-    add_batches(batches_in_first(slots[sends + spare_slots(sends)], sends), last, sends, slots, xin, base, params, total)
+    count, every, number = batches(sends, early, slots)
+    masked = early or sends % BATCH != 0
+    add_batches(count, every, lead_of(early), number, masked, slots, xin, base, weights, total)
     for b in range(half):
         near[b] = fold(total.at[half + b])
+
+
+def opening_kernel(sizes, place, tile_pos, tile_dest, both, ext, tables, params, fields, coef, slots, begun, *rest):
+    *weights, xin, base, ids, start = rest
+    prepare(params, weights)
+    inner_kernel(sizes, place, tile_pos, tile_dest, both, ext, tables, fields, coef, xin, base, slots, ids, start)
+    begun[...] = jnp.zeros_like(begun)
+    number = slots[2 * slot_count(sizes[0], True)]
+    add_batches(0, jnp.minimum(number, 1), 0, number, True, slots, xin, base, weights, begun)
+
+
+def edge_kernel(sizes, place, tile_pos, slots, both, ext, first, second, tables, coef, fields, begun, *rest):
+    *weights, xin, base, strip, outer, far, total, ids, work = rest
+    first_strip_kernel(
+        sizes, place, tile_pos, slots, both, ext, first, second, tables, coef, fields, xin, base, strip, outer, ids, work
+    )
+    total[...] = begun[...]
+    first_gradients(sizes[0], True, slots, xin, base, weights, far, total)
 
 
 def combine_kernel(entries, own, other, out):
@@ -423,9 +492,10 @@
 
     odd = j % 2 == 1
     inner = [(i, i ^ 1) for i in range(solvers)]
-    outer_pairs = [(i, i + 1) for i in range(1, solvers - 1, 2)] + [(i + 1, i) for i in range(1, solvers - 1, 2)]
+    outer_pairs = [(i, (i + 1 if i % 2 else i - 1) % solvers) for i in range(solvers)]
     first = lax.ppermute(edge_rows(~odd), "solver", inner)
     second = lax.ppermute(edge_rows(odd), "solver", outer_pairs)
+    second = jnp.where((j == 0) | (j == solvers - 1), 0.0, second)
 
     vr, vc = drift_table[0], drift_table[1]
     tables = jnp.stack(
@@ -443,74 +513,87 @@
 
     sizes = (sends, lanes // TW, half, rows // TR)
     wide = lanes + EXT
-    spare = spare_slots(sends)
-    tile_shapes = (
-        jax.ShapeDtypeStruct((sends + spare, TR, 8, TW), F32),
-        jax.ShapeDtypeStruct((sends + spare, TR, TW), F32),
-        jax.ShapeDtypeStruct((sends + spare + 1,), jnp.int32),
-    )
-    tile_specs = (VMEM, VMEM, SMEM)
-    fields, coef = pl.pallas_call(
-        inner_kernel,
+    def tile_shapes(number):
+        return (
+            jax.ShapeDtypeStruct((number, TR, 8, TW), F32),
+            jax.ShapeDtypeStruct((number, TR, TW), F32),
+        )
+
+    def slots_shape(early):
+        return jax.ShapeDtypeStruct((2 * slot_count(sends, early) + 3,), jnp.int32)
+
+    held = slot_count(sends, False)
+    params = pack_weights(conv_in, mix_weight, conv_out)
+    changes = []
+    work = 3 * 2 * 20000 * TR * TW * sends // 2
+    folded = jax.ShapeDtypeStruct((half,) + params.shape, F32)
+    totals = jax.ShapeDtypeStruct((2 * half, 256, 128), F32)
+
+    prepared = tuple(jax.ShapeDtypeStruct(shape, BF16) for shape in WEIGHTS)
+
+    def room(shape):
+        return pltpu.VMEM(shape.shape, shape.dtype)
+
+    fields, coef, slots, begun, *weights = pl.pallas_call(
+        functools.partial(opening_kernel, sizes),
         out_shape=(
             jax.ShapeDtypeStruct((STEPS, rows, wide), F32),
             jax.ShapeDtypeStruct((4, rows, wide), F32),
-        ),
-        in_specs=[VMEM] * 3,
-        out_specs=(VMEM,) * 2,
-        scratch_shapes=[pltpu.VMEM((rows, wide), jnp.int32), pltpu.VMEM((rows, wide), F32)],
+            slots_shape(True),
+            totals,
+        )
+        + prepared,
+        in_specs=[SMEM] * 3 + [VMEM] * 4,
+        out_specs=(VMEM, VMEM, SMEM, VMEM) + (VMEM,) * len(prepared),
+        scratch_shapes=[room(x) for x in tile_shapes(BATCH)]
+        + [pltpu.VMEM((rows, wide), jnp.int32), pltpu.VMEM((rows, wide), F32)],
         compiler_params=PARAMS,
         cost_estimate=pl.CostEstimate(flops=1 << 31, bytes_accessed=1 << 23, transcendentals=0),
-    )(both, ext, tables)
-    *tiles_0, strip, outer = pl.pallas_call(
-        functools.partial(first_strip_kernel, sizes),
-        out_shape=tile_shapes
-        + (jax.ShapeDtypeStruct((24, wide), F32), jax.ShapeDtypeStruct((4, 8, wide), F32)),
-        in_specs=[SMEM] * 3 + [VMEM] * 7,
-        out_specs=tile_specs + (VMEM, VMEM),
+    )(place, tile_pos, tile_dest, both, ext, tables, params)
+
+    def gradients(kernel, tiles, others, out_shape, scratch):
+        xin, base, slots = tiles
+        return pl.pallas_call(
+            kernel,
+            out_shape=out_shape,
+            in_specs=[SMEM] + [VMEM] * (2 + len(others)),
+            out_specs=jax.tree.map(lambda _: VMEM, out_shape),
+            scratch_shapes=scratch,
+            compiler_params=PARAMS,
+            cost_estimate=pl.CostEstimate(flops=work * 16, bytes_accessed=1 << 21, transcendentals=1 << 20),
+        )(slots, xin, base, *others)
+
+    xin, base, strip, outer, far, begun = pl.pallas_call(
+        functools.partial(edge_kernel, sizes),
+        out_shape=tile_shapes(held)
+        + (jax.ShapeDtypeStruct((24, wide), F32), jax.ShapeDtypeStruct((4, 8, wide), F32), folded, totals),
+        in_specs=[SMEM] * 3 + [VMEM] * (8 + len(weights)),
+        out_specs=(VMEM,) * 6,
         scratch_shapes=[pltpu.VMEM((8, wide), jnp.int32), pltpu.VMEM((2, 24, wide), F32)],
         compiler_params=PARAMS,
-    )(place, tile_pos, tile_dest, both, ext, first, second, tables, coef, fields)
+    )(place, tile_pos, slots, both, ext, first, second, tables, coef, fields, begun, *weights)
 
     def second_part(fields, strip):
         return pl.pallas_call(
             functools.partial(second_strip_kernel, sizes),
-            out_shape=(jax.ShapeDtypeStruct((rows, lanes), F32),) + tile_shapes,
+            out_shape=(jax.ShapeDtypeStruct((rows, lanes), F32),) + tile_shapes(held) + (slots_shape(False),),
             in_specs=[SMEM] * 3 + [VMEM] * 6,
-            out_specs=(VMEM,) + tile_specs,
+            out_specs=(VMEM,) * 3 + (SMEM,),
             scratch_shapes=[pltpu.VMEM((2, 24, wide), F32)],
             compiler_params=PARAMS,
             cost_estimate=pl.CostEstimate(flops=1 << 31, bytes_accessed=1 << 23, transcendentals=0),
         )(place, tile_pos, tile_dest, both, tables, coef, fields, strip, outer)
 
-    params = pack_weights(conv_in, mix_weight, conv_out)
-    changes = []
-    work = 3 * 2 * 20000 * TR * TW * sends // 2
-
-    def gradients(kernel, tiles, params, begun, out_shape, scratch, share):
-        xin, base, slots = tiles
-        return pl.pallas_call(
-            functools.partial(kernel, sends),
-            out_shape=out_shape,
-            in_specs=[SMEM] + [VMEM] * (3 + len(begun)),
-            out_specs=jax.tree.map(lambda _: VMEM, out_shape),
-            scratch_shapes=scratch,
-            compiler_params=PARAMS,
-            cost_estimate=pl.CostEstimate(
-                flops=int(work * 32 * share), bytes_accessed=1 << 21, transcendentals=1 << 20
-            ),
-        )(slots, xin, base, params, *begun)
-
-    folded = jax.ShapeDtypeStruct((half,) + params.shape, F32)
-    totals = (2 * half, 256, 128)
-    tiles = tiles_0
+    tiles = (xin, base, slots)
     for snapshot in range(SNAPS):
-        far, begun = gradients(
-            first_gradient_kernel, tiles, params, [], (folded, jax.ShapeDtypeStruct(totals, F32)), [], 0.75
-        )
+        early = snapshot == 0
+        if not early:
+            far, begun, *weights = gradients(
+                functools.partial(first_gradient_kernel, sends), tiles, [params], (folded, totals) + prepared, []
+            )
         arrived = swap(far, "solver", half)
         near = gradients(
-            second_gradient_kernel, tiles, params, [begun], folded, [pltpu.VMEM(totals, F32)], 0.5
+            functools.partial(second_gradient_kernel, sends, early), tiles, [begun, *weights], folded, [room(totals)]
         )
         near = near + arrived
         if snapshot == 0:

time: 80.5 us -> 77.7 us (0.965)
  starting transfers between devices: 16.6 us -> 11.9 us
  waiting for transfers between devices: 28.4 us -> 30.3 us
    ppermute x9, starting transfers between devices: 12.9 us -> 5.18 us  [swap(): return lax.ppermute(x, axis, [(i, i ^ bit) for i in range(count)])]
    ppermute x1, starting transfers between devices: 0.67 us -> 3.61 us  [local(): second = lax.ppermute(edge_rows(odd), 'solver', outer_pairs)]
    ppermute x9, waiting for transfers between devices: 19.3 us -> 21.8 us  [swap(): return lax.ppermute(x, axis, [(i, i ^ bit) for i in range(count)])]
    pallas_call x6 -> x5, Pallas kernels: 28 us -> 28 us  [the longest x3 15.3 us: gradients(): pl.pallas_call(kernel, out_shape=out_shape, in_specs=[SMEM] + [VMEM] * (2...]
  transfers between devices with their start and end apart: 13 -> 13, of which waited for: 12 -> 11; matrix products, arithmetic and copies ran while one was open for 1% -> 1% of each run, Pallas kernels for 17% -> 23%
where the time goes in v4:
time: 77.7 us; the launch traced here: 77.5 us
  Pallas kernels  31.4 us (40%)
  waiting for transfers between devices  30.3 us (39%)
  starting transfers between devices  11.9 us (15%)
  other arithmetic  2.58 us (3%)
  between operations  1.03 us (1%)
    ppermute x9, waiting for transfers between devices, swap(): return lax.ppermute(x, axis, [(i, i ^ bit) for i in range(count)])  21.8 us
    pallas_call x3, Pallas kernels, gradients(): pl.pallas_call(kernel, out_shape=out_shape, in_specs=[SMEM] + [VMEM] * (2...  15.3 us
    ppermute x2, waiting for transfers between devices, local(): lax.ppermute(direction, ('solver', 'trainer'), across)  8.52 us
    pallas_call x1, Pallas kernels, local(): pl.pallas_call(functools.partial(opening_kernel, sizes), out_shape=(jax.S...  7.55 us
    ppermute x9, starting transfers between devices, swap(): return lax.ppermute(x, axis, [(i, i ^ bit) for i in range(count)])  5.18 us
    pallas_call x1, Pallas kernels, local(): pl.pallas_call(functools.partial(edge_kernel, sizes), out_shape=tile_shap...  5.12 us
    ppermute x1, starting transfers between devices, local(): second = lax.ppermute(edge_rows(odd), 'solver', outer_pairs)  3.61 us
    ppermute x1, starting transfers between devices, local(): first = lax.ppermute(edge_rows(~odd), 'solver', inner)  2.93 us
  transfers between devices with their start and end apart: 13, of which 11 were waited for; matrix products, arithmetic and copies ran while one was open for 1% of the time, Pallas kernels for 23%

profile of v4, /device:TPU:0, one launch (start us, length us, event | category | flops | bytes accessed | tf_op | source)
XLA Modules:
  0.0 77.5 jit_solution(12255757355564242666)
XLA Ops:
  0.6 1.1 %convert_bitcast_fusion = f32[1,32,4096]{2,1,0:T(8,128)S(1)} fusion(s32[32,4096]{1,0:T(8,128)} %param.10), kind=kLoop, calls=%fused_computation.1 | loop fusion | flops 262144 | bytes 1048576 | tf_op jit(solution)/shard_map/stack | solution.py:480
  1.8 1.1 %pad_maximum_fusion.both = f32[2,32,4096]{2,1,0:T(8,128)S(1)} fusion(f32[1,32,4096]{2,1,0:T(8,128)S(1)} %convert_bitcast_fusion, f32[1,32,4096]{2,1,0:T(8,128)} %bitcast.73), kind=kLoop, calls=%fused_computation | loop fusion | flops 262144 | bytes 2097152 | tf_op jit(solution)/shard_map/stack | solution.py:480
  3.0 0.5 collective-permute-start
  3.8 0.1 fusion.1.params
  3.9 0.1 pad.8.tables
  4.0 0.3 collective-permute-done
  4.4 2.9 %collective-permute-start.1 = (f32[7,4224]{1,0:T(8,128)S(1)}, f32[7,4224]{1,0:T(8,128)S(1)}, u32[]{:S(2)}, u32[]{:S(2)}) collective-permute-start(f32[7,4224]{1,0:T(8,128)S(1)} %maximum_maximum_fusion), channel_id=1, source_target_pairs={{0,2},{2,0},{4,6},{6,4},{8,10},{10,8},{12,14},{14,12},{1,3},{3,1},... | collective-permute-start | bytes 354824 | tf_op jit(solution)/shard_map/ppermute | solution.py:496
  7.4 3.6 %collective-permute-start.2 = (f32[7,4224]{1,0:T(8,128)S(1)}, f32[7,4224]{1,0:T(8,128)S(1)}, u32[]{:S(2)}, u32[]{:S(2)}) collective-permute-start(f32[7,4224]{1,0:T(8,128)S(1)} %maximum_maximum_fusion.1), channel_id=1, source_target_pairs={{0,14},{2,4},{4,2},{6,8},{8,6},{10,12},{12,10},{14,0},{1,15},{3,5}... | collective-permute-start | bytes 354824 | tf_op jit(solution)/shard_map/ppermute | solution.py:497
  11.0 7.5 %shard_map.120 = (f32[4,32,4224]{2,1,0:T(8,128)S(1)}, f32[4,32,4224]{2,1,0:T(8,128)S(1)}, s32[67]{0:T(128)S(1)}, f32[8,256,128]{2,1,0:T(8,128)S(1)}, bf16[64,144...) custom-call(s32[1]{0:T(128)} %bitcast.place, ...), custom_call_target="tpu_custom_call" | custom-call | flops 2147483648 | bytes 8388608 | tf_op jit(solution)/shard_map/pallas_call | solution.py:537
  18.6 5.1 %shard_map.121 = (f32[24,4,8,128]{3,2,1,0:T(8,128)S(1)}, f32[24,4,128]{2,1,0:T(4,128)S(1)}, f32[24,4224]{1,0:T(8,128)S(1)}, f32[4,8,4224]{2,1,0:T(8,128)S(1)}, f...) custom-call(s32[1]{0:T(128)} %bitcast.place, s32[2,24]{1,0:T(2,128)S(1)} %bitcast.69, ...), custom_call_target="tpu_custom_call" | custom-call | tf_op jit(solution)/shard_map/pallas_call | solution.py:566
  23.7 0.1 collective-permute-start.3
  23.8 4.1 %shard_map.122 = f32[4,56,128]{2,1,0:T(8,128)S(1)} custom-call(s32[67]{0:T(128)S(1)} %get-tuple-element.41.slots, f32[24,4,8,128]{3,2,1,0:T(8,128)S(1)} %get-tuple-element.49.xin, f32[24,4,128]{2,1,0:T(4,128)S(1)} %get-tuple-element.50.base, f32[8,256,128]{2,1,0:T(8,128)S(1)} %get-tuple-element.51.begun, bf16[64,144]{1,0:T(8,128)(2,1)S(1)} %get-tuple-element.44.rest_0_, ...), custom_call_target="tpu_custom_call" | custom-call | flops 11796480000 | bytes 2097152 | tf_op jit(solution)/shard_map/pallas_call | solution.py:556
  28.0 1.6 %collective-permute-done.3 = f32[4,56,128]{2,1,0:T(8,128)S(1)} collective-permute-done((f32[4,56,128]{2,1,0:T(8,128)S(1)}, f32[4,56,128]{2,1,0:T(8,128)S(1)}, u32[]{:S(2)}, u32[]{:S(2)}) %collective-permute-start.3) | collective-permute-done | bytes 114720 | tf_op jit(solution)/shard_map/ppermute | solution.py:475
  29.6 1.7 %collective-permute-start.4 = (f32[4,56,128]{2,1,0:T(8,128)S(1)}, f32[4,56,128]{2,1,0:T(8,128)S(1)}, u32[]{:S(2)}, u32[]{:S(2)}) collective-permute-start(f32[4,56,128]{2,1,0:T(8,128)S(1)} %add.57), channel_id=1, source_target_pairs={{0,2},{2,0},{4,6},{6,4},{8,10},{10,8},{12,14},{14,12},{1,3},{3,1},... | collective-permute-start | bytes 344072 | tf_op jit(solution)/shard_map/ppermute | solution.py:475
  31.4 2.4 %shard_map.123 = (f32[32,4096]{1,0:T(8,128)}, f32[24,4,8,128]{3,2,1,0:T(8,128)S(1)}, f32[24,4,128]{2,1,0:T(4,128)S(1)}, s32[51]{0:T(128)S(1)}) custom-call(s32[1]{0:T(128)} %bitcast.place, s32[2,24]{1,0:T(2,128)S(1)} %bitcast.70, s32[2,24]{1,0:T(2,128)S(1)} %bitcast.72, f32[2,32,4096]{2,1,0:T(8,128)S(1)} %pad_maximum_fusion.both, f32[16,128]{1,0:T(8,128)S(1)} %pad.8.tables, ...), custom_call_target="tpu_custom_call" | custom-call | flops 2147483648 | bytes 8388608 | tf_op jit(solution)/shard_map/pallas_call | solution.py:577
  33.8 0.7 collective-permute-done.4
  34.6 4.8 %collective-permute-done.5.other = f32[4,56,128]{2,1,0:T(8,128)S(1)} collective-permute-done((f32[4,56,128]{2,1,0:T(8,128)S(1)}, f32[4,56,128]{2,1,0:T(8,128)S(1)}, u32[]{:S(2)}, u32[]{:S(2)}) %collective-permute-start.5) | collective-permute-done | bytes 114720 | tf_op jit(solution)/shard_map/ppermute | solution.py:475
  39.4 0.1 shard_map.124
  39.6 4.2 %collective-permute-done.6 = f32[56,128]{1,0:T(8,128)S(1)} collective-permute-done((f32[56,128]{1,0:T(8,128)S(1)}, f32[56,128]{1,0:T(8,128)S(1)}, u32[]{:S(2)}, u32[]{:S(2)}) %collective-permute-start.6) | collective-permute-done | bytes 28704 | tf_op jit(solution)/shard_map/ppermute | solution.py:616
  43.8 1.2 %collective-permute-done.7 = f32[56,128]{1,0:T(8,128)S(1)} collective-permute-done((f32[56,128]{1,0:T(8,128)S(1)}, f32[56,128]{1,0:T(8,128)S(1)}, u32[]{:S(2)}, u32[]{:S(2)}) %collective-permute-start.7) | collective-permute-done | bytes 28704 | tf_op jit(solution)/shard_map/ppermute | solution.py:475
  45.0 0.1 multiply_subtract_fusion
  45.1 7.3 %shard_map.125 = (f32[4,56,128]{2,1,0:T(8,128)S(1)}, f32[8,256,128]{2,1,0:T(8,128)S(1)}, bf16[64,144]{1,0:T(8,128)(2,1)S(1)}, bf16[64,192]{1,0:T(8,128)(2,1)S(1)...) custom-call(s32[51]{0:T(128)S(1)} %get-tuple-element.63.slots, ...), custom_call_target="tpu_custom_call" | custom-call | flops 11796480000 | bytes 2097152 | tf_op jit(solution)/shard_map/pallas_call | solution.py:556
  52.4 1.3 %collective-permute-start.8 = (f32[4,56,128]{2,1,0:T(8,128)S(1)}, f32[4,56,128]{2,1,0:T(8,128)S(1)}, u32[]{:S(2)}, u32[]{:S(2)}) collective-permute-start(f32[4,56,128]{2,1,0:T(8,128)S(1)} %get-tuple-element.72), channel_id=1, source_target_pairs={{0,8},{2,10},{4,12},{6,14},{8,0},{10,2},{12,4},{14,6},{1,9},{3,11}... | collective-permute-start | bytes 344072 | tf_op jit(solution)/shard_map/ppermute | solution.py:475
  53.7 3.9 %shard_map.126 = f32[4,56,128]{2,1,0:T(8,128)S(1)} custom-call(s32[51]{0:T(128)S(1)} %get-tuple-element.63.slots, f32[24,4,8,128]{3,2,1,0:T(8,128)S(1)} %get-tuple-element.64.xin, f32[24,4,128]{2,1,0:T(4,128)S(1)} %get-tuple-element.65.base, f32[8,256,128]{2,1,0:T(8,128)S(1)} %get-tuple-element.66.begun, bf16[64,144]{1,0:T(8,128)(2,1)S(1)} %get-tuple-element.67.rest_0_, ...), custom_call_target="tpu_custom_call" | custom-call | flops 11796480000 | bytes 2097152 | tf_op jit(solution)/shard_map/pallas_call | solution.py:556
  57.6 3.4 %collective-permute-done.8 = f32[4,56,128]{2,1,0:T(8,128)S(1)} collective-permute-done((f32[4,56,128]{2,1,0:T(8,128)S(1)}, f32[4,56,128]{2,1,0:T(8,128)S(1)}, u32[]{:S(2)}, u32[]{:S(2)}) %collective-permute-start.8) | collective-permute-done | bytes 114720 | tf_op jit(solution)/shard_map/ppermute | solution.py:475
  61.0 1.4 %collective-permute-start.9 = (f32[4,56,128]{2,1,0:T(8,128)S(1)}, f32[4,56,128]{2,1,0:T(8,128)S(1)}, u32[]{:S(2)}, u32[]{:S(2)}) collective-permute-start(f32[4,56,128]{2,1,0:T(8,128)S(1)} %add.61), channel_id=1, source_target_pairs={{0,2},{2,0},{4,6},{6,4},{8,10},{10,8},{12,14},{14,12},{1,3},{3,1},... | collective-permute-start | bytes 344072 | tf_op jit(solution)/shard_map/ppermute | solution.py:475
  62.4 3.8 %collective-permute-done.9 = f32[4,56,128]{2,1,0:T(8,128)S(1)} collective-permute-done((f32[4,56,128]{2,1,0:T(8,128)S(1)}, f32[4,56,128]{2,1,0:T(8,128)S(1)}, u32[]{:S(2)}, u32[]{:S(2)}) %collective-permute-start.9) | collective-permute-done | bytes 114720 | tf_op jit(solution)/shard_map/ppermute | solution.py:475
  66.3 4.8 %collective-permute-done.10.other = f32[4,56,128]{2,1,0:T(8,128)S(1)} collective-permute-done((f32[4,56,128]{2,1,0:T(8,128)S(1)}, f32[4,56,128]{2,1,0:T(8,128)S(1)}, u32[]{:S(2)}, u32[]{:S(2)}) %collective-permute-start.10) | collective-permute-done | bytes 114720 | tf_op jit(solution)/shard_map/ppermute | solution.py:475
  71.1 0.1 shard_map.127
  71.3 4.3 %collective-permute-done.11 = f32[56,128]{1,0:T(8,128)S(1)} collective-permute-done((f32[56,128]{1,0:T(8,128)S(1)}, f32[56,128]{1,0:T(8,128)S(1)}, u32[]{:S(2)}, u32[]{:S(2)}) %collective-permute-start.11) | collective-permute-done | bytes 28704 | tf_op jit(solution)/shard_map/ppermute | solution.py:616
  75.6 1.2 %collective-permute-done.12 = f32[56,128]{1,0:T(8,128)S(1)} collective-permute-done((f32[56,128]{1,0:T(8,128)S(1)}, f32[56,128]{1,0:T(8,128)S(1)}, u32[]{:S(2)}, u32[]{:S(2)}) %collective-permute-start.12) | collective-permute-done | bytes 28704 | tf_op jit(solution)/shard_map/ppermute | solution.py:475
  76.8 0.7 shard_map.128
  (50 shorter events, 0.8 us)
Async XLA Ops:
  1.7 1.8 %copy-start.5 = (f32[9,1,64]{2,1,0:T(1,128)S(1)}, f32[9,1,64]{2,1,0:T(1,128)}, u32[]{:S(2)}) copy-start(f32[9,1,64]{2,1,0:T(1,128)} %param.17) | copy-start | bytes 6916
  1.7 1.9 %copy-start.3 = (f32[9,64,4]{1,2,0:T(4,128)S(1)}, f32[9,64,4]{1,2,0:T(4,128)}, u32[]{:S(2)}) copy-start(f32[9,64,4]{1,2,0:T(4,128)} %param.15) | copy-start | bytes 27652
  1.7 1.9 %copy-start.2 = (f32[64,64]{1,0:T(8,128)S(1)}, f32[64,64]{1,0:T(8,128)}, u32[]{:S(2)}) copy-start(f32[64,64]{1,0:T(8,128)} %param.16) | copy-start | bytes 49156
  1.8 1.9 %copy-start.4 = (f32[2,16]{1,0:T(2,128)S(1)}, f32[2,16]{1,0:T(2,128)}, u32[]{:S(2)}) copy-start(f32[2,16]{1,0:T(2,128)} %param.12) | copy-start | bytes 388
  1.8 1.9 %copy-start.6 = (f32[16]{0:T(128)S(1)}, f32[16]{0:T(128)}, u32[]{:S(2)}) copy-start(f32[16]{0:T(128)} %param.11) | copy-start | bytes 196
  2.9 8.1 %copy-start = (s32[2,1,1,24]{3,2,1,0:T(1,128)S(1)}, s32[2,1,1,24]{3,2,1,0:T(1,128)}, u32[]{:S(2)}) copy-start(s32[2,1,1,24]{3,2,1,0:T(1,128)} %param.13) | copy-start | bytes 580
  2.9 8.1 %copy-start.1 = (s32[2,1,1,24,1]{3,4,2,1,0:T(1,128)S(1)}, s32[2,1,1,24,1]{3,4,2,1,0:T(1,128)}, u32[]{:S(2)}) copy-start(s32[2,1,1,24,1]{3,4,2,1,0:T(1,128)} %param.14) | copy-start | bytes 580
  3.0 1.4 %collective-permute-start = (f32[2,32,128]{2,1,0:T(8,128)S(1)}, f32[2,32,128]{2,1,0:T(8,128)S(1)}, u32[]{:S(2)}, u32[]{:S(2)}) collective-permute-start(f32[2,32,128]{2,1,0:T(8,128)S(1)} %slice_select_fusion), channel_id=1, source_target_pairs={{0,1},{1,0},{2,3},{3,2},{4,5},{5,4},{6,7},{7,6},{8,9},{9,8},{10,11... | collective-permute-start | bytes 98312 | tf_op jit(solution)/shard_map/ppermute | solution.py:475
  4.4 14.2 %collective-permute-start.1 = (f32[7,4224]{1,0:T(8,128)S(1)}, f32[7,4224]{1,0:T(8,128)S(1)}, u32[]{:S(2)}, u32[]{:S(2)}) collective-permute-start(f32[7,4224]{1,0:T(8,128)S(1)} %maximum_maximum_fusion), channel_id=1, source_target_pairs={{0,2},{2,0},{4,6},{6,4},{8,10},{10,8},{12,14},{14,12},{1,3},{3,1},... | collective-permute-start | bytes 354824 | tf_op jit(solution)/shard_map/ppermute | solution.py:496
  7.4 11.2 %collective-permute-start.2 = (f32[7,4224]{1,0:T(8,128)S(1)}, f32[7,4224]{1,0:T(8,128)S(1)}, u32[]{:S(2)}, u32[]{:S(2)}) collective-permute-start(f32[7,4224]{1,0:T(8,128)S(1)} %maximum_maximum_fusion.1), channel_id=1, source_target_pairs={{0,14},{2,4},{4,2},{6,8},{8,6},{10,12},{12,10},{14,0},{1,15},{3,5}... | collective-permute-start | bytes 354824 | tf_op jit(solution)/shard_map/ppermute | solution.py:497
  23.7 5.9 %collective-permute-start.3 = (f32[4,56,128]{2,1,0:T(8,128)S(1)}, f32[4,56,128]{2,1,0:T(8,128)S(1)}, u32[]{:S(2)}, u32[]{:S(2)}) collective-permute-start(f32[4,56,128]{2,1,0:T(8,128)S(1)} %get-tuple-element.52), channel_id=1, source_target_pairs={{0,8},{2,10},{4,12},{6,14},{8,0},{10,2},{12,4},{14,6},{1,9},{3,11}... | collective-permute-start | bytes 344072 | tf_op jit(solution)/shard_map/ppermute | solution.py:475
  29.6 4.9 %collective-permute-start.4 = (f32[4,56,128]{2,1,0:T(8,128)S(1)}, f32[4,56,128]{2,1,0:T(8,128)S(1)}, u32[]{:S(2)}, u32[]{:S(2)}) collective-permute-start(f32[4,56,128]{2,1,0:T(8,128)S(1)} %add.57), channel_id=1, source_target_pairs={{0,2},{2,0},{4,6},{6,4},{8,10},{10,8},{12,14},{14,12},{1,3},{3,1},... | collective-permute-start | bytes 344072 | tf_op jit(solution)/shard_map/ppermute | solution.py:475
  34.5 4.9 %collective-permute-start.5 = (f32[4,56,128]{2,1,0:T(8,128)S(1)}, f32[4,56,128]{2,1,0:T(8,128)S(1)}, u32[]{:S(2)}, u32[]{:S(2)}) collective-permute-start(f32[4,56,128]{2,1,0:T(8,128)S(1)} %add.58.own), channel_id=1, source_target_pairs={{0,4},{2,6},{4,0},{6,2},{8,12},{10,14},{12,8},{14,10},{1,5},{3,7},... | collective-permute-start | bytes 344072 | tf_op jit(solution)/shard_map/ppermute | solution.py:475
  39.5 4.3 %collective-permute-start.6 = (f32[56,128]{1,0:T(8,128)S(1)}, f32[56,128]{1,0:T(8,128)S(1)}, u32[]{:S(2)}, u32[]{:S(2)}) collective-permute-start(f32[56,128]{1,0:T(8,128)S(1)} %shard_map.124), channel_id=1, source_target_pairs={{0,9},{1,8},{2,11},{3,10},{4,13},{5,12},{6,15},{7,14},{8,1},{9,0},... | collective-permute-start | bytes 86024 | tf_op jit(solution)/shard_map/ppermute | solution.py:616
  43.8 1.2 %collective-permute-start.7 = (f32[56,128]{1,0:T(8,128)S(1)}, f32[56,128]{1,0:T(8,128)S(1)}, u32[]{:S(2)}, u32[]{:S(2)}) collective-permute-start(f32[56,128]{1,0:T(8,128)S(1)} %add.59), channel_id=1, source_target_pairs={{0,1},{1,0},{2,3},{3,2},{4,5},{5,4},{6,7},{7,6},{8,9},{9,8},{10,11... | collective-permute-start | bytes 86024 | tf_op jit(solution)/shard_map/ppermute | solution.py:475
  52.4 8.6 %collective-permute-start.8 = (f32[4,56,128]{2,1,0:T(8,128)S(1)}, f32[4,56,128]{2,1,0:T(8,128)S(1)}, u32[]{:S(2)}, u32[]{:S(2)}) collective-permute-start(f32[4,56,128]{2,1,0:T(8,128)S(1)} %get-tuple-element.72), channel_id=1, source_target_pairs={{0,8},{2,10},{4,12},{6,14},{8,0},{10,2},{12,4},{14,6},{1,9},{3,11}... | collective-permute-start | bytes 344072 | tf_op jit(solution)/shard_map/ppermute | solution.py:475
  61.0 5.2 %collective-permute-start.9 = (f32[4,56,128]{2,1,0:T(8,128)S(1)}, f32[4,56,128]{2,1,0:T(8,128)S(1)}, u32[]{:S(2)}, u32[]{:S(2)}) collective-permute-start(f32[4,56,128]{2,1,0:T(8,128)S(1)} %add.61), channel_id=1, source_target_pairs={{0,2},{2,0},{4,6},{6,4},{8,10},{10,8},{12,14},{14,12},{1,3},{3,1},... | collective-permute-start | bytes 344072 | tf_op jit(solution)/shard_map/ppermute | solution.py:475
  66.2 4.9 %collective-permute-start.10 = (f32[4,56,128]{2,1,0:T(8,128)S(1)}, f32[4,56,128]{2,1,0:T(8,128)S(1)}, u32[]{:S(2)}, u32[]{:S(2)}) collective-permute-start(f32[4,56,128]{2,1,0:T(8,128)S(1)} %add.62.own), channel_id=1, source_target_pairs={{0,4},{2,6},{4,0},{6,2},{8,12},{10,14},{12,8},{14,10},{1,5},{3,7},... | collective-permute-start | bytes 344072 | tf_op jit(solution)/shard_map/ppermute | solution.py:475
  71.2 4.4 %collective-permute-start.11 = (f32[56,128]{1,0:T(8,128)S(1)}, f32[56,128]{1,0:T(8,128)S(1)}, u32[]{:S(2)}, u32[]{:S(2)}) collective-permute-start(f32[56,128]{1,0:T(8,128)S(1)} %shard_map.127), channel_id=1, source_target_pairs={{0,9},{1,8},{2,11},{3,10},{4,13},{5,12},{6,15},{7,14},{8,1},{9,0},... | collective-permute-start | bytes 86024 | tf_op jit(solution)/shard_map/ppermute | solution.py:616
  75.6 1.2 %collective-permute-start.12 = (f32[56,128]{1,0:T(8,128)S(1)}, f32[56,128]{1,0:T(8,128)S(1)}, u32[]{:S(2)}, u32[]{:S(2)}) collective-permute-start(f32[56,128]{1,0:T(8,128)S(1)} %add.63), channel_id=1, source_target_pairs={{0,1},{1,0},{2,3},{3,2},{4,5},{5,4},{6,7},{7,6},{8,9},{9,8},{10,11... | collective-permute-start | bytes 86024 | tf_op jit(solution)/shard_map/ppermute | solution.py:475

commit v5 on v4

--- a/solution.py
+++ b/solution.py
@@ -127,7 +127,7 @@
     total = slot_count(sends, early)
     sub = lax.broadcasted_iota(jnp.int32, (8, 128), 0)
     channel = tables[8:16]
-    for slot in range(xin.shape[0]):
+    def pick(slot):
         where = tile_pos[snapshot, slots[total + first + slot]]
         block = lax.div(where, per_row)
         lanes = pl.ds(pl.multiple_of(lax.rem(where, per_row) * TW, TW), TW)
@@ -151,6 +151,17 @@
         for r in range(TR):
             found = jnp.take_along_axis(channel, jnp.broadcast_to(which[r : r + 1], (8, 128)), axis=1)
             xin[slot, r] = jnp.where(sub % 4 == 0, jnp.broadcast_to(old[r : r + 1], (8, 128)), found)
+
+    last = xin.shape[0] - BATCH
+    for slot in range(xin.shape[0]):
+        if first == 0 or slot < last:
+            pick(slot)
+    if first:
+
+        @pl.when(slots[2 * total + 2] > last)
+        def _():
+            for slot in range(last, xin.shape[0]):
+                pick(slot)
 
 
 def strip_coef(coef, outer, rows):
@@ -492,9 +503,14 @@
 
     odd = j % 2 == 1
     inner = [(i, i ^ 1) for i in range(solvers)]
-    outer_pairs = [(i, (i + 1 if i % 2 else i - 1) % solvers) for i in range(solvers)]
+    outer_pairs = []
+    for i in range(solvers):
+        beside = i + 1 if i % 2 else i - 1
+        for k in range(trainers):
+            there = beside * trainers + k if 0 <= beside < solvers else i * trainers + (k ^ 1)
+            outer_pairs.append((i * trainers + k, there))
     first = lax.ppermute(edge_rows(~odd), "solver", inner)
-    second = lax.ppermute(edge_rows(odd), "solver", outer_pairs)
+    second = lax.ppermute(edge_rows(odd), ("solver", "trainer"), outer_pairs)
     second = jnp.where((j == 0) | (j == solvers - 1), 0.0, second)
 
     vr, vc = drift_table[0], drift_table[1]
@@ -596,15 +612,13 @@
             functools.partial(second_gradient_kernel, sends, early), tiles, [begun, *weights], folded, [room(totals)]
         )
         near = near + arrived
-        if snapshot == 0:
-            near, fields, strip = lax.optimization_barrier((near, fields, strip))
-            final, *tiles = second_part(fields, strip)
         bit = 1
         while 2 * bit < half:
             near = near + swap(near, "solver", bit)
             bit = 2 * bit
-            if snapshot == 0:
-                near, *tiles = lax.optimization_barrier((near, *tiles))
+        if snapshot == 0:
+            near, fields, strip = lax.optimization_barrier((near, fields, strip))
+            final, *tiles = second_part(fields, strip)
         direction = pl.pallas_call(
             functools.partial(combine_kernel, entries),
             out_shape=jax.ShapeDtypeStruct(params.shape, F32),
@@ -612,6 +626,8 @@
             out_specs=VMEM,
             compiler_params=PARAMS,
         )(near, swap(near, "solver", bit))
+        if snapshot == 0:
+            direction, *tiles = lax.optimization_barrier((direction, *tiles))
         across = [(i, i ^ (half * trainers + 1)) for i in range(solvers * trainers)]
         direction = direction + lax.ppermute(direction, ("solver", "trainer"), across)
         direction = direction + swap(direction, "trainer", 1)

time: 77.7 us -> 77 us (level)
  waiting for transfers between devices: 30.3 us -> 28.9 us
    ppermute x9, starting transfers between devices: 5.18 us -> 9.45 us  [swap(): return lax.ppermute(x, axis, [(i, i ^ bit) for i in range(count)])]
    ppermute x1, starting transfers between devices: 3.61 us -> 0.07 us  [local(): second = lax.ppermute(edge_rows(odd), ('solver', 'trainer'), outer_pairs)]
    ppermute x9, waiting for transfers between devices: 21.8 us -> 20.6 us  [swap(): return lax.ppermute(x, axis, [(i, i ^ bit) for i in range(count)])]
where the time goes in v5:
time: 77 us; the launch traced here: 76.8 us
  Pallas kernels  31.3 us (41%)
  waiting for transfers between devices  28.9 us (38%)
  starting transfers between devices  12.6 us (16%)
  other arithmetic  2.58 us (3%)
  between operations  1.04 us (1%)
    ppermute x9, waiting for transfers between devices, swap(): return lax.ppermute(x, axis, [(i, i ^ bit) for i in range(count)])  20.6 us
    pallas_call x3, Pallas kernels, gradients(): pl.pallas_call(kernel, out_shape=out_shape, in_specs=[SMEM] + [VMEM] * (2...  15.3 us
    ppermute x9, starting transfers between devices, swap(): return lax.ppermute(x, axis, [(i, i ^ bit) for i in range(count)])  9.45 us
    ppermute x2, waiting for transfers between devices, local(): lax.ppermute(direction, ('solver', 'trainer'), across)  8.36 us
    pallas_call x1, Pallas kernels, local(): pl.pallas_call(functools.partial(opening_kernel, sizes), out_shape=(jax.S...  7.55 us
    pallas_call x1, Pallas kernels, local(): pl.pallas_call(functools.partial(edge_kernel, sizes), out_shape=tile_shap...  5.07 us
    ppermute x1, starting transfers between devices, local(): first = lax.ppermute(edge_rows(~odd), 'solver', inner)  2.93 us
    pallas_call x1, Pallas kernels, second_part(): pl.pallas_call(functools.partial(second_strip_kernel, sizes), out_shape=(...  2.42 us
  transfers between devices with their start and end apart: 13, of which 11 were waited for; matrix products, arithmetic and copies ran while one was open for 1% of the time, Pallas kernels for 23%

profile of v5, /device:TPU:0, one launch (start us, length us, event | category | flops | bytes accessed | tf_op | source)
XLA Modules:
  0.0 76.8 jit_solution(14383403675688839968)
XLA Ops:
  0.6 1.1 %convert_bitcast_fusion = f32[1,32,4096]{2,1,0:T(8,128)S(1)} fusion(s32[32,4096]{1,0:T(8,128)} %param.10), kind=kLoop, calls=%fused_computation.1 | loop fusion | flops 262144 | bytes 1048576 | tf_op jit(solution)/shard_map/stack | solution.py:491
  1.8 1.1 %pad_maximum_fusion.both = f32[2,32,4096]{2,1,0:T(8,128)S(1)} fusion(f32[1,32,4096]{2,1,0:T(8,128)S(1)} %convert_bitcast_fusion, f32[1,32,4096]{2,1,0:T(8,128)} %bitcast.73), kind=kLoop, calls=%fused_computation | loop fusion | flops 262144 | bytes 2097152 | tf_op jit(solution)/shard_map/stack | solution.py:491
  3.0 0.5 collective-permute-start
  3.8 0.1 fusion.1.params
  3.9 0.1 pad.8.tables
  4.0 0.3 collective-permute-done
  4.4 2.9 %collective-permute-start.1 = (f32[7,4224]{1,0:T(8,128)S(1)}, f32[7,4224]{1,0:T(8,128)S(1)}, u32[]{:S(2)}, u32[]{:S(2)}) collective-permute-start(f32[7,4224]{1,0:T(8,128)S(1)} %maximum_maximum_fusion), channel_id=1, source_target_pairs={{0,2},{2,0},{4,6},{6,4},{8,10},{10,8},{12,14},{14,12},{1,3},{3,1},... | collective-permute-start | bytes 354824 | tf_op jit(solution)/shard_map/ppermute | solution.py:512
  7.5 7.6 %shard_map.120 = (f32[4,32,4224]{2,1,0:T(8,128)S(1)}, f32[4,32,4224]{2,1,0:T(8,128)S(1)}, s32[67]{0:T(128)S(1)}, f32[8,256,128]{2,1,0:T(8,128)S(1)}, bf16[64,144...) custom-call(s32[1]{0:T(128)} %bitcast.place, ...), custom_call_target="tpu_custom_call" | custom-call | flops 2147483648 | bytes 8388608 | tf_op jit(solution)/shard_map/pallas_call | solution.py:553
  15.1 5.1 %shard_map.121 = (f32[24,4,8,128]{3,2,1,0:T(8,128)S(1)}, f32[24,4,128]{2,1,0:T(4,128)S(1)}, f32[24,4224]{1,0:T(8,128)S(1)}, f32[4,8,4224]{2,1,0:T(8,128)S(1)}, f...) custom-call(s32[1]{0:T(128)} %bitcast.place, s32[2,24]{1,0:T(2,128)S(1)} %bitcast.69, ...), custom_call_target="tpu_custom_call" | custom-call | tf_op jit(solution)/shard_map/pallas_call | solution.py:582
  20.2 3.0 %collective-permute-start.3 = (f32[4,56,128]{2,1,0:T(8,128)S(1)}, f32[4,56,128]{2,1,0:T(8,128)S(1)}, u32[]{:S(2)}, u32[]{:S(2)}) collective-permute-start(f32[4,56,128]{2,1,0:T(8,128)S(1)} %get-tuple-element.52), channel_id=1, source_target_pairs={{0,8},{2,10},{4,12},{6,14},{8,0},{10,2},{12,4},{14,6},{1,9},{3,11}... | collective-permute-start | bytes 344072 | tf_op jit(solution)/shard_map/ppermute | solution.py:486
  23.2 4.1 %shard_map.122 = f32[4,56,128]{2,1,0:T(8,128)S(1)} custom-call(s32[67]{0:T(128)S(1)} %get-tuple-element.41.slots, f32[24,4,8,128]{3,2,1,0:T(8,128)S(1)} %get-tuple-element.49.xin, f32[24,4,128]{2,1,0:T(4,128)S(1)} %get-tuple-element.50.base, f32[8,256,128]{2,1,0:T(8,128)S(1)} %get-tuple-element.51.begun, bf16[64,144]{1,0:T(8,128)(2,1)S(1)} %get-tuple-element.44.rest_0_, ...), custom_call_target="tpu_custom_call" | custom-call | flops 11796480000 | bytes 2097152 | tf_op jit(solution)/shard_map/pallas_call | solution.py:572
  27.3 1.8 %collective-permute-done.3 = f32[4,56,128]{2,1,0:T(8,128)S(1)} collective-permute-done((f32[4,56,128]{2,1,0:T(8,128)S(1)}, f32[4,56,128]{2,1,0:T(8,128)S(1)}, u32[]{:S(2)}, u32[]{:S(2)}) %collective-permute-start.3) | collective-permute-done | bytes 114720 | tf_op jit(solution)/shard_map/ppermute | solution.py:486
  29.1 2.2 %collective-permute-start.4 = (f32[4,56,128]{2,1,0:T(8,128)S(1)}, f32[4,56,128]{2,1,0:T(8,128)S(1)}, u32[]{:S(2)}, u32[]{:S(2)}) collective-permute-start(f32[4,56,128]{2,1,0:T(8,128)S(1)} %add.57), channel_id=1, source_target_pairs={{0,2},{2,0},{4,6},{6,4},{8,10},{10,8},{12,14},{14,12},{1,3},{3,1},... | collective-permute-start | bytes 344072 | tf_op jit(solution)/shard_map/ppermute | solution.py:486
  31.4 2.8 %collective-permute-done.4 = f32[4,56,128]{2,1,0:T(8,128)S(1)} collective-permute-done((f32[4,56,128]{2,1,0:T(8,128)S(1)}, f32[4,56,128]{2,1,0:T(8,128)S(1)}, u32[]{:S(2)}, u32[]{:S(2)}) %collective-permute-start.4) | collective-permute-done | bytes 114720 | tf_op jit(solution)/shard_map/ppermute | solution.py:486
  34.1 0.3 collective-permute-start.5
  34.5 2.4 %shard_map.123 = (f32[32,4096]{1,0:T(8,128)}, f32[24,4,8,128]{3,2,1,0:T(8,128)S(1)}, f32[24,4,128]{2,1,0:T(4,128)S(1)}, s32[51]{0:T(128)S(1)}) custom-call(s32[1]{0:T(128)} %bitcast.place, s32[2,24]{1,0:T(2,128)S(1)} %bitcast.70, s32[2,24]{1,0:T(2,128)S(1)} %bitcast.72, f32[2,32,4096]{2,1,0:T(8,128)S(1)} %pad_maximum_fusion.both, f32[16,128]{1,0:T(8,128)S(1)} %pad.8.tables, ...), custom_call_target="tpu_custom_call" | custom-call | flops 2147483648 | bytes 8388608 | tf_op jit(solution)/shard_map/pallas_call | solution.py:593
  36.9 2.1 %collective-permute-done.5.other = f32[4,56,128]{2,1,0:T(8,128)S(1)} collective-permute-done((f32[4,56,128]{2,1,0:T(8,128)S(1)}, f32[4,56,128]{2,1,0:T(8,128)S(1)}, u32[]{:S(2)}, u32[]{:S(2)}) %collective-permute-start.5) | collective-permute-done | bytes 114720 | tf_op jit(solution)/shard_map/ppermute | solution.py:486
  39.0 0.1 shard_map.124
  39.2 4.2 %collective-permute-done.6 = f32[56,128]{1,0:T(8,128)S(1)} collective-permute-done((f32[56,128]{1,0:T(8,128)S(1)}, f32[56,128]{1,0:T(8,128)S(1)}, u32[]{:S(2)}, u32[]{:S(2)}) %collective-permute-start.6) | collective-permute-done | bytes 28704 | tf_op jit(solution)/shard_map/ppermute | solution.py:632
  43.4 1.2 %collective-permute-done.7 = f32[56,128]{1,0:T(8,128)S(1)} collective-permute-done((f32[56,128]{1,0:T(8,128)S(1)}, f32[56,128]{1,0:T(8,128)S(1)}, u32[]{:S(2)}, u32[]{:S(2)}) %collective-permute-start.7) | collective-permute-done | bytes 28704 | tf_op jit(solution)/shard_map/ppermute | solution.py:486
  44.6 0.1 multiply_subtract_fusion
  44.7 7.3 %shard_map.125 = (f32[4,56,128]{2,1,0:T(8,128)S(1)}, f32[8,256,128]{2,1,0:T(8,128)S(1)}, bf16[64,144]{1,0:T(8,128)(2,1)S(1)}, bf16[64,192]{1,0:T(8,128)(2,1)S(1)...) custom-call(s32[51]{0:T(128)S(1)} %get-tuple-element.63.slots, ...), custom_call_target="tpu_custom_call" | custom-call | flops 11796480000 | bytes 2097152 | tf_op jit(solution)/shard_map/pallas_call | solution.py:572
  52.0 1.7 %collective-permute-start.8 = (f32[4,56,128]{2,1,0:T(8,128)S(1)}, f32[4,56,128]{2,1,0:T(8,128)S(1)}, u32[]{:S(2)}, u32[]{:S(2)}) collective-permute-start(f32[4,56,128]{2,1,0:T(8,128)S(1)} %get-tuple-element.72), channel_id=1, source_target_pairs={{0,8},{2,10},{4,12},{6,14},{8,0},{10,2},{12,4},{14,6},{1,9},{3,11}... | collective-permute-start | bytes 344072 | tf_op jit(solution)/shard_map/ppermute | solution.py:486
  53.7 3.9 %shard_map.126 = f32[4,56,128]{2,1,0:T(8,128)S(1)} custom-call(s32[51]{0:T(128)S(1)} %get-tuple-element.63.slots, f32[24,4,8,128]{3,2,1,0:T(8,128)S(1)} %get-tuple-element.64.xin, f32[24,4,128]{2,1,0:T(4,128)S(1)} %get-tuple-element.65.base, f32[8,256,128]{2,1,0:T(8,128)S(1)} %get-tuple-element.66.begun, bf16[64,144]{1,0:T(8,128)(2,1)S(1)} %get-tuple-element.67.rest_0_, ...), custom_call_target="tpu_custom_call" | custom-call | flops 11796480000 | bytes 2097152 | tf_op jit(solution)/shard_map/pallas_call | solution.py:572
  57.5 3.1 %collective-permute-done.8 = f32[4,56,128]{2,1,0:T(8,128)S(1)} collective-permute-done((f32[4,56,128]{2,1,0:T(8,128)S(1)}, f32[4,56,128]{2,1,0:T(8,128)S(1)}, u32[]{:S(2)}, u32[]{:S(2)}) %collective-permute-start.8) | collective-permute-done | bytes 114720 | tf_op jit(solution)/shard_map/ppermute | solution.py:486
  60.6 1.7 %collective-permute-start.9 = (f32[4,56,128]{2,1,0:T(8,128)S(1)}, f32[4,56,128]{2,1,0:T(8,128)S(1)}, u32[]{:S(2)}, u32[]{:S(2)}) collective-permute-start(f32[4,56,128]{2,1,0:T(8,128)S(1)} %add.61), channel_id=1, source_target_pairs={{0,2},{2,0},{4,6},{6,4},{8,10},{10,8},{12,14},{14,12},{1,3},{3,1},... | collective-permute-start | bytes 344072 | tf_op jit(solution)/shard_map/ppermute | solution.py:486
  62.3 3.3 %collective-permute-done.9 = f32[4,56,128]{2,1,0:T(8,128)S(1)} collective-permute-done((f32[4,56,128]{2,1,0:T(8,128)S(1)}, f32[4,56,128]{2,1,0:T(8,128)S(1)}, u32[]{:S(2)}, u32[]{:S(2)}) %collective-permute-start.9) | collective-permute-done | bytes 114720 | tf_op jit(solution)/shard_map/ppermute | solution.py:486
  65.7 4.8 %collective-permute-done.10.other = f32[4,56,128]{2,1,0:T(8,128)S(1)} collective-permute-done((f32[4,56,128]{2,1,0:T(8,128)S(1)}, f32[4,56,128]{2,1,0:T(8,128)S(1)}, u32[]{:S(2)}, u32[]{:S(2)}) %collective-permute-start.10) | collective-permute-done | bytes 114720 | tf_op jit(solution)/shard_map/ppermute | solution.py:486
  70.5 0.1 shard_map.127
  70.8 4.2 %collective-permute-done.11 = f32[56,128]{1,0:T(8,128)S(1)} collective-permute-done((f32[56,128]{1,0:T(8,128)S(1)}, f32[56,128]{1,0:T(8,128)S(1)}, u32[]{:S(2)}, u32[]{:S(2)}) %collective-permute-start.11) | collective-permute-done | bytes 28704 | tf_op jit(solution)/shard_map/ppermute | solution.py:632
  75.0 1.2 %collective-permute-done.12 = f32[56,128]{1,0:T(8,128)S(1)} collective-permute-done((f32[56,128]{1,0:T(8,128)S(1)}, f32[56,128]{1,0:T(8,128)S(1)}, u32[]{:S(2)}, u32[]{:S(2)}) %collective-permute-start.12) | collective-permute-done | bytes 28704 | tf_op jit(solution)/shard_map/ppermute | solution.py:486
  76.2 0.7 shard_map.128
  (50 shorter events, 0.8 us)
Async XLA Ops:
  1.7 1.8 %copy-start.5 = (f32[9,1,64]{2,1,0:T(1,128)S(1)}, f32[9,1,64]{2,1,0:T(1,128)}, u32[]{:S(2)}) copy-start(f32[9,1,64]{2,1,0:T(1,128)} %param.17) | copy-start | bytes 6916
  1.7 1.9 %copy-start.3 = (f32[9,64,4]{1,2,0:T(4,128)S(1)}, f32[9,64,4]{1,2,0:T(4,128)}, u32[]{:S(2)}) copy-start(f32[9,64,4]{1,2,0:T(4,128)} %param.15) | copy-start | bytes 27652
  1.7 1.9 %copy-start.2 = (f32[64,64]{1,0:T(8,128)S(1)}, f32[64,64]{1,0:T(8,128)}, u32[]{:S(2)}) copy-start(f32[64,64]{1,0:T(8,128)} %param.16) | copy-start | bytes 49156
  1.8 1.9 %copy-start.4 = (f32[2,16]{1,0:T(2,128)S(1)}, f32[2,16]{1,0:T(2,128)}, u32[]{:S(2)}) copy-start(f32[2,16]{1,0:T(2,128)} %param.12) | copy-start | bytes 388
  1.8 1.9 %copy-start.6 = (f32[16]{0:T(128)S(1)}, f32[16]{0:T(128)}, u32[]{:S(2)}) copy-start(f32[16]{0:T(128)} %param.11) | copy-start | bytes 196
  2.9 4.6 %copy-start = (s32[2,1,1,24]{3,2,1,0:T(1,128)S(1)}, s32[2,1,1,24]{3,2,1,0:T(1,128)}, u32[]{:S(2)}) copy-start(s32[2,1,1,24]{3,2,1,0:T(1,128)} %param.13) | copy-start | bytes 580
  2.9 4.6 %copy-start.1 = (s32[2,1,1,24,1]{3,4,2,1,0:T(1,128)S(1)}, s32[2,1,1,24,1]{3,4,2,1,0:T(1,128)}, u32[]{:S(2)}) copy-start(s32[2,1,1,24,1]{3,4,2,1,0:T(1,128)} %param.14) | copy-start | bytes 580
  3.0 1.4 %collective-permute-start = (f32[2,32,128]{2,1,0:T(8,128)S(1)}, f32[2,32,128]{2,1,0:T(8,128)S(1)}, u32[]{:S(2)}, u32[]{:S(2)}) collective-permute-start(f32[2,32,128]{2,1,0:T(8,128)S(1)} %slice_select_fusion), channel_id=1, source_target_pairs={{0,1},{1,0},{2,3},{3,2},{4,5},{5,4},{6,7},{7,6},{8,9},{9,8},{10,11... | collective-permute-start | bytes 98312 | tf_op jit(solution)/shard_map/ppermute | solution.py:486
  4.4 10.7 %collective-permute-start.1 = (f32[7,4224]{1,0:T(8,128)S(1)}, f32[7,4224]{1,0:T(8,128)S(1)}, u32[]{:S(2)}, u32[]{:S(2)}) collective-permute-start(f32[7,4224]{1,0:T(8,128)S(1)} %maximum_maximum_fusion), channel_id=1, source_target_pairs={{0,2},{2,0},{4,6},{6,4},{8,10},{10,8},{12,14},{14,12},{1,3},{3,1},... | collective-permute-start | bytes 354824 | tf_op jit(solution)/shard_map/ppermute | solution.py:512
  7.4 7.7 %collective-permute-start.2 = (f32[7,4224]{1,0:T(8,128)S(1)}, f32[7,4224]{1,0:T(8,128)S(1)}, u32[]{:S(2)}, u32[]{:S(2)}) collective-permute-start(f32[7,4224]{1,0:T(8,128)S(1)} %maximum_maximum_fusion.1), channel_id=1, source_target_pairs={{0,1},{1,0},{2,4},{3,5},{4,2},{5,3},{6,8},{7,9},{8,6},{9,7},{10,12... | collective-permute-start | bytes 354824 | tf_op jit(solution)/shard_map/ppermute | solution.py:513
  20.2 8.9 %collective-permute-start.3 = (f32[4,56,128]{2,1,0:T(8,128)S(1)}, f32[4,56,128]{2,1,0:T(8,128)S(1)}, u32[]{:S(2)}, u32[]{:S(2)}) collective-permute-start(f32[4,56,128]{2,1,0:T(8,128)S(1)} %get-tuple-element.52), channel_id=1, source_target_pairs={{0,8},{2,10},{4,12},{6,14},{8,0},{10,2},{12,4},{14,6},{1,9},{3,11}... | collective-permute-start | bytes 344072 | tf_op jit(solution)/shard_map/ppermute | solution.py:486
  29.1 5.0 %collective-permute-start.4 = (f32[4,56,128]{2,1,0:T(8,128)S(1)}, f32[4,56,128]{2,1,0:T(8,128)S(1)}, u32[]{:S(2)}, u32[]{:S(2)}) collective-permute-start(f32[4,56,128]{2,1,0:T(8,128)S(1)} %add.57), channel_id=1, source_target_pairs={{0,2},{2,0},{4,6},{6,4},{8,10},{10,8},{12,14},{14,12},{1,3},{3,1},... | collective-permute-start | bytes 344072 | tf_op jit(solution)/shard_map/ppermute | solution.py:486
  34.1 4.9 %collective-permute-start.5 = (f32[4,56,128]{2,1,0:T(8,128)S(1)}, f32[4,56,128]{2,1,0:T(8,128)S(1)}, u32[]{:S(2)}, u32[]{:S(2)}) collective-permute-start(f32[4,56,128]{2,1,0:T(8,128)S(1)} %add.58.own), channel_id=1, source_target_pairs={{0,4},{2,6},{4,0},{6,2},{8,12},{10,14},{12,8},{14,10},{1,5},{3,7},... | collective-permute-start | bytes 344072 | tf_op jit(solution)/shard_map/ppermute | solution.py:486
  39.2 4.3 %collective-permute-start.6 = (f32[56,128]{1,0:T(8,128)S(1)}, f32[56,128]{1,0:T(8,128)S(1)}, u32[]{:S(2)}, u32[]{:S(2)}) collective-permute-start(f32[56,128]{1,0:T(8,128)S(1)} %shard_map.124), channel_id=1, source_target_pairs={{0,9},{1,8},{2,11},{3,10},{4,13},{5,12},{6,15},{7,14},{8,1},{9,0},... | collective-permute-start | bytes 86024 | tf_op jit(solution)/shard_map/ppermute | solution.py:632
  43.4 1.2 %collective-permute-start.7 = (f32[56,128]{1,0:T(8,128)S(1)}, f32[56,128]{1,0:T(8,128)S(1)}, u32[]{:S(2)}, u32[]{:S(2)}) collective-permute-start(f32[56,128]{1,0:T(8,128)S(1)} %add.59), channel_id=1, source_target_pairs={{0,1},{1,0},{2,3},{3,2},{4,5},{5,4},{6,7},{7,6},{8,9},{9,8},{10,11... | collective-permute-start | bytes 86024 | tf_op jit(solution)/shard_map/ppermute | solution.py:486
  52.0 8.6 %collective-permute-start.8 = (f32[4,56,128]{2,1,0:T(8,128)S(1)}, f32[4,56,128]{2,1,0:T(8,128)S(1)}, u32[]{:S(2)}, u32[]{:S(2)}) collective-permute-start(f32[4,56,128]{2,1,0:T(8,128)S(1)} %get-tuple-element.72), channel_id=1, source_target_pairs={{0,8},{2,10},{4,12},{6,14},{8,0},{10,2},{12,4},{14,6},{1,9},{3,11}... | collective-permute-start | bytes 344072 | tf_op jit(solution)/shard_map/ppermute | solution.py:486
  60.6 5.0 %collective-permute-start.9 = (f32[4,56,128]{2,1,0:T(8,128)S(1)}, f32[4,56,128]{2,1,0:T(8,128)S(1)}, u32[]{:S(2)}, u32[]{:S(2)}) collective-permute-start(f32[4,56,128]{2,1,0:T(8,128)S(1)} %add.61), channel_id=1, source_target_pairs={{0,2},{2,0},{4,6},{6,4},{8,10},{10,8},{12,14},{14,12},{1,3},{3,1},... | collective-permute-start | bytes 344072 | tf_op jit(solution)/shard_map/ppermute | solution.py:486
  65.7 4.9 %collective-permute-start.10 = (f32[4,56,128]{2,1,0:T(8,128)S(1)}, f32[4,56,128]{2,1,0:T(8,128)S(1)}, u32[]{:S(2)}, u32[]{:S(2)}) collective-permute-start(f32[4,56,128]{2,1,0:T(8,128)S(1)} %add.62.own), channel_id=1, source_target_pairs={{0,4},{2,6},{4,0},{6,2},{8,12},{10,14},{12,8},{14,10},{1,5},{3,7},... | collective-permute-start | bytes 344072 | tf_op jit(solution)/shard_map/ppermute | solution.py:486
  70.7 4.3 %collective-permute-start.11 = (f32[56,128]{1,0:T(8,128)S(1)}, f32[56,128]{1,0:T(8,128)S(1)}, u32[]{:S(2)}, u32[]{:S(2)}) collective-permute-start(f32[56,128]{1,0:T(8,128)S(1)} %shard_map.127), channel_id=1, source_target_pairs={{0,9},{1,8},{2,11},{3,10},{4,13},{5,12},{6,15},{7,14},{8,1},{9,0},... | collective-permute-start | bytes 86024 | tf_op jit(solution)/shard_map/ppermute | solution.py:632
  74.9 1.2 %collective-permute-start.12 = (f32[56,128]{1,0:T(8,128)S(1)}, f32[56,128]{1,0:T(8,128)S(1)}, u32[]{:S(2)}, u32[]{:S(2)}) collective-permute-start(f32[56,128]{1,0:T(8,128)S(1)} %add.63), channel_id=1, source_target_pairs={{0,1},{1,0},{2,3},{3,2},{4,5},{5,4},{6,7},{7,6},{8,9},{9,8},{10,11... | collective-permute-start | bytes 86024 | tf_op jit(solution)/shard_map/ppermute | solution.py:486
